TPU v7x, 32 devices: a whole 2x2x4 slice. The times are simulated.
32 devices in a mesh: dp: 4 (over y, x), ctx: 8 (over z, core).
Axes of the slice: x: 2, y: 2, z: 4, core: 2. Of those that a mesh axis runs over, the one named last changes fastest.
Arguments:
- hidden_in: bfloat16 [8, 2048, 960], P('dp', 'ctx'), may hold values from -6 to 6
- positions: int32 [8, 2048], P('dp', 'ctx'), may hold values from 0 to 2047, as said below
- attn_gain: bfloat16 [960], P('ctx'), may hold values from 0.099609375 to 1.8984375
- w_query: bfloat16 [960, 960], P('dp', 'ctx'), may hold values from -0.1875 to 0.1875
- key_projection_weight: bfloat16 [960, 320], P('dp', 'ctx'), may hold values from -0.1875 to 0.1875
- w_value: bfloat16 [960, 320], P('dp', 'ctx'), may hold values from -0.1875 to 0.1875
- w_out: bfloat16 [960, 960], P('dp', 'ctx'), may hold values from -2 to 2
- ffn_gain: bfloat16 [960], P('ctx'), may hold values from 0.099609375 to 1.8984375
- w_gate: bfloat16 [960, 2560], P('dp', 'ctx'), may hold values from -0.1875 to 0.1875
- w_up: bfloat16 [960, 2560], P('dp', 'ctx'), may hold values from -0.1875 to 0.1875
- w_down: bfloat16 [2560, 960], P('dp', 'ctx'), may hold values from -0.125 to 0.125
- out_grad: bfloat16 [8, 2048, 960], P('dp', 'ctx'), may hold values from -6 to 6
Outputs:
- layer_out: bfloat16 [8, 2048, 960], P('dp', 'ctx')
- input_grad: bfloat16 [8, 2048, 960], P('dp', 'ctx')
- attn_gain_grad: float32 [960], P('ctx')
- w_query_grad: float32 [960, 960], P('dp', 'ctx')
- w_key_grad: float32 [960, 320], P('dp', 'ctx')
- w_value_grad: float32 [960, 320], P('dp', 'ctx')
- w_out_grad: float32 [960, 960], P('dp', 'ctx')
- ffn_gain_grad: float32 [960], P('ctx')
- w_gate_grad: float32 [960, 2560], P('dp', 'ctx')
- w_up_grad: float32 [960, 2560], P('dp', 'ctx')
- w_down_grad: float32 [2560, 960], P('dp', 'ctx')
Inputs may be any that keep to these rules, and one draw needn't show every extreme that they name: Every sequence is packed with documents: positions is 0 at a document's first token and rises by one from token to token within it; the first token of every sequence begins a document, and one sequence is a single document.
All inputs are finite; a program needn't handle non-finite values.
Results may differ from a plain program's by a relative error of at most 0.024.
Values may be sent and summed in bfloat16 or wider, within the bound.
No kernel may reach another device: no remote copies, remote signals or barrier semaphores. Data moves between devices by JAX's collectives and lax.ppermute only.
A program may use at most 320 MiB of HBM per device.

v0:
```python
import math

import jax
import jax.numpy as jnp
from jax import lax
from jax.sharding import PartitionSpec as P

QUERY_HEADS = 15
KEY_VALUE_HEADS = 5
HEAD_SIZE = 64


epsilon = 1e-05
theta_base = 100000.0
causal_masked_score = -1e30


def angles(pos_local):
    half_size = HEAD_SIZE // 2
    frequency = jnp.power(theta_base, -jnp.arange(half_size, dtype=jnp.float32) * 2.0 / HEAD_SIZE)
    angle_table = pos_local.astype(jnp.float32)[:, None] * frequency[None, :]
    return (jnp.cos(angle_table)[:, None, :], jnp.sin(angle_table)[:, None, :])


def rotary_pair_rotation(value_matrix, cosine_table, sine_table, heads):
    token_length = value_matrix.shape[0]
    half_size = HEAD_SIZE // 2
    split_heads = value_matrix.reshape(token_length, heads, HEAD_SIZE)
    first_half = split_heads[..., :half_size]
    second_half = split_heads[..., half_size:]
    turned = jnp.concatenate(
        [
            first_half * cosine_table - second_half * sine_table,
            second_half * cosine_table + first_half * sine_table,
        ],
        axis=-1,
    )
    return turned.reshape(token_length, heads * HEAD_SIZE)


def norm_scale(value_matrix):
    return lax.rsqrt(jnp.mean(value_matrix * value_matrix, axis=-1, keepdims=True) + epsilon)


def visible(query_index, query_pos, key_index, key_pos):
    causal = key_index[None, :] <= query_index[:, None]
    same_doc = query_index[:, None] - key_index[None, :] == query_pos[:, None] - key_pos[None, :]
    return causal & same_doc


def to_rows(value_matrix, span_length):
    heads_per_group = QUERY_HEADS // KEY_VALUE_HEADS
    return (
        value_matrix.reshape(span_length, KEY_VALUE_HEADS, heads_per_group, HEAD_SIZE)
        .transpose(1, 2, 0, 3)
        .reshape(KEY_VALUE_HEADS, heads_per_group * span_length, HEAD_SIZE)
    )


def from_rows(value_matrix, span_length):
    heads_per_group = QUERY_HEADS // KEY_VALUE_HEADS
    return (
        value_matrix.reshape(KEY_VALUE_HEADS, heads_per_group, span_length, HEAD_SIZE)
        .transpose(2, 0, 1, 3)
        .reshape(span_length, QUERY_HEADS * HEAD_SIZE)
    )


def product_reduced_precision(left_rows, right_rows):
    return jnp.dot(left_rows, right_rows, preferred_element_type=jnp.float32)


def matmul_back(left_rows, weight_full):
    return jnp.einsum("tf,df->td", left_rows, weight_full, preferred_element_type=jnp.float32)


def outer_product(left_rows, right_rows):
    return jnp.einsum("ti,tj->ij", left_rows, right_rows, preferred_element_type=jnp.float32)


def fetch_weights(
    w_query, key_projection_weight, w_value, w_out, w_gate, w_up, w_down, attn_row, ffn_row
):
    tall = (
        lax.all_gather(w_query, "dp", axis=0, tiled=True),
        lax.all_gather(key_projection_weight, "dp", axis=0, tiled=True),
        lax.all_gather(w_value, "dp", axis=0, tiled=True),
        lax.all_gather(w_out, "dp", axis=0, tiled=True),
        lax.all_gather(w_gate, "dp", axis=0, tiled=True),
        lax.all_gather(w_up, "dp", axis=0, tiled=True),
        lax.all_gather(w_down, "dp", axis=0, tiled=True),
    )
    joined = (
        lax.all_gather(tall[0], "ctx", axis=1, tiled=True),
        lax.all_gather(tall[1], "ctx", axis=1, tiled=True),
        lax.all_gather(tall[2], "ctx", axis=1, tiled=True),
        lax.all_gather(tall[3], "ctx", axis=1, tiled=True),
        lax.all_gather(tall[4], "ctx", axis=1, tiled=True),
        lax.all_gather(tall[5], "ctx", axis=1, tiled=True),
        lax.all_gather(tall[6], "ctx", axis=1, tiled=True),
        lax.all_gather(attn_row, "ctx", axis=1, tiled=True),
        lax.all_gather(ffn_row, "ctx", axis=1, tiled=True),
    )
    whole = (joined[0], joined[1], joined[2], joined[3], joined[4], joined[5], joined[6])
    gain_pair = (joined[7], joined[8])
    return (
        tuple(whole),
        gain_pair[0].reshape(-1).astype(jnp.float32),
        gain_pair[1].reshape(-1).astype(jnp.float32),
    )


def reduce_grads(grad_list, attn_sum, ffn_sum):
    gain_total = lax.psum((attn_sum, ffn_sum), "dp")
    attn_rows = gain_total[0].reshape(1, -1)
    ffn_rows = gain_total[1].reshape(1, -1)
    part_sums = (
        lax.psum_scatter(
            grad_list[0].astype(jnp.bfloat16), "ctx", scatter_dimension=1, tiled=True
        ).astype(jnp.float32),
        lax.psum_scatter(
            grad_list[1].astype(jnp.bfloat16), "ctx", scatter_dimension=1, tiled=True
        ).astype(jnp.float32),
        lax.psum_scatter(
            grad_list[2].astype(jnp.bfloat16), "ctx", scatter_dimension=1, tiled=True
        ).astype(jnp.float32),
        lax.psum_scatter(
            grad_list[3].astype(jnp.bfloat16), "ctx", scatter_dimension=1, tiled=True
        ).astype(jnp.float32),
        lax.psum_scatter(
            grad_list[4].astype(jnp.bfloat16), "ctx", scatter_dimension=1, tiled=True
        ).astype(jnp.float32),
        lax.psum_scatter(
            grad_list[5].astype(jnp.bfloat16), "ctx", scatter_dimension=1, tiled=True
        ).astype(jnp.float32),
        lax.psum_scatter(
            grad_list[6].astype(jnp.bfloat16), "ctx", scatter_dimension=1, tiled=True
        ).astype(jnp.float32),
        lax.psum_scatter(
            attn_rows.astype(jnp.bfloat16), "ctx", scatter_dimension=1, tiled=True
        ).astype(jnp.float32),
        lax.psum_scatter(
            ffn_rows.astype(jnp.bfloat16), "ctx", scatter_dimension=1, tiled=True
        ).astype(jnp.float32),
    )
    finished = (
        lax.psum_scatter(
            part_sums[0].astype(jnp.bfloat16), "dp", scatter_dimension=0, tiled=True
        ).astype(jnp.float32),
        lax.psum_scatter(
            part_sums[1].astype(jnp.bfloat16), "dp", scatter_dimension=0, tiled=True
        ).astype(jnp.float32),
        lax.psum_scatter(
            part_sums[2].astype(jnp.bfloat16), "dp", scatter_dimension=0, tiled=True
        ).astype(jnp.float32),
        lax.psum_scatter(
            part_sums[3].astype(jnp.bfloat16), "dp", scatter_dimension=0, tiled=True
        ).astype(jnp.float32),
        lax.psum_scatter(
            part_sums[4].astype(jnp.bfloat16), "dp", scatter_dimension=0, tiled=True
        ).astype(jnp.float32),
        lax.psum_scatter(
            part_sums[5].astype(jnp.bfloat16), "dp", scatter_dimension=0, tiled=True
        ).astype(jnp.float32),
        lax.psum_scatter(
            part_sums[6].astype(jnp.bfloat16), "dp", scatter_dimension=0, tiled=True
        ).astype(jnp.float32),
    )
    matrices = (
        finished[0],
        finished[1],
        finished[2],
        finished[3],
        finished[4],
        finished[5],
        finished[6],
    )
    gain_pair = (part_sums[7], part_sums[8])
    return (matrices, gain_pair[0].reshape(-1), gain_pair[1].reshape(-1))


def attend(query_rows, keys_seq, values_seq, query_index, query_pos, sequence_positions, last_row):
    token_length = keys_seq.shape[0]
    block_length = min(512, token_length)
    count_of_rows = query_rows.shape[1]
    score_scale = 1.0 / math.sqrt(HEAD_SIZE)

    def one_block(block_number, state_in):
        running_top, row_total, weighted_sum = state_in
        offset = block_number * block_length
        split_key_heads = lax.dynamic_slice_in_dim(keys_seq, offset, block_length, 0).reshape(
            block_length, KEY_VALUE_HEADS, HEAD_SIZE
        )
        split_value_heads = lax.dynamic_slice_in_dim(values_seq, offset, block_length, 0).reshape(
            block_length, KEY_VALUE_HEADS, HEAD_SIZE
        )
        raw_scores = (
            jnp.einsum(
                "hrd,nhd->hrn", query_rows, split_key_heads, preferred_element_type=jnp.float32
            )
            * score_scale
        )
        key_index = offset + jnp.arange(block_length, dtype=jnp.int32)
        key_pos = lax.dynamic_slice_in_dim(sequence_positions, offset, block_length, 0)
        allowed = visible(query_index, query_pos, key_index, key_pos)[None]
        scores = jnp.where(allowed, raw_scores, causal_masked_score)
        new_top = jnp.maximum(running_top, jnp.max(scores, axis=-1))
        rescale = jnp.exp(running_top - new_top)
        expo = jnp.where(allowed, jnp.exp(scores - new_top[..., None]), 0.0)
        row_total = row_total * rescale + jnp.sum(expo, axis=-1)
        weighted_sum = weighted_sum * rescale[..., None] + jnp.einsum(
            "hrn,nhd->hrd",
            expo.astype(jnp.bfloat16),
            split_value_heads,
            preferred_element_type=jnp.float32,
        )
        return (new_top, row_total, weighted_sum)

    stop_block = last_row // block_length + 1
    start_state = (
        jnp.full((KEY_VALUE_HEADS, count_of_rows), causal_masked_score, jnp.float32),
        jnp.zeros((KEY_VALUE_HEADS, count_of_rows), jnp.float32),
        jnp.zeros((KEY_VALUE_HEADS, count_of_rows, HEAD_SIZE), jnp.float32),
    )
    running_top, row_total, weighted_sum = lax.fori_loop(0, stop_block, one_block, start_state)
    return (weighted_sum / row_total[..., None], running_top + jnp.log(row_total))


def attend_back(
    query_rows,
    grad_rows,
    attended_rows,
    log_total,
    keys_seq,
    values_seq,
    query_index,
    query_pos,
    sequence_positions,
    last_row,
):
    token_length = keys_seq.shape[0]
    block_length = min(512, token_length)
    count_of_rows = query_rows.shape[1]
    score_scale = 1.0 / math.sqrt(HEAD_SIZE)
    row_dot = jnp.sum(grad_rows.astype(jnp.float32) * attended_rows, axis=-1)

    def one_block(block_number, state_in):
        grad_query, score_grads, prob_store = state_in
        offset = block_number * block_length
        split_key_heads = lax.dynamic_slice_in_dim(keys_seq, offset, block_length, 0).reshape(
            block_length, KEY_VALUE_HEADS, HEAD_SIZE
        )
        split_value_heads = lax.dynamic_slice_in_dim(values_seq, offset, block_length, 0).reshape(
            block_length, KEY_VALUE_HEADS, HEAD_SIZE
        )
        raw_scores = (
            jnp.einsum(
                "hrd,nhd->hrn", query_rows, split_key_heads, preferred_element_type=jnp.float32
            )
            * score_scale
        )
        key_index = offset + jnp.arange(block_length, dtype=jnp.int32)
        key_pos = lax.dynamic_slice_in_dim(sequence_positions, offset, block_length, 0)
        allowed = visible(query_index, query_pos, key_index, key_pos)[None]
        probabilities = jnp.where(allowed, jnp.exp(raw_scores - log_total[..., None]), 0.0)
        grad_probs = jnp.einsum(
            "hrd,nhd->hrn", grad_rows, split_value_heads, preferred_element_type=jnp.float32
        )
        grad_scores = (probabilities * (grad_probs - row_dot[..., None]) * score_scale).astype(
            jnp.bfloat16
        )
        grad_query = grad_query + jnp.einsum(
            "hrn,nhd->hrd", grad_scores, split_key_heads, preferred_element_type=jnp.float32
        )
        score_grads = lax.dynamic_update_slice_in_dim(score_grads, grad_scores, offset, 2)
        prob_store = lax.dynamic_update_slice_in_dim(
            prob_store, probabilities.astype(jnp.bfloat16), offset, 2
        )
        return (grad_query, score_grads, prob_store)

    stop_block = last_row // block_length + 1
    start_state = (
        jnp.zeros(query_rows.shape, jnp.float32),
        jnp.zeros((KEY_VALUE_HEADS, count_of_rows, token_length), jnp.bfloat16),
        jnp.zeros((KEY_VALUE_HEADS, count_of_rows, token_length), jnp.bfloat16),
    )
    return lax.fori_loop(0, stop_block, one_block, start_state)


def on_device(
    hidden_in,
    positions,
    attn_gain,
    w_query,
    key_projection_weight,
    w_value,
    w_out,
    ffn_gain,
    w_gate,
    w_up,
    w_down,
    out_grad,
):
    micro_count = hidden_in.shape[0]
    span_length = hidden_in.shape[1]
    width = hidden_in.shape[2]
    total_rows = micro_count * span_length
    heads_per_group = QUERY_HEADS // KEY_VALUE_HEADS
    ctx_rank = lax.axis_index("ctx")
    pos_all = lax.all_gather(positions, "ctx", axis=1, tiled=True)
    attn_row = attn_gain.reshape(1, -1)
    ffn_row = ffn_gain.reshape(1, -1)
    forward_weights = fetch_weights(
        w_query, key_projection_weight, w_value, w_out, w_gate, w_up, w_down, attn_row, ffn_row
    )
    (
        (full_query, complete_key, full_value, full_out, full_gate, full_up, full_down),
        gain_attn,
        gain_ffn,
    ) = forward_weights
    local_index = ctx_rank * span_length + jnp.arange(span_length, dtype=jnp.int32)
    last_row = ctx_rank * span_length + span_length - 1
    query_index = jnp.tile(local_index, heads_per_group)
    inputs_flat = hidden_in.reshape(total_rows, width).astype(jnp.float32)
    pos_flat = positions.reshape(total_rows)
    cosine_table, sine_table = angles(pos_flat)
    scale_one = norm_scale(inputs_flat)
    first_normed_input = (inputs_flat * scale_one * gain_attn).astype(jnp.bfloat16)
    query_matrix = rotary_pair_rotation(
        product_reduced_precision(first_normed_input, full_query),
        cosine_table,
        sine_table,
        QUERY_HEADS,
    ).astype(jnp.bfloat16)
    local_keys = rotary_pair_rotation(
        product_reduced_precision(first_normed_input, complete_key),
        cosine_table,
        sine_table,
        KEY_VALUE_HEADS,
    ).astype(jnp.bfloat16)
    values_own = product_reduced_precision(first_normed_input, full_value).astype(jnp.bfloat16)
    keys_every, values_every = (
        lax.all_gather(local_keys.reshape(micro_count, span_length, -1), "ctx", axis=1, tiled=True),
        lax.all_gather(values_own.reshape(micro_count, span_length, -1), "ctx", axis=1, tiled=True),
    )
    query_row_list, attended_row_list, log_list, attended_parts = ([], [], [], [])
    for micro_step in range(micro_count):
        query_pos = jnp.tile(positions[micro_step], heads_per_group)
        query_rows = to_rows(
            query_matrix[micro_step * span_length : (micro_step + 1) * span_length], span_length
        )
        attended_rows, log_total = attend(
            query_rows,
            keys_every[micro_step],
            values_every[micro_step],
            query_index,
            query_pos,
            pos_all[micro_step],
            last_row,
        )
        query_row_list.append(query_rows)
        attended_row_list.append(attended_rows)
        log_list.append(log_total)
        attended_parts.append(from_rows(attended_rows, span_length).astype(jnp.bfloat16))
    attended = jnp.concatenate(attended_parts, axis=0)
    residual_mid = inputs_flat + product_reduced_precision(attended, full_out)
    scale_two = norm_scale(residual_mid)
    normed_two = (residual_mid * scale_two * gain_ffn).astype(jnp.bfloat16)
    gate_proj = product_reduced_precision(normed_two, full_gate)
    up_proj = product_reduced_precision(normed_two, full_up)
    sigmoid_gate = jax.nn.sigmoid(gate_proj)
    hidden = (gate_proj * sigmoid_gate * up_proj).astype(jnp.bfloat16)
    layer_out = (residual_mid + product_reduced_precision(hidden, full_down)).astype(jnp.bfloat16)
    (
        (full_query, complete_key, full_value, full_out, full_gate, full_up, full_down),
        gain_attn,
        gain_ffn,
    ) = forward_weights
    grad_top = out_grad.reshape(total_rows, width)
    grad_hidden = matmul_back(grad_top, full_down)
    grad_gate = (
        grad_hidden * up_proj * sigmoid_gate * (1.0 + gate_proj * (1.0 - sigmoid_gate))
    ).astype(jnp.bfloat16)
    grad_up = (grad_hidden * gate_proj * sigmoid_gate).astype(jnp.bfloat16)
    grad_normed_two = matmul_back(grad_gate, full_gate) + matmul_back(grad_up, full_up)
    weighted_two = grad_normed_two * gain_ffn
    ffn_sum = jnp.sum(grad_normed_two * residual_mid * scale_two, axis=0)
    grad_mid = (
        grad_top.astype(jnp.float32)
        + scale_two * weighted_two
        - residual_mid
        * (scale_two * scale_two * scale_two)
        * jnp.mean(weighted_two * residual_mid, axis=-1, keepdims=True)
    )
    grad_mid_low = grad_mid.astype(jnp.bfloat16)
    grad_attended = matmul_back(grad_mid_low, full_out).astype(jnp.bfloat16)
    key_width = local_keys.shape[1]
    query_grad_parts, key_grad_parts, value_grad_parts = ([], [], [])
    for micro_step in range(micro_count):
        query_pos = jnp.tile(positions[micro_step], heads_per_group)
        query_rows = query_row_list[micro_step]
        grad_rows = to_rows(
            grad_attended[micro_step * span_length : (micro_step + 1) * span_length], span_length
        )
        grad_query_rows, score_grads, prob_store = attend_back(
            query_rows,
            grad_rows,
            attended_row_list[micro_step],
            log_list[micro_step],
            keys_every[micro_step],
            values_every[micro_step],
            query_index,
            query_pos,
            pos_all[micro_step],
            last_row,
        )

        def key_terms(
            start,
            count,
            score_grads=score_grads,
            prob_store=prob_store,
            query_rows=query_rows,
            grad_rows=grad_rows,
        ):
            key_term = jnp.einsum(
                "hrn,hrd->nhd", score_grads, query_rows, preferred_element_type=jnp.float32
            ).reshape(count, key_width)
            value_term = jnp.einsum(
                "hrn,hrd->nhd", prob_store, grad_rows, preferred_element_type=jnp.float32
            ).reshape(count, key_width)
            return jnp.concatenate([key_term, value_term], axis=1)

        key_value_grads = lax.psum_scatter(
            key_terms(jnp.int32(0), span_length * lax.axis_size("ctx")).astype(jnp.bfloat16),
            "ctx",
            scatter_dimension=0,
            tiled=True,
        ).astype(jnp.float32)
        query_grad_parts.append(from_rows(grad_query_rows, span_length))
        key_grad_parts.append(key_value_grads[:, :key_width])
        value_grad_parts.append(key_value_grads[:, key_width:])
    grad_query_pre = rotary_pair_rotation(
        jnp.concatenate(query_grad_parts, axis=0), cosine_table, -sine_table, QUERY_HEADS
    ).astype(jnp.bfloat16)
    key_gradient_unrotated = rotary_pair_rotation(
        jnp.concatenate(key_grad_parts, axis=0), cosine_table, -sine_table, KEY_VALUE_HEADS
    ).astype(jnp.bfloat16)
    grad_value_low = jnp.concatenate(value_grad_parts, axis=0).astype(jnp.bfloat16)
    grad_normed_one = (
        matmul_back(grad_query_pre, full_query)
        + matmul_back(key_gradient_unrotated, complete_key)
        + matmul_back(grad_value_low, full_value)
    )
    weighted_one = grad_normed_one * gain_attn
    attn_sum = jnp.sum(grad_normed_one * inputs_flat * scale_one, axis=0)
    grad_input = (
        grad_mid
        + scale_one * weighted_one
        - inputs_flat
        * (scale_one * scale_one * scale_one)
        * jnp.mean(weighted_one * inputs_flat, axis=-1, keepdims=True)
    )
    grad_list = (
        outer_product(first_normed_input, grad_query_pre),
        outer_product(first_normed_input, key_gradient_unrotated),
        outer_product(first_normed_input, grad_value_low),
        outer_product(attended, grad_mid_low),
        outer_product(normed_two, grad_gate),
        outer_product(normed_two, grad_up),
        outer_product(hidden, grad_top),
    )
    matrices, attn_grad_own, ffn_grad_own = reduce_grads(grad_list, attn_sum, ffn_sum)
    return (
        layer_out.reshape(micro_count, span_length, width),
        grad_input.astype(jnp.bfloat16).reshape(micro_count, span_length, width),
        attn_grad_own,
        matrices[0],
        matrices[1],
        matrices[2],
        matrices[3],
        ffn_grad_own,
        matrices[4],
        matrices[5],
        matrices[6],
    )


def solution(mesh):
    placed = (
        P("dp", "ctx", None),
        P("dp", "ctx"),
        P("ctx"),
        P("dp", "ctx"),
        P("dp", "ctx"),
        P("dp", "ctx"),
        P("dp", "ctx"),
        P("ctx"),
        P("dp", "ctx"),
        P("dp", "ctx"),
        P("dp", "ctx"),
        P("dp", "ctx", None),
    )
    return jax.shard_map(
        on_device,
        mesh=mesh,
        in_specs=placed,
        out_specs=(
            P("dp", "ctx", None),
            P("dp", "ctx", None),
            P("ctx"),
            P("dp", "ctx"),
            P("dp", "ctx"),
            P("dp", "ctx"),
            P("dp", "ctx"),
            P("ctx"),
            P("dp", "ctx"),
            P("dp", "ctx"),
            P("dp", "ctx"),
        ),
        check_vma=False,
    )
```

profile of v0, /device:TPU:0, one launch (start us, length us, event | category | flops | bytes accessed | tf_op | source)
XLA Modules:
  0.0 1048.0 jit_solution(16831399521310134453)
XLA Ops:
  7.2 10.8 %all_gather.62 = bf16[960,120]{1,0:T(8,128)(2,1)S(1)} all-gather(bf16[240,120]{1,0:T(8,128)(2,1)} %param.23), channel_id=1, replica_groups=mesh['dp'=4,'ctx'=8] {'dp'}, dimensions={0}, use_global_device_ids=true | all-gather | bytes 288000 | tf_op jit(solution)/shard_map/all_gather | solution.py:85
  22.7 15.9 %all-reduce.12 = (bf16[960]{0:T(1024)(128)(2,1)S(1)}, bf16[960]{0:T(1024)(128)(2,1)}) all-reduce(bf16[960]{0:T(1024)(128)(2,1)S(1)} %dynamic-update-slice, bf16[960]{0:T(1024)(128)(2,1)S(1)} %dynamic-update-slice.1), channel_id=2, replica_groups=mesh['dp'=4,'ctx'=8] {'ctx'}, use_global_device_ids=true, to_apply=%add | all-reduce | flops 1920 | bytes 7680
  51.1 15.4 %all_gather.60 = bf16[960,320]{0,1:T(8,128)(2,1)S(1)} all-gather(bf16[960,40]{0,1:T(8,128)(2,1)S(1)} %reshape.794), channel_id=1, replica_groups=mesh['dp'=4,'ctx'=8] {'ctx'}, dimensions={1}, use_global_device_ids=true | all-gather | bytes 691200 | tf_op jit(solution)/shard_map/all_gather | solution.py:95
  78.0 17.5 %all_gather.65 = bf16[960,320]{0,1:T(8,128)(2,1)S(1)} all-gather(bf16[960,40]{0,1:T(8,128)(2,1)S(1)} %reshape.796), channel_id=1, replica_groups=mesh['dp'=4,'ctx'=8] {'ctx'}, dimensions={1}, use_global_device_ids=true | all-gather | bytes 691200 | tf_op jit(solution)/shard_map/all_gather | solution.py:96
  106.8 11.0 %all-gather.4 = bf16[4,240,320]{1,2,0:T(8,128)(2,1)S(1)} all-gather(bf16[1,240,320]{1,2,0:T(8,128)(2,1)S(1)} %bitcast.391), channel_id=1, replica_groups=mesh['dp'=4,'ctx'=8] {'dp'}, dimensions={0}, use_global_device_ids=true | all-gather | bytes 768000 | tf_op jit(solution)/shard_map/all_gather | solution.py:89
  121.8 9.9 all-gather.5
  135.7 11.8 %all_gather.74 = bf16[2560,120]{0,1:T(8,128)(2,1)} all-gather(bf16[640,120]{0,1:T(8,128)(2,1)S(1)} %copy-done.38), channel_id=1, replica_groups=mesh['dp'=4,'ctx'=8] {'dp'}, dimensions={0}, use_global_device_ids=true | all-gather | bytes 768000 | tf_op jit(solution)/shard_map/all_gather | solution.py:91
  147.6 13.0 %all_gather.57 = s32[2,2048]{1,0:T(2,128)S(1)} all-gather(s32[2,256]{1,0:T(2,128)S(1)} %copy-done.50), channel_id=1, replica_groups=mesh['dp'=4,'ctx'=8] {'ctx'}, dimensions={1}, use_global_device_ids=true | all-gather | bytes 18432 | tf_op jit(solution)/shard_map/all_gather | solution.py:310
  199.1 9.0 while.61
  235.2 49.2 %all-gather.24.cloned.1.call-done = bf16[960,2560]{0,1:T(8,128)(2,1)} async-done(((bf16[960,320]{0,1:T(8,128)(2,1)}), bf16[960,2560]{0,1:T(8,128)(2,1)}) %all-gather.24.cloned.1.call-update) | async-done | bytes 4915216 | tf_op jit(solution)/shard_map/all_gather | solution.py:99
  291.6 46.5 %all-gather.26.cloned.1.call-done = bf16[2560,960]{0,1:T(8,128)(2,1)} async-done(((bf16[2560,120]{0,1:T(8,128)(2,1)}), bf16[2560,960]{0,1:T(8,128)(2,1)}) %all-gather.26.cloned.1.call-update) | async-done | bytes 4915216 | tf_op jit(solution)/shard_map/all_gather | solution.py:100
  338.1 10.5 %multiply_convert_fusion = (bf16[512,2560]{1,0:T(8,128)(2,1)S(1)}, bf16[512,2560]{1,0:T(8,128)(2,1)S(1)}, bf16[512,2560]{1,0:T(8,128)(2,1)}) fusion(f32[512,2560]{1,0:T(8,128)} %fusion.79, f32[512,2560]{1,0:T(8,128)} %fusion.80, bf16[512,960]{0,1:T(8,128)(2,1)S(1)} %bitcast.357, bf16[2560,960]{0,1:T(8,128)(2,1)} %all-gather.26.cloned.1.call-done), kind=kOutput, calls=%fused_computation.73 | convolution fusion | flops 2537553920 | bytes 24248320 | tf_op jit(solution)/shard_map/tf,df->td/dot_general | solution.py:74
  378.3 11.5 %while.62 = (s32[]{:T(128)}, f32[5,768,64]{1,2,0:T(8,128)S(1)}, bf16[5,768,2048]{1,2,0:T(8,128)(2,1)}, bf16[5,768,2048]{1,2,0:T(8,128)(2,1)}, s32[]{:T(128)}, /*...) while((s32[]{:T(128)}, f32[5,768,64]{1,2,0:T(8,128)S(1)}, ...), condition=%wide.region_13.14_spmd.clone, body=%wide.region_12.13_spmd.clone.sunk | while | flops 778813952 | bytes 37962984 | solution.py:287
  409.4 11.2 %while.63 = (s32[]{:T(128)}, f32[5,768,64]{1,2,0:T(8,128)S(1)}, bf16[5,768,2048]{1,2,0:T(8,128)(2,1)}, bf16[5,768,2048]{1,2,0:T(8,128)(2,1)}, s32[]{:T(128)}, /*...) while((s32[]{:T(128)}, f32[5,768,64]{1,2,0:T(8,128)S(1)}, ...), condition=%wide.region_16.17_spmd.clone, body=%wide.region_15.16_spmd.clone.sunk | while | flops 778813952 | bytes 39929088 | solution.py:287
  443.5 10.3 convolution_convert_fusion.6
  453.8 10.3 convolution_convert_fusion.5
  465.9 10.3 convolution_convert_fusion.4
  476.3 10.3 convolution_convert_fusion.3
  495.7 41.3 %reduce-scatter.43.cloned.1.call-done = bf16[120,960]{1,0:T(8,128)(2,1)} async-done(((bf16[960,960]{1,0:T(8,128)(2,1)}), bf16[120,960]{1,0:T(8,128)(2,1)}) %reduce-scatter.43.cloned.1.call-update) | async-done | bytes 230416
  538.9 34.5 %reduce-scatter.45.cloned.1.call-done = bf16[120,960]{1,0:T(8,128)(2,1)} async-done(((bf16[960,960]{1,0:T(8,128)(2,1)}), bf16[120,960]{1,0:T(8,128)(2,1)}) %reduce-scatter.45.cloned.1.call-update) | async-done | bytes 230416
  575.5 35.9 %reduce-scatter.29.cloned.1.call-done = bf16[256,640]{0,1:T(8,128)(2,1)} async-done(((bf16[2048,640]{0,1:T(8,128)(2,1)}), bf16[256,640]{0,1:T(8,128)(2,1)}) %reduce-scatter.29.cloned.1.call-update) | async-done | bytes 327696 | tf_op jit(solution)/shard_map/reduce_scatter | solution.py:434
  613.1 37.2 %reduce-scatter.31.cloned.1.call-done = bf16[256,640]{0,1:T(8,128)(2,1)} async-done(((bf16[2048,640]{0,1:T(8,128)(2,1)}), bf16[256,640]{0,1:T(8,128)(2,1)}) %reduce-scatter.31.cloned.1.call-update) | async-done | bytes 327696 | tf_op jit(solution)/shard_map/reduce_scatter | solution.py:434
  675.5 32.9 %reduce-scatter.41.cloned.1.call-done = bf16[2560,120]{0,1:T(8,128)(2,1)} async-done(((bf16[2560,960]{0,1:T(8,128)(2,1)}), bf16[2560,120]{0,1:T(8,128)(2,1)}) %reduce-scatter.41.cloned.1.call-update) | async-done | bytes 614416 | tf_op jit(solution)/shard_map/reduce_scatter | solution.py:136
  721.1 12.5 %reduce-scatter.49.cloned.1.call-done = bf16[240,120]{1,0:T(8,128)(2,1)} async-done(((bf16[960,120]{1,0:T(8,128)(2,1)}), bf16[240,120]{1,0:T(8,128)(2,1)}) %reduce-scatter.49.cloned.1.call-update) | async-done | bytes 57616
  735.1 25.3 %reduce-scatter.51.cloned.1.call-done = bf16[240,120]{1,0:T(8,128)(2,1)} async-done(((bf16[960,120]{1,0:T(8,128)(2,1)}), bf16[240,120]{1,0:T(8,128)(2,1)}) %reduce-scatter.51.cloned.1.call-update) | async-done | bytes 57616
  765.1 28.8 %reduce-scatter.35.cloned.1.call-done = bf16[960,40]{0,1:T(8,128)(2,1)} async-done(((bf16[960,320]{0,1:T(8,128)(2,1)}), bf16[960,40]{0,1:T(8,128)(2,1)}) %reduce-scatter.35.cloned.1.call-update) | async-done | bytes 76816 | tf_op jit(solution)/shard_map/reduce_scatter | solution.py:124
  793.9 32.2 %reduce-scatter.33.cloned.1.call-done = bf16[960,40]{0,1:T(8,128)(2,1)} async-done(((bf16[960,320]{0,1:T(8,128)(2,1)}), bf16[960,40]{0,1:T(8,128)(2,1)}) %reduce-scatter.33.cloned.1.call-update) | async-done | bytes 76816 | tf_op jit(solution)/shard_map/reduce_scatter | solution.py:121
  826.1 60.4 %reduce-scatter.37.cloned.1.call-done = bf16[960,320]{0,1:T(8,128)(2,1)} async-done(((bf16[960,2560]{0,1:T(8,128)(2,1)}), bf16[960,320]{0,1:T(8,128)(2,1)}) %reduce-scatter.37.cloned.1.call-update) | async-done | bytes 614416 | tf_op jit(solution)/shard_map/reduce_scatter | solution.py:130
  886.4 60.4 %reduce-scatter.39.cloned.1.call-done = bf16[960,320]{0,1:T(8,128)(2,1)} async-done(((bf16[960,2560]{0,1:T(8,128)(2,1)}), bf16[960,320]{0,1:T(8,128)(2,1)}) %reduce-scatter.39.cloned.1.call-update) | async-done | bytes 614416 | tf_op jit(solution)/shard_map/reduce_scatter | solution.py:133
  951.5 10.2 all-reduce.10
  961.8 13.9 %all-reduce.11 = (bf16[1,960]{1,0:T(2,128)(2,1)S(1)}, bf16[1,960]{1,0:T(2,128)(2,1)S(1)}) all-reduce(bf16[1,960]{1,0:T(2,128)(2,1)S(1)} %convert_element_type.258, bf16[1,960]{1,0:T(2,128)(2,1)S(1)} %convert_element_type.268), channel_id=6, replica_groups=mesh['dp'=4,'ctx'=8] {'ctx'}, use_global_device_ids=true, to_apply=%region_22.23.clone | all-reduce | flops 1920 | bytes 7680
  982.2 55.2 %all-reduce.16.cloned.1.call-done = (bf16[960,40]{0,1:T(8,128)(2,1)}, bf16[960,40]{0,1:T(8,128)(2,1)}, bf16[960,320]{0,1:T(8,128)(2,1)}, bf16[960,320]{0,1:T(8,128)(2,1)}) async-done(((bf16[960,40]{0,1:T(8,128)(2,1)}, bf16[960,40]{0,1:T(8,128)(2,1)}, bf16[960,320]{0,1:T(8,128)(2,1)}, bf16[960,320]{0,1:T(8,128)(2,1)}), (bf16[960,40]{0,1:T(8,128)(2,1)}, bf16[960,40]{0,1:T(8,128)(2,1)}, ...) | async-done | bytes 1382416
  (350 shorter events, 304.6 us)
Async XLA Ops:
  7.2 158.1 %all-gather.16.cloned.1.call-start = ((), (), s32[]{:S(2)}) async-start(), calls=%async_computation.13 | async-start | bytes 2211840 | tf_op jit(solution)/shard_map/all_gather | solution.py:94
  19.0 155.7 %all-gather.14.cloned.1.call-start = ((), (), s32[]{:S(2)}) async-start(), calls=%async_computation.12 | async-start | bytes 2949120 | tf_op jit(solution)/shard_map/all_gather | solution.py:343
  38.6 122.0 %copy-start.34 = (f32[960]{0:T(1024)}, f32[960]{0:T(1024)S(1)}, u32[]{:S(2)}) copy-start(f32[960]{0:T(1024)S(1)} %mul.488) | copy-start | bytes 11524
  51.1 117.3 %copy-start.24 = (f32[512,32]{0,1:T(8,128)}, f32[512,32]{0,1:T(8,128)S(1)}, u32[]{:S(2)}) copy-start(f32[512,32]{0,1:T(8,128)S(1)} %get-tuple-element.626) | copy-start | bytes 196612
  68.8 109.5 %all-gather.18.cloned.1.call-start = ((), (), s32[]{:S(2)}) async-start(), calls=%async_computation.14 | async-start | bytes 2949120 | tf_op jit(solution)/shard_map/all_gather | solution.py:344
  69.3 145.1 %copy-start = (f32[2,120,8,256]{3,2,0,1:T(8,128)}, f32[2,120,8,256]{3,2,0,1:T(8,128)S(1)}, u32[]{:S(2)}) copy-start(f32[2,120,8,256]{3,2,0,1:T(8,128)S(1)} %copy.159) | copy-start | bytes 5898244
  97.7 116.8 %all-gather.20.cloned.1.call-start = ((), (), s32[]{:S(2)}) async-start(), calls=%async_computation.15 | async-start | bytes 2211840 | tf_op jit(solution)/shard_map/all_gather | solution.py:97
  106.7 121.2 %all-gather.22.cloned.1.call-start = ((), (), s32[]{:S(2)}) async-start(), calls=%async_computation.16 | async-start | bytes 5898240 | tf_op jit(solution)/shard_map/all_gather | solution.py:98
  121.7 162.6 %all-gather.24.cloned.1.call-start = ((), (), s32[]{:S(2)}) async-start(), calls=%async_computation.17 | async-start | bytes 5898240 | tf_op jit(solution)/shard_map/all_gather | solution.py:99
  121.8 38.8 %copy-start.48 = (f32[2,256]{1,0:T(2,128)S(1)}, f32[2,256]{1,0:T(2,128)}, u32[]{:S(2)}) copy-start(f32[2,256]{1,0:T(2,128)} %copy-done.47) | copy-start | bytes 6148
  135.7 202.5 %all-gather.26.cloned.1.call-start = ((), (), s32[]{:S(2)}) async-start(), calls=%async_computation.18 | async-start | bytes 5529600 | tf_op jit(solution)/shard_map/all_gather | solution.py:100
  147.5 389.5 %reduce-scatter.43.cloned.1.call-start = ((), (), s32[]{:S(2)}) async-start(), calls=%async_computation.26 | async-start | bytes 2211840
  219.0 65.4 %copy-start.28 = (bf16[512,960]{0,1:T(8,128)(2,1)}, bf16[512,960]{0,1:T(8,128)(2,1)S(1)}, u32[]{:S(2)}) copy-start(bf16[512,960]{0,1:T(8,128)(2,1)S(1)} %multiply_convert_fusion.3) | copy-start | bytes 2949124
  235.2 103.0 %copy-start.18 = (bf16[2,120,8,256]{3,2,0,1:T(8,128)(2,1)S(1)}, bf16[2,120,8,256]{3,2,0,1:T(8,128)(2,1)}, u32[]{:S(2)}) copy-start(bf16[2,120,8,256]{3,2,0,1:T(8,128)(2,1)} %copy.160) | copy-start | bytes 2949124
  435.6 137.8 %reduce-scatter.45.cloned.1.call-start = ((), (), s32[]{:S(2)}) async-start(), calls=%async_computation.27 | async-start | bytes 2211840
  443.4 168.0 %reduce-scatter.29.cloned.1.call-start = ((), (), s32[]{:S(2)}) async-start(), calls=%async_computation.19 | async-start | bytes 2949120 | tf_op jit(solution)/shard_map/reduce_scatter | solution.py:434
  465.8 184.4 %reduce-scatter.31.cloned.1.call-start = ((), (), s32[]{:S(2)}) async-start(), calls=%async_computation.20 | async-start | bytes 2949120 | tf_op jit(solution)/shard_map/reduce_scatter | solution.py:434
  488.3 220.0 %reduce-scatter.41.cloned.1.call-start = ((), (), s32[]{:S(2)}) async-start(), calls=%async_computation.25 | async-start | bytes 5529600 | tf_op jit(solution)/shard_map/reduce_scatter | solution.py:136
  495.6 157.0 %copy-start.1 = (f32[2,120,8,256]{3,2,0,1:T(8,128)S(1)}, f32[2,120,8,256]{3,2,0,1:T(8,128)}, u32[]{:S(2)}) copy-start(f32[2,120,8,256]{3,2,0,1:T(8,128)} %copy-done) | copy-start | bytes 5898244
  495.7 157.0 %copy-start.35 = (f32[960]{0:T(1024)S(1)}, f32[960]{0:T(1024)}, u32[]{:S(2)}) copy-start(f32[960]{0:T(1024)} %copy-done.34) | copy-start | bytes 11524
  495.7 157.0 %copy-start.40 = (f32[1,2,2,128]{3,1,2,0:T(2,128)S(1)}, f32[1,2,2,128]{3,1,2,0:T(2,128)}, u32[]{:S(2)}) copy-start(f32[1,2,2,128]{3,1,2,0:T(2,128)} %copy-done.39) | copy-start | bytes 6148
  495.7 238.0 %reduce-scatter.49.cloned.1.call-start = ((), (), s32[]{:S(2)}) async-start(), calls=%async_computation.29 | async-start | bytes 307200
  538.8 221.6 %reduce-scatter.51.cloned.1.call-start = ((), (), s32[]{:S(2)}) async-start(), calls=%async_computation.30 | async-start | bytes 307200
  575.2 218.7 %reduce-scatter.35.cloned.1.call-start = ((), (), s32[]{:S(2)}) async-start(), calls=%async_computation.22 | async-start | bytes 737280 | tf_op jit(solution)/shard_map/reduce_scatter | solution.py:124
  654.2 171.9 %reduce-scatter.33.cloned.1.call-start = ((), (), s32[]{:S(2)}) async-start(), calls=%async_computation.21 | async-start | bytes 737280 | tf_op jit(solution)/shard_map/reduce_scatter | solution.py:121
  657.8 228.6 %reduce-scatter.37.cloned.1.call-start = ((), (), s32[]{:S(2)}) async-start(), calls=%async_computation.23 | async-start | bytes 5898240 | tf_op jit(solution)/shard_map/reduce_scatter | solution.py:130
  665.2 281.7 %reduce-scatter.39.cloned.1.call-start = ((), (), s32[]{:S(2)}) async-start(), calls=%async_computation.24 | async-start | bytes 5898240 | tf_op jit(solution)/shard_map/reduce_scatter | solution.py:133
  673.0 37.6 %copy-start.31 = (bf16[512,15,64]{0,2,1:T(8,128)(2,1)S(1)}, bf16[512,15,64]{0,2,1:T(8,128)(2,1)}, u32[]{:S(2)}) copy-start(bf16[512,15,64]{0,2,1:T(8,128)(2,1)} %copy-done.30) | copy-start | bytes 2949124
  673.0 307.4 %reduce-scatter.47.cloned.1.call-start = ((), (), s32[]{:S(2)}) async-start(), calls=%async_computation.28 | async-start | bytes 819200
  710.5 326.8 %all-reduce.16.cloned.1.call-start = ((), (), s32[]{:S(2)}) async-start(), calls=%async_computation.31 | async-start | bytes 2949120
  721.1 225.8 %copy-start.15 = (bf16[960,320]{0,1:T(8,128)(2,1)S(1)}, bf16[960,320]{0,1:T(8,128)(2,1)}, u32[]{:S(2)}) copy-start(bf16[960,320]{0,1:T(8,128)(2,1)} %copy-done.14) | copy-start | bytes 1843204
  721.1 225.8 %copy-start.27 = (bf16[256,320]{0,1:T(8,128)(2,1)S(1)}, bf16[256,320]{0,1:T(8,128)(2,1)}, u32[]{:S(2)}) copy-start(bf16[256,320]{0,1:T(8,128)(2,1)} %copy-done.26) | copy-start | bytes 491524
  (47 other events, 332.0 us)
Sparse Core Ops, SparseCore 0:
  19.1 28.4 all-gather.15
  69.0 37.4 all-gather.13
  108.7 33.4 all-gather.17
  144.2 26.6 all-gather.19
  172.4 55.5 all-gather.21
  229.4 54.8 all-gather.23
  286.0 52.0 all-gather.25
  435.8 101.2 reduce-scatter.42
  539.5 33.9 reduce-scatter.44
  575.6 35.8 reduce-scatter.28
  613.7 36.4 reduce-scatter.30
  652.4 55.8 reduce-scatter.40
  711.7 21.9 reduce-scatter.48
  736.8 23.5 reduce-scatter.50
  762.6 31.2 reduce-scatter.34
  796.6 29.4 reduce-scatter.32
  828.2 58.1 reduce-scatter.36
  888.6 58.2 reduce-scatter.38
  949.8 23.8 reduce-scatter.46
  977.3 60.0 all-reduce.15
where the time goes:
time: 1060 us; the launch traced here: 1050 us
  waiting for transfers between devices  562 us (53%)
  matrix products  159 us (15%)
  blocking collectives  153 us (14%)
  local copies, waits for them, and re-layouts  118 us (11%)
  other arithmetic  36.3 us (3%)
  between operations  17.4 us (2%)
    unnamed x26, waiting for transfers between devices  169 us
    reduce_scatter x2, waiting for transfers between devices, on_device(): lax.psum_scatter(key_terms(jnp.int32(0), span_length * lax.axis_size('ctx...  73.1 us
    reduce_scatter x1, waiting for transfers between devices, reduce_grads(): lax.psum_scatter(grad_list[5].astype(jnp.bfloat16), 'ctx', scatter_dimens...  60.4 us
    reduce_scatter x1, waiting for transfers between devices, reduce_grads(): lax.psum_scatter(grad_list[4].astype(jnp.bfloat16), 'ctx', scatter_dimens...  60.4 us
    all_gather x1, waiting for transfers between devices, fetch_weights(): lax.all_gather(tall[5], 'ctx', axis=1, tiled=True)  49.2 us
    all_gather x1, waiting for transfers between devices, fetch_weights(): lax.all_gather(tall[6], 'ctx', axis=1, tiled=True)  46.5 us
    dot_general x7, matrix products, matmul_back(): jnp.einsum('tf,df->td', left_rows, weight_full, preferred_element_type=jn...  34.8 us
    unnamed x127, local copies, waits for them, and re-layouts  33.5 us
  transfers between devices with their start and end apart: 20, of which 15 were waited for; matrix products, arithmetic and copies ran while one was open for 19% of the time, Pallas kernels for 0%

commit v1 on v0

v1 whole, which is shorter than its diff:
```python
import functools

import jax
import jax.numpy as jnp
import numpy as np
from jax import lax
from jax.experimental import pallas as pl
from jax.experimental.pallas import tpu as pltpu
from jax.sharding import PartitionSpec as P

QUERY_HEADS = 15
KEY_VALUE_HEADS = 5
HEAD_SIZE = 64
GROUP = QUERY_HEADS // KEY_VALUE_HEADS
HALF = HEAD_SIZE // 2

epsilon = 1e-05
theta_base = 100000.0
masked_score = -1e30
lowest_top = -1e29
score_scale = 0.125
VMEM_BYTES = 56 * 1024 * 1024

BF = jnp.bfloat16
F32 = jnp.float32


def dot_nn(a, b):
    return lax.dot_general(a, b, (((1,), (0,)), ((), ())), preferred_element_type=F32)


def dot_nt(a, b):
    return lax.dot_general(a, b, (((1,), (1,)), ((), ())), preferred_element_type=F32)


def dot_tn(a, b):
    return lax.dot_general(a, b, (((0,), (0,)), ((), ())), preferred_element_type=F32)


def vmem_spec():
    return pl.BlockSpec(memory_space=pltpu.VMEM)


def smem_spec():
    return pl.BlockSpec(memory_space=pltpu.SMEM)


def params():
    return pltpu.CompilerParams(vmem_limit_bytes=VMEM_BYTES)


def cost(flops, bytes_accessed, transcendentals=0):
    return pl.CostEstimate(
        flops=int(flops), bytes_accessed=int(bytes_accessed), transcendentals=int(transcendentals)
    )


def rotate(value, cosine, sine, limit=None):
    width = value.shape[1]
    lane = lax.broadcasted_iota(jnp.int32, value.shape, 1)
    ahead = pltpu.roll(value, width - HALF, 1)
    behind = pltpu.roll(value, HALF, 1)
    swapped = jnp.where(lane % HEAD_SIZE < HALF, ahead, behind)
    copies = width // 128
    cos_wide = jnp.concatenate([cosine] * copies, axis=1)
    sin_wide = jnp.concatenate([sine] * copies, axis=1)
    turned = value * cos_wide + swapped * sin_wide
    if limit is not None:
        turned = jnp.where(lane < limit, turned, value)
    return turned


def projection_kernel(count, columns, turn, index_ref, x_ref, *rest):
    weights = rest[:count]
    rest = rest[count:]
    if turn:
        cos_ref, sin_ref, out_ref = rest
    else:
        (out_ref,) = rest
    for start in range(0, columns, 256):
        size = min(256, columns - start)
        total = None
        for m in range(count):
            term = dot_nt(x_ref[index_ref[m]], weights[m][start : start + size, :])
            total = term if total is None else total + term
        if turn > start:
            total = rotate(total, cos_ref[...], sin_ref[...], turn - start if turn < start + size else None)
        out_ref[:, start : start + size] = total.astype(out_ref.dtype)


def project(x_blocks, index, weights, out_dtype, tables=None, turn=0):
    count = len(weights)
    rows = x_blocks.shape[1]
    columns = weights[0].shape[0]
    depth = x_blocks.shape[2]
    operands = [index, x_blocks, *weights] + (list(tables) if tables else [])
    return pl.pallas_call(
        functools.partial(projection_kernel, count, columns, turn),
        out_shape=jax.ShapeDtypeStruct((rows, columns), out_dtype),
        in_specs=[smem_spec()] + [vmem_spec()] * (len(operands) - 1),
        out_specs=vmem_spec(),
        compiler_params=params(),
        cost_estimate=cost(2 * rows * columns * depth * count, 2 * columns * depth * count + 4 * rows * columns),
    )(*operands)


def projection_back_kernel(count, columns, index_ref, dy_ref, x_ref, *rest):
    weights = rest[:count]
    dx_ref, dw_ref = rest[count:]
    for m in range(count):
        place = index_ref[m]
        dx_ref[place] = dot_nn(dy_ref[...], weights[m][...])
        for start in range(0, columns, 256):
            size = min(256, columns - start)
            dw_ref[m, start : start + size, :] = dot_tn(
                dy_ref[:, start : start + size], x_ref[place]
            ).astype(BF)


def project_back(dy, x_blocks, index, weights):
    count = len(weights)
    rows, depth = x_blocks.shape[1:]
    columns = weights[0].shape[0]
    return pl.pallas_call(
        functools.partial(projection_back_kernel, count, columns),
        out_shape=(
            jax.ShapeDtypeStruct((count, rows, depth), F32),
            jax.ShapeDtypeStruct((count, columns, depth), BF),
        ),
        in_specs=[smem_spec()] + [vmem_spec()] * (2 + count),
        out_specs=(vmem_spec(), vmem_spec()),
        compiler_params=params(),
        cost_estimate=cost(4 * rows * columns * depth * count, 4 * columns * depth * count + 4 * rows * columns),
    )(index, dy, x_blocks, *weights)


def ffn_kernel(nd, nz, dp_ref, z_ref, n2_ref, dy_ref, *rest):
    gu = rest[:nd]
    down = rest[nd : nd + nz]
    out_ref, dn_ref, dgu_ref, dd_ref = rest[nd + nz :]

    @pl.when(pl.program_id(0) == 0)
    def _():
        out_ref[...] = jnp.zeros_like(out_ref)
        dn_ref[...] = jnp.zeros_like(dn_ref)

    gate = up = grad_hidden = None
    for m in range(nd):
        rows = n2_ref[dp_ref[m]]
        term_g = dot_nt(rows, gu[m][0])
        term_u = dot_nt(rows, gu[m][1])
        gate = term_g if gate is None else gate + term_g
        up = term_u if up is None else up + term_u
    for s in range(nz):
        term = dot_nt(dy_ref[z_ref[s]], down[s][...])
        grad_hidden = term if grad_hidden is None else grad_hidden + term
    sig = jax.nn.sigmoid(gate)
    act = gate * sig
    hidden = (act * up).astype(BF)
    d_gate = (grad_hidden * up * sig * (1.0 + gate * (1.0 - sig))).astype(BF)
    d_up = (grad_hidden * act).astype(BF)
    for s in range(nz):
        place = z_ref[s]
        out_ref[place] += dot_nn(hidden, down[s][...])
        dd_ref[s] = dot_tn(hidden, dy_ref[place]).astype(BF)
    for m in range(nd):
        place = dp_ref[m]
        rows = n2_ref[place]
        dn_ref[place] += dot_nn(d_gate, gu[m][0]) + dot_nn(d_up, gu[m][1])
        dgu_ref[m, 0] = dot_tn(d_gate, rows).astype(BF)
        dgu_ref[m, 1] = dot_tn(d_up, rows).astype(BF)


def feed_forward(n2_blocks, dy_blocks, dp_index, z_index, gu, down):
    nd, nz = len(gu), len(down)
    rows = n2_blocks.shape[1]
    units = gu[0].shape[1]
    chunk = 256
    dl, zl = n2_blocks.shape[2], dy_blocks.shape[2]
    flops = 2 * rows * units * (nd * dl) * 9
    return pl.pallas_call(
        functools.partial(ffn_kernel, nd, nz),
        grid=(units // chunk,),
        out_shape=(
            jax.ShapeDtypeStruct((nz, rows, zl), F32),
            jax.ShapeDtypeStruct((nd, rows, dl), F32),
            jax.ShapeDtypeStruct((nd, 2, units, dl), BF),
            jax.ShapeDtypeStruct((nz, units, zl), BF),
        ),
        in_specs=[smem_spec(), smem_spec()]
        + [
            pl.BlockSpec(n2_blocks.shape, lambda i: (0, 0, 0)),
            pl.BlockSpec(dy_blocks.shape, lambda i: (0, 0, 0)),
        ]
        + [pl.BlockSpec((2, chunk, dl), lambda i: (0, i, 0))] * nd
        + [pl.BlockSpec((chunk, zl), lambda i: (i, 0))] * nz,
        out_specs=(
            pl.BlockSpec((nz, rows, zl), lambda i: (0, 0, 0)),
            pl.BlockSpec((nd, rows, dl), lambda i: (0, 0, 0)),
            pl.BlockSpec((nd, 2, chunk, dl), lambda i: (0, 0, i, 0)),
            pl.BlockSpec((nz, chunk, zl), lambda i: (0, i, 0)),
        ),
        compiler_params=params(),
        cost_estimate=cost(flops, 12 * units * nd * dl, rows * units),
    )(dp_index, z_index, n2_blocks, dy_blocks, *gu, *down)


def group_rows(ref, g):
    return jnp.concatenate(
        [ref[:, (g * GROUP + i) * HEAD_SIZE : (g * GROUP + i + 1) * HEAD_SIZE] for i in range(GROUP)],
        axis=0,
    )


def bias_of(start_ref, first_query, first_key, span, size):
    key = first_key + lax.broadcasted_iota(jnp.int32, (span, size), 1)
    query = first_query + lax.broadcasted_iota(jnp.int32, (span, size), 0)
    allowed = (key <= query) & (key >= start_ref[...])
    return jnp.where(allowed, 0.0, masked_score)


def attend_kernel(span, size, info_ref, start_ref, q_ref, kv_ref, att_ref, lse_ref, acc, top, total):
    first_query = info_ref[0]
    top[...] = jnp.full_like(top, lowest_top)
    total[...] = jnp.zeros_like(total)
    acc[...] = jnp.zeros_like(acc)
    value_at = KEY_VALUE_HEADS * HEAD_SIZE

    def one_block(block, carry):
        first_key = pl.multiple_of(block * size, size)
        bias = bias_of(start_ref, first_query, first_key, span, size)
        bias = jnp.concatenate([bias] * GROUP, axis=0)
        for g in range(KEY_VALUE_HEADS):
            rows = group_rows(q_ref, g) * BF(score_scale)
            keys = kv_ref[pl.ds(first_key, size), g * HEAD_SIZE : (g + 1) * HEAD_SIZE]
            values = kv_ref[
                pl.ds(first_key, size), value_at + g * HEAD_SIZE : value_at + (g + 1) * HEAD_SIZE
            ]
            scores = dot_nt(rows, keys) + bias
            old_top = top[g]
            new_top = jnp.maximum(old_top, jnp.max(scores, axis=1, keepdims=True))
            rescale = jnp.exp(old_top - new_top)
            expo = jnp.exp(scores - new_top)
            total[g] = total[g] * rescale + jnp.sum(expo, axis=1, keepdims=True)
            acc[g] = acc[g] * rescale + dot_nn(expo.astype(BF), values)
            top[g] = new_top
        return carry

    lax.fori_loop(info_ref[1], info_ref[2], one_block, 0)
    lane = lax.broadcasted_iota(jnp.int32, lse_ref.shape, 1)
    lse = jnp.zeros(lse_ref.shape, F32)
    for g in range(KEY_VALUE_HEADS):
        whole = total[g]
        result = (acc[g] * (1.0 / whole)).astype(BF)
        log_total = top[g] + jnp.log(whole)
        for i in range(GROUP):
            h = g * GROUP + i
            att_ref[:, h * HEAD_SIZE : (h + 1) * HEAD_SIZE] = result[i * span : (i + 1) * span]
            lse = jnp.where(lane == h, log_total[i * span : (i + 1) * span], lse)
    lse_ref[...] = lse


def attend(info, start, q, kv, size):
    span = q.shape[0]
    rows = GROUP * span
    length = kv.shape[0]
    return pl.pallas_call(
        functools.partial(attend_kernel, span, size),
        out_shape=(
            jax.ShapeDtypeStruct((span, QUERY_HEADS * HEAD_SIZE), BF),
            jax.ShapeDtypeStruct((span, 128), F32),
        ),
        in_specs=[smem_spec()] + [vmem_spec()] * 3,
        out_specs=(vmem_spec(), vmem_spec()),
        scratch_shapes=[
            pltpu.VMEM((KEY_VALUE_HEADS, rows, HEAD_SIZE), F32),
            pltpu.VMEM((KEY_VALUE_HEADS, rows, 1), F32),
            pltpu.VMEM((KEY_VALUE_HEADS, rows, 1), F32),
        ],
        compiler_params=params(),
        cost_estimate=cost(
            16 * QUERY_HEADS * HEAD_SIZE * span * length,
            4 * length * KEY_VALUE_HEADS * HEAD_SIZE,
            QUERY_HEADS * span * length,
        ),
    )(info, start, q, kv)


def attend_back_kernel(
    span, size, info_ref, start_ref, q_ref, kv_ref, att_ref, datt_ref, lse_ref, cos_ref, sin_ref,
    dq_ref, dkv_ref, dq_acc, q_rows, d_rows, lse_rows, dot_rows,
):
    first_query = info_ref[0]
    value_at = KEY_VALUE_HEADS * HEAD_SIZE
    dq_acc[...] = jnp.zeros_like(dq_acc)
    dkv_ref[...] = jnp.zeros_like(dkv_ref)
    for g in range(KEY_VALUE_HEADS):
        grads = group_rows(datt_ref, g)
        q_rows[g] = group_rows(q_ref, g) * BF(score_scale)
        d_rows[g] = grads
        dot_rows[g] = jnp.sum(
            grads.astype(F32) * group_rows(att_ref, g).astype(F32), axis=1, keepdims=True
        )
        lse_rows[g] = jnp.concatenate(
            [lse_ref[:, g * GROUP + i : g * GROUP + i + 1] for i in range(GROUP)], axis=0
        )

    def one_block(block, carry):
        first_key = pl.multiple_of(block * size, size)
        bias = bias_of(start_ref, first_query, first_key, span, size)
        bias = jnp.concatenate([bias] * GROUP, axis=0)
        for g in range(KEY_VALUE_HEADS):
            k_at, v_at = g * HEAD_SIZE, value_at + g * HEAD_SIZE
            rows = q_rows[g]
            grads = d_rows[g]
            keys = kv_ref[pl.ds(first_key, size), k_at : k_at + HEAD_SIZE]
            values = kv_ref[pl.ds(first_key, size), v_at : v_at + HEAD_SIZE]
            probs = jnp.exp((dot_nt(rows, keys) + bias) - lse_rows[g])
            d_probs = dot_nt(grads, values)
            d_scores = (probs * (d_probs - dot_rows[g])).astype(BF)
            dkv_ref[pl.ds(first_key, size), v_at : v_at + HEAD_SIZE] = dot_tn(
                probs.astype(BF), grads
            ).astype(BF)
            dkv_ref[pl.ds(first_key, size), k_at : k_at + HEAD_SIZE] = dot_tn(d_scores, rows).astype(BF)
            dq_acc[g] += dot_nn(d_scores, keys)
        return carry

    lax.fori_loop(info_ref[1], info_ref[2], one_block, 0)
    cosine, sine = cos_ref[...], -sin_ref[...]
    for start in range(0, QUERY_HEADS + 1, 2):
        parts = []
        for h in (start, start + 1):
            if h < QUERY_HEADS:
                g, i = h // GROUP, h % GROUP
                parts.append(dq_acc[g, i * span : (i + 1) * span] * score_scale)
            else:
                parts.append(jnp.zeros((span, HEAD_SIZE), F32))
        pair = jnp.concatenate(parts, axis=1)
        dq_ref[:, start * HEAD_SIZE : (start + 2) * HEAD_SIZE] = rotate(pair, cosine, sine).astype(BF)


def attend_back(info, start, q, kv, att, datt, lse, cosine, sine, size):
    span = q.shape[0]
    rows = GROUP * span
    length = kv.shape[0]
    per_head = (KEY_VALUE_HEADS, rows, HEAD_SIZE)
    per_row = (KEY_VALUE_HEADS, rows, 1)
    return pl.pallas_call(
        functools.partial(attend_back_kernel, span, size),
        out_shape=(
            jax.ShapeDtypeStruct((span, q.shape[1]), BF),
            jax.ShapeDtypeStruct(kv.shape, BF),
        ),
        in_specs=[smem_spec()] + [vmem_spec()] * 8,
        out_specs=(vmem_spec(), vmem_spec()),
        scratch_shapes=[
            pltpu.VMEM(per_head, F32),
            pltpu.VMEM(per_head, BF),
            pltpu.VMEM(per_head, BF),
            pltpu.VMEM(per_row, F32),
            pltpu.VMEM(per_row, F32),
        ],
        compiler_params=params(),
        cost_estimate=cost(
            40 * QUERY_HEADS * HEAD_SIZE * span * length,
            8 * length * KEY_VALUE_HEADS * HEAD_SIZE,
            QUERY_HEADS * span * length,
        ),
    )(info, start, q, kv, att, datt, lse, cosine, sine)


def norm_scale(value):
    return lax.rsqrt(jnp.mean(value * value, axis=-1, keepdims=True) + epsilon)


def to_blocks(value, count):
    rows, width = value.shape
    return value.reshape(rows, count, width // count).transpose(1, 0, 2)


def from_blocks(value):
    count, rows, width = value.shape
    return value.transpose(1, 0, 2).reshape(rows, count * width)


def on_device(
    hidden_in,
    positions,
    attn_gain,
    w_query,
    key_projection_weight,
    w_value,
    w_out,
    ffn_gain,
    w_gate,
    w_up,
    w_down,
    out_grad,
):
    nd, nc = lax.axis_size("dp"), lax.axis_size("ctx")
    nz = nc // 2
    seqs, span, width = hidden_in.shape
    rows = seqs * span
    length = span * nc
    d, rank = lax.axis_index("dp"), lax.axis_index("ctx")
    z, c = rank // 2, rank % 2
    first = c == 0
    block_size = min(512, length)

    def send(value, to):
        pairs = []
        for di in range(nd):
            for zi in range(nz):
                for ci in range(2):
                    target = to(di, zi, ci)
                    if target is not None:
                        dt, zt, ct = target
                        pairs.append((di * nc + zi * 2 + ci, dt * nc + zt * 2 + ct))
        return lax.ppermute(value, ("dp", "ctx"), pairs)

    def z_shift(value, s):
        return send(value, lambda di, zi, ci: (di, (zi + s) % nz, ci))

    def z_up(value):
        return send(value, lambda di, zi, ci: (di, zi + 1, ci) if zi + 1 < nz else None)

    def z_down(value, s):
        return send(value, lambda di, zi, ci: (di, zi - s, ci) if zi >= s else None)

    def dp_xor(value, m):
        return send(value, lambda di, zi, ci: (di ^ m, zi, ci))

    def core_swap(value):
        return send(value, lambda di, zi, ci: (di, zi, 1 - ci))

    def put(buffer, piece, axis, place):
        return lax.dynamic_update_slice_in_dim(buffer, piece, place, axis)

    def take(value, axis, place):
        return lax.dynamic_index_in_dim(value, place, axis, keepdims=False)

    def gather_z(value, axis):
        shape = list(value.shape)
        shape[axis] = nz
        buffer = put(jnp.zeros(shape, value.dtype), value, axis, z)
        for s in range(1, nz):
            buffer = put(buffer, z_shift(value, s), axis, (z - s) % nz)
        return buffer

    def in_core_order(own, other, axis):
        return jnp.stack([jnp.where(first, own, other), jnp.where(first, other, own)], axis=axis)

    dp_index = jnp.bitwise_xor(d, jnp.arange(nd, dtype=jnp.int32))
    z_index = (z - jnp.arange(nz, dtype=jnp.int32)) % nz

    gains = jnp.stack([attn_gain, ffn_gain]).reshape(2, 1, -1)
    gains = gather_z(gains, 1)
    gains = in_core_order(gains, core_swap(gains), 2).reshape(2, width).astype(F32)
    gain_attn, gain_ffn = gains[0], gains[1]

    def gather_pair(left, right):
        value = jnp.stack([left.T, right.T])[:, None]
        own = gather_z(value, 1)
        own = [own] + [dp_xor(own, m) for m in range(1, nd)]
        whole = []
        for piece in own:
            both = in_core_order(piece, core_swap(piece), 2)
            whole.append(both.reshape(2, -1, piece.shape[-1]))
        return whole

    kv_weights = [w.reshape(-1, w.shape[-1]) for w in gather_pair(key_projection_weight, w_value)]
    qo_weights = gather_pair(w_query, w_out)
    padding = -(QUERY_HEADS * HEAD_SIZE) % 128
    q_weights = [jnp.pad(w[0], ((0, padding), (0, 0))) for w in qo_weights]
    o_weights = [w[1] for w in qo_weights]

    gu_local = jnp.stack([w_gate.T, w_up.T])[:, None]
    gu_own = gather_z(gu_local, 1)
    gu_own = gu_own.reshape(2, -1, gu_own.shape[-1])
    gu_own = [gu_own] + [dp_xor(gu_own, m) for m in range(1, nd)]
    gu_other = [core_swap(piece) for piece in gu_own]

    units = w_gate.shape[1]
    down_cut = w_down.reshape(-1, 2, units, w_down.shape[1])
    down_mine = take(down_cut, 1, c).reshape(-1, w_down.shape[1])
    down_from = core_swap(take(down_cut, 1, 1 - c).reshape(-1, w_down.shape[1]))
    down_local = in_core_order(down_mine, down_from, 1).reshape(down_mine.shape[0], -1)
    down_own = put(jnp.zeros((nd,) + down_local.shape, BF), down_local[None], 0, d)
    for m in range(1, nd):
        down_own = put(down_own, dp_xor(down_local, m)[None], 0, d ^ m)
    down_own = down_own.reshape(-1, down_local.shape[1])
    down_own = [down_own] + [z_shift(down_own, s) for s in range(1, nz)]
    down_other = [core_swap(piece) for piece in down_own]

    lane = np.arange(128)
    frequency = jnp.power(theta_base, -jnp.asarray(lane % HALF, F32) * 2.0 / HEAD_SIZE)
    angle = positions.reshape(rows, 1).astype(F32) * frequency[None, :]
    cosine = jnp.cos(angle)
    sine = jnp.sin(angle) * jnp.asarray(np.where(lane % HEAD_SIZE < HALF, -1.0, 1.0), F32)[None, :]

    inputs = hidden_in.reshape(rows, width).astype(F32)
    scale_one = norm_scale(inputs)
    normed_one = (inputs * scale_one * gain_attn).astype(BF)
    one_blocks = to_blocks(normed_one, nd)
    kw = KEY_VALUE_HEADS * HEAD_SIZE
    kv_own = project(one_blocks, dp_index, kv_weights, BF, (cosine, sine), kw)
    query = project(one_blocks, dp_index, q_weights, BF, (cosine, sine), QUERY_HEADS * HEAD_SIZE)

    first_query = rank * span
    att_list, lse_list, kv_list, info_list, start_list = [], [], [], [], []
    for i in range(seqs):
        own = kv_own[i * span : (i + 1) * span][None, None]
        buffer = jnp.zeros((nz, 2, span, 2 * kw), BF)
        piece = own
        for s in range(nz):
            if s:
                piece = z_up(piece)
            place = (z - s) % nz
            buffer = lax.dynamic_update_slice(buffer, piece, (place, c, 0, 0))
            buffer = lax.dynamic_update_slice(buffer, core_swap(piece), (place, 1 - c, 0, 0))
        kv = buffer.reshape(length, 2 * kw)
        begin = (first_query + jnp.arange(span, dtype=jnp.int32) - positions[i]).reshape(span, 1)
        info = jnp.stack(
            [first_query, begin[0, 0] // block_size, (first_query + span - 1) // block_size + 1]
        ).astype(jnp.int32)
        att, lse = attend(info, begin, query[i * span : (i + 1) * span], kv, block_size)
        att_list.append(att)
        lse_list.append(lse)
        kv_list.append(kv)
        info_list.append(info)
        start_list.append(begin)
    attended = jnp.concatenate(att_list, axis=0)
    att_blocks = to_blocks(attended, nd)
    mid = inputs + project(att_blocks, dp_index, o_weights, F32)

    scale_two = norm_scale(mid)
    normed_two = (mid * scale_two * gain_ffn).astype(BF)
    two_blocks = to_blocks(normed_two, nd)
    top_grad = out_grad.reshape(rows, width)
    top_blocks = to_blocks(top_grad, nz)
    out_other, dn_other, dgu_other, dd_other = feed_forward(
        two_blocks, top_blocks, dp_index, z_index, gu_other, down_other
    )
    out_own, dn_own, dgu_own, dd_own = feed_forward(
        two_blocks, top_blocks, dp_index, z_index, gu_own, down_own
    )
    layer_out = (mid + from_blocks(out_other + out_own)).astype(BF)
    grad_two = from_blocks(dn_other + dn_own)

    def add(*values):
        total = values[0].astype(F32)
        for value in values[1:]:
            total = total + value.astype(F32)
        return total

    def over_dp(value):
        return add(value[0], *[dp_xor(value[m], m) for m in range(1, nd)])

    def over_z(value, axis):
        return add(take(value, axis, z), *[z_shift(take(value, axis, (z + s) % nz), s) for s in range(1, nz)])

    dgu = add(dgu_own, core_swap(dgu_other)).astype(BF)
    dgu = over_dp(dgu).astype(BF)
    dgu = over_z(dgu.reshape(2, nz, -1, dgu.shape[-1]), 1)
    w_gate_grad, w_up_grad = dgu[0].T, dgu[1].T

    dd = add(dd_own, core_swap(dd_other)).astype(BF)
    dd = add(dd[0], *[z_shift(dd[s], -s) for s in range(1, nz)]).astype(BF)
    dd = dd.reshape(nd, -1, dd.shape[-1])
    dd = add(take(dd, 0, d), *[dp_xor(take(dd, 0, d ^ m), m) for m in range(1, nd)])
    dd = dd.reshape(dd.shape[0], 2, -1)
    dd_from = core_swap(take(dd, 1, 1 - c))
    dd = in_core_order(
        take(dd, 1, c).reshape(-1, units, dd.shape[-1]), dd_from.reshape(-1, units, dd.shape[-1]), 1
    )
    w_down_grad = dd.reshape(w_down.shape)

    weighted_two = grad_two * gain_ffn
    ffn_sum = jnp.sum(grad_two * mid * scale_two, axis=0)
    grad_mid = (
        top_grad.astype(F32)
        + scale_two * weighted_two
        - mid * (scale_two * scale_two * scale_two) * jnp.mean(weighted_two * mid, axis=-1, keepdims=True)
    )
    grad_att, do = project_back(grad_mid.astype(BF), att_blocks, dp_index, o_weights)
    grad_att = from_blocks(grad_att).astype(BF)

    def rows_of(value, parts):
        cut = value.reshape(nd, parts, nz, 2, -1, value.shape[-1])

        def half(which):
            return take(cut, 3, which).transpose(0, 2, 1, 3, 4).reshape(nd, nz, -1, value.shape[-1])

        return half(c), half(1 - c)

    do_mine, do_other = rows_of(do, 1)
    do = over_dp(add(do_mine, core_swap(do_other)).astype(BF)).astype(BF)
    w_out_grad = over_z(do, 0).T

    dq_list, dkv_list = [], []
    for i in range(seqs):
        here = slice(i * span, (i + 1) * span)
        dq, dkv = attend_back(
            info_list[i], start_list[i], query[here], kv_list[i], att_list[i], grad_att[here], lse_list[i],
            cosine[here], sine[here], block_size,
        )
        cut = dkv.reshape(nz, 2, span, 2 * kw)
        mine = add(take(cut, 1, c), core_swap(take(cut, 1, 1 - c))).astype(BF)
        total = take(mine, 0, z).astype(F32)
        for s in range(1, nz):
            total = total + z_down(take(mine, 0, (z - s) % nz), s).astype(F32)
        dq_list.append(dq)
        dkv_list.append(total)
    dq = jnp.concatenate(dq_list, axis=0)
    dkv = jnp.concatenate(dkv_list, axis=0)
    dk, dv = dkv[:, :kw], dkv[:, kw:]
    lane = np.arange(kw)
    swapped = jnp.where(lane % HEAD_SIZE < HALF, jnp.roll(dk, -HALF, 1), jnp.roll(dk, HALF, 1))
    cos_wide = jnp.tile(cosine[:, :HEAD_SIZE], (1, KEY_VALUE_HEADS))
    sin_wide = jnp.tile(sine[:, :HEAD_SIZE], (1, KEY_VALUE_HEADS))
    dkv = jnp.concatenate([dk * cos_wide - swapped * sin_wide, dv], axis=1).astype(BF)

    dq_one, dq_w = project_back(dq, one_blocks, dp_index, q_weights)
    dkv_one, dkv_w = project_back(dkv, one_blocks, dp_index, kv_weights)
    q_mine, q_other = rows_of(dq_w[:, : QUERY_HEADS * HEAD_SIZE], 1)
    kv_mine, kv_other = rows_of(dkv_w, 2)
    q_rows = q_mine.shape[2]
    dw = add(
        jnp.concatenate([q_mine, kv_mine], axis=2),
        core_swap(jnp.concatenate([q_other, kv_other], axis=2)),
    ).astype(BF)
    dw = over_z(over_dp(dw).astype(BF), 0)
    k_rows = (dw.shape[0] - q_rows) // 2
    w_query_grad = dw[:q_rows].T
    w_key_grad = dw[q_rows : q_rows + k_rows].T
    w_value_grad = dw[q_rows + k_rows :].T

    grad_one = from_blocks(dq_one + dkv_one)
    weighted_one = grad_one * gain_attn
    attn_sum = jnp.sum(grad_one * inputs * scale_one, axis=0)
    grad_input = (
        grad_mid
        + scale_one * weighted_one
        - inputs * (scale_one * scale_one * scale_one) * jnp.mean(weighted_one * inputs, axis=-1, keepdims=True)
    )
    gain_sums = lax.psum(jnp.stack([attn_sum, ffn_sum]), ("dp", "ctx"))
    gain_own = lax.dynamic_slice_in_dim(gain_sums, rank * (width // nc), width // nc, 1)
    return (
        layer_out.reshape(seqs, span, width),
        grad_input.astype(BF).reshape(seqs, span, width),
        gain_own[0],
        w_query_grad,
        w_key_grad,
        w_value_grad,
        w_out_grad,
        gain_own[1],
        w_gate_grad,
        w_up_grad,
        w_down_grad,
    )


def solution(mesh):
    placed = (
        P("dp", "ctx", None),
        P("dp", "ctx"),
        P("ctx"),
        P("dp", "ctx"),
        P("dp", "ctx"),
        P("dp", "ctx"),
        P("dp", "ctx"),
        P("ctx"),
        P("dp", "ctx"),
        P("dp", "ctx"),
        P("dp", "ctx"),
        P("dp", "ctx", None),
    )
    return jax.shard_map(
        on_device,
        mesh=mesh,
        in_specs=placed,
        out_specs=(
            P("dp", "ctx", None),
            P("dp", "ctx", None),
            P("ctx"),
            P("dp", "ctx"),
            P("dp", "ctx"),
            P("dp", "ctx"),
            P("dp", "ctx"),
            P("ctx"),
            P("dp", "ctx"),
            P("dp", "ctx"),
            P("dp", "ctx"),
        ),
        check_vma=False,
    )
```

time: 1060 us -> 879 us (0.83)
  waiting for transfers between devices: 562 us -> 208 us
  starting transfers between devices: 1.22 us -> 192 us
  matrix products: 159 us -> 0 us
  Pallas kernels: 0 us -> 117 us
  local copies, waits for them, and re-layouts: 118 us -> 213 us
  blocking collectives: 153 us -> 65.2 us
  other arithmetic: 36.3 us -> 73.4 us
    reduce_scatter x7 -> x0, waiting for transfers between devices: 288 us -> none  [the longest x2 73.1 us: on_device(): lax.psum_scatter(key_terms(jnp.int32(0), span_length * lax.axis_size('ctx...]
    ppermute x0 -> x96, waiting for transfers between devices: none -> 208 us  [send(): return lax.ppermute(value, ('dp', 'ctx'), pairs)]
    ppermute x0 -> x96, starting transfers between devices: none -> 192 us  [send(): return lax.ppermute(value, ('dp', 'ctx'), pairs)]
    unnamed x26 -> x0, waiting for transfers between devices: 169 us -> none
    dot_general x35 -> x0, matrix products: 159 us -> none  [the longest x7 34.8 us: matmul_back(): jnp.einsum('tf,df->td', left_rows, weight_full, preferred_element_type=jn...]
    pallas_call x0 -> x12, Pallas kernels: none -> 117 us  [the longest x2 36.2 us: feed_forward(): pl.pallas_call(functools.partial(ffn_kernel, nd, nz), grid=(units // chun...]
    all_gather x10 -> x0, blocking collectives: 113 us -> none  [the longest x1 17.5 us: fetch_weights(): lax.all_gather(tall[2], 'ctx', axis=1, tiled=True)]
    all_gather x7 -> x0, waiting for transfers between devices: 105 us -> none  [the longest x1 49.2 us: fetch_weights(): lax.all_gather(tall[5], 'ctx', axis=1, tiled=True)]
  transfers between devices with their start and end apart: 20 -> 96, of which waited for: 15 -> 20; matrix products, arithmetic and copies ran while one was open for 19% -> 27% of each run, Pallas kernels for 0% -> 11%
where the time goes in v1:
time: 879 us; the launch traced here: 876 us
  local copies, waits for them, and re-layouts  213 us (24%)
  waiting for transfers between devices  208 us (24%)
  starting transfers between devices  192 us (22%)
  Pallas kernels  117 us (13%)
  other arithmetic  73.4 us (8%)
  blocking collectives  65.2 us (7%)
    ppermute x96, waiting for transfers between devices, send(): return lax.ppermute(value, ('dp', 'ctx'), pairs)  208 us
    ppermute x96, starting transfers between devices, send(): return lax.ppermute(value, ('dp', 'ctx'), pairs)  192 us
    psum x1, blocking collectives, on_device(): gain_sums = lax.psum(jnp.stack([attn_sum, ffn_sum]), ('dp', 'ctx'))  65.2 us
    ppermute x28, local copies, waits for them, and re-layouts, send(): return lax.ppermute(value, ('dp', 'ctx'), pairs)  55 us
    pallas_call x2, Pallas kernels, feed_forward(): pl.pallas_call(functools.partial(ffn_kernel, nd, nz), grid=(units // chun...  36.2 us
    pallas_call x2, Pallas kernels, attend_back(): pl.pallas_call(functools.partial(attend_back_kernel, span, size), out_sha...  26.1 us
    pallas_call x2, Pallas kernels, attend(): pl.pallas_call(functools.partial(attend_kernel, span, size), out_shape=(j...  23.7 us
    pallas_call x3, Pallas kernels, project_back(): pl.pallas_call(functools.partial(projection_back_kernel, count, columns),...  18 us
  transfers between devices with their start and end apart: 96, of which 20 were waited for; matrix products, arithmetic and copies ran while one was open for 27% of the time, Pallas kernels for 11%

profile of v1, /device:TPU:0, one launch (start us, length us, event | category | flops | bytes accessed | tf_op | source)
XLA Modules:
  0.0 875.8 jit_solution(2820710430337790673)
XLA Ops:
  93.1 5.5 collective-permute-done.49
  118.9 11.3 %collective-permute-done.20 = bf16[2,4,40,240]{3,2,1,0:T(8,128)(2,1)S(1)} collective-permute-done((bf16[2,4,40,240]{3,2,1,0:T(8,128)(2,1)}, bf16[2,4,40,240]{3,2,1,0:T(8,128)(2,1)S(1)}, u32[]{:S(2)}, u32[]{:S(2)}) %collective-permute-start.20) | collective-permute-done | bytes 153632 | tf_op jit(solution)/shard_map/ppermute | solution.py:419
  151.6 5.2 collective-permute-start.32
  158.7 38.7 %collective-permute-done.32 = bf16[1,1,256,640]{3,2,1,0:T(8,128)(2,1)} collective-permute-done((bf16[1,1,256,640]{3,2,1,0:T(8,128)(2,1)S(1)}, bf16[1,1,256,640]{3,2,1,0:T(8,128)(2,1)}, u32[]{:S(2)}, u32[]{:S(2)}) %collective-permute-start.32) | collective-permute-done | bytes 327712 | tf_op jit(solution)/shard_map/ppermute | solution.py:419
  200.0 17.7 %collective-permute-start.27 = (bf16[1,1,256,640]{3,2,1,0:T(8,128)(2,1)S(1)}, bf16[1,1,256,640]{3,2,1,0:T(8,128)(2,1)}, u32[]{:S(2)}, u32[]{:S(2)}) collective-permute-start(bf16[1,1,256,640]{3,2,1,0:T(8,128)(2,1)S(1)} %collective-permute-done.25), channel_id=1, source_target_pairs={{0,2},{1,3},{2,4},{3,5},{4,6},{5,7},{8,10},{9,11},{10,12},{11,13},... | collective-permute-start | bytes 983048 | tf_op jit(solution)/shard_map/ppermute | solution.py:419
  240.0 5.2 collective-permute-start.29
  247.6 4.7 collective-permute-done.29
  252.3 5.5 collective-permute-start.36
  269.3 4.7 shard_map.230
  288.4 27.5 %collective-permute-done.44 = bf16[2,1280,240]{1,2,0:T(8,128)(2,1)} collective-permute-done((bf16[2,1280,240]{1,2,0:T(8,128)(2,1)}, bf16[2,1280,240]{1,2,0:T(8,128)(2,1)}, u32[]{:S(2)}, u32[]{:S(2)}) %collective-permute-start.44) | collective-permute-done | bytes 1228832 | tf_op jit(solution)/shard_map/ppermute | solution.py:419
  325.5 12.3 %shard_map.232 = (bf16[256,960]{1,0:T(8,128)(2,1)}, f32[256,128]{1,0:T(8,128)}) custom-call(s32[3]{0:T(128)} %add_add_fusion.info_ref, s32[256,1]{1,0:T(8,128)} %fusion.47.start_ref, bf16[256,1024]{1,0:T(8,128)(2,1)} %get-tuple-element.139.q_ref, bf16[2048,640]{1,0:T(8,128)(2,1)} %bitcast.390), custom_call_target="tpu_custom_call" | custom-call | flops 8053063680 | bytes 2621440 | tf_op jit(solution)/shard_map/pallas_call | solution.py:267
  337.8 11.4 %shard_map.233 = (bf16[256,960]{1,0:T(8,128)(2,1)}, f32[256,128]{1,0:T(8,128)}) custom-call(s32[3]{0:T(128)} %add_add_fusion.1.info_ref, s32[256,1]{1,0:T(8,128)} %fusion.46.start_ref, bf16[256,1024]{1,0:T(8,128)(2,1)} %get-tuple-element.140.q_ref, bf16[2048,640]{1,0:T(8,128)(2,1)} %bitcast.388), custom_call_target="tpu_custom_call" | custom-call | flops 8053063680 | bytes 2621440 | tf_op jit(solution)/shard_map/pallas_call | solution.py:267
  362.4 18.0 %shard_map.236 = (f32[4,512,240]{2,1,0:T(8,128)}, f32[4,512,240]{2,1,0:T(8,128)}, bf16[4,2,1280,240]{3,2,1,0:T(8,128)(2,1)}, bf16[4,1280,240]{2,1,0:T(8,128)(2,1)}) custom-call(s32[4]{0:T(128)} %iota_xor_fusion.index_ref.dp_ref, s32[4]{0:T(128)} %and_select_fusion.z_ref, bf16[4,512,240]{2,1,0:T(8,128)(2,1)} %bitcast.426, bf16[4,512,240]{2,1,0:T(8,128)(2,1)} %bitcast.424, ...), custom_call_target="tpu_custom_call" | custom-call | flops 11324620800 | bytes 14745600 | tf_op jit(solution)/shard_map/pallas_call | solution.py:181
  387.8 18.2 %shard_map.235 = (f32[4,512,240]{2,1,0:T(8,128)}, f32[4,512,240]{2,1,0:T(8,128)}, bf16[4,2,1280,240]{3,2,1,0:T(8,128)(2,1)}, bf16[4,1280,240]{2,1,0:T(8,128)(2,1)}) custom-call(s32[4]{0:T(128)} %iota_xor_fusion.index_ref.dp_ref, s32[4]{0:T(128)} %and_select_fusion.z_ref, bf16[4,512,240]{2,1,0:T(8,128)(2,1)} %bitcast.427, bf16[4,512,240]{2,1,0:T(8,128)(2,1)} %bitcast.425, ...), custom_call_target="tpu_custom_call" | custom-call | flops 11324620800 | bytes 14745600 | tf_op jit(solution)/shard_map/pallas_call | solution.py:181
  431.8 6.4 shard_map.237
  446.4 13.2 %shard_map.238 = (bf16[256,1024]{1,0:T(8,128)(2,1)}, bf16[2048,640]{1,0:T(8,128)(2,1)}) custom-call(s32[3]{0:T(128)} %add_add_fusion.info_ref, s32[256,1]{1,0:T(8,128)} %fusion.47.start_ref, bf16[256,1024]{1,0:T(8,128)(2,1)} %get-tuple-element.139.q_ref, bf16[2048,640]{1,0:T(8,128)(2,1)} %bitcast.391, bf16[256,960]{1,0:T(8,128)(2,1)} %get-tuple-element.33.att_ref, ...), custom_call_target="tpu_custom_call" | custom-call | flops 20132659200 | bytes 5242880 | tf_op jit(solution)/shard_map/pallas_call | solution.py:348
  463.3 12.9 %shard_map.239 = (bf16[256,1024]{1,0:T(8,128)(2,1)}, bf16[2048,640]{1,0:T(8,128)(2,1)}) custom-call(s32[3]{0:T(128)} %add_add_fusion.1.info_ref, s32[256,1]{1,0:T(8,128)} %fusion.46.start_ref, bf16[256,1024]{1,0:T(8,128)(2,1)} %get-tuple-element.140.q_ref, bf16[2048,640]{1,0:T(8,128)(2,1)} %bitcast.389, bf16[256,960]{1,0:T(8,128)(2,1)} %get-tuple-element.34.att_ref, ...), custom_call_target="tpu_custom_call" | custom-call | flops 20132659200 | bytes 5242880 | tf_op jit(solution)/shard_map/pallas_call | solution.py:348
  487.8 6.4 shard_map.240
  498.6 7.7 copy.309
  511.8 24.7 %collective-permute-start.78 = (bf16[120,240]{0,1:T(8,128)(2,1)S(1)}, bf16[120,240]{0,1:T(8,128)(2,1)S(1)}, u32[]{:S(2)}, u32[]{:S(2)}) collective-permute-start(bf16[120,240]{0,1:T(8,128)(2,1)S(1)} %get-tuple-element.186), channel_id=1, source_target_pairs={{0,2},{1,3},{2,4},{3,5},{4,6},{5,7},{6,0},{7,1},{8,10},{9,11},{10,... | collective-permute-start | bytes 172808 | tf_op jit(solution)/shard_map/ppermute | solution.py:419
  536.5 49.9 %collective-permute-start.79 = (bf16[120,240]{0,1:T(8,128)(2,1)S(1)}, bf16[120,240]{0,1:T(8,128)(2,1)S(1)}, u32[]{:S(2)}, u32[]{:S(2)}) collective-permute-start(bf16[120,240]{0,1:T(8,128)(2,1)S(1)} %get-tuple-element.188), channel_id=1, source_target_pairs={{0,4},{1,5},{2,6},{3,7},{4,0},{5,1},{6,2},{7,3},{8,12},{9,13},{10,... | collective-permute-start | bytes 172808 | tf_op jit(solution)/shard_map/ppermute | solution.py:419
  600.5 33.5 %collective-permute-done.61 = bf16[256,640]{1,0:T(8,128)(2,1)S(1)} collective-permute-done((bf16[256,640]{1,0:T(8,128)(2,1)S(1)}, bf16[256,640]{1,0:T(8,128)(2,1)S(1)}, u32[]{:S(2)}, u32[]{:S(2)}) %collective-permute-start.61) | collective-permute-done | bytes 327712 | tf_op jit(solution)/shard_map/ppermute | solution.py:419
  636.1 12.7 %collective-permute-done.65 = bf16[256,640]{1,0:T(8,128)(2,1)S(1)} collective-permute-done((bf16[256,640]{1,0:T(8,128)(2,1)S(1)}, bf16[256,640]{1,0:T(8,128)(2,1)S(1)}, u32[]{:S(2)}, u32[]{:S(2)}) %collective-permute-start.65) | collective-permute-done | bytes 327712 | tf_op jit(solution)/shard_map/ppermute | solution.py:419
  652.0 5.2 shard_map.241
  687.5 65.2 %psum.7 = f32[2,960]{1,0:T(2,128)S(1)} all-reduce(f32[2,960]{1,0:T(2,128)S(1)} %pad_maximum_fusion.17), channel_id=1, replica_groups=mesh['dp'=4,'ctx'=8] {'dp','ctx'}, use_global_device_ids=true, to_apply=%region_6.7 | all-reduce | flops 1920 | bytes 15360 | tf_op jit(solution)/shard_map/psum | solution.py:646
  768.7 7.8 copy.310
  776.5 5.3 add_convert_fusion
  800.9 5.4 collective-permute-done.71
  812.2 9.7 %collective-permute-done.82 = bf16[2,1280,240]{1,2,0:T(8,128)(2,1)S(1)} collective-permute-done((bf16[2,1280,240]{1,2,0:T(8,128)(2,1)}, bf16[2,1280,240]{1,2,0:T(8,128)(2,1)S(1)}, u32[]{:S(2)}, u32[]{:S(2)}) %collective-permute-start.82) | collective-permute-done | bytes 1228832 | tf_op jit(solution)/shard_map/ppermute | solution.py:419
  822.5 23.2 %collective-permute-done.83 = bf16[2,1280,240]{1,2,0:T(8,128)(2,1)} collective-permute-done((bf16[2,1280,240]{1,2,0:T(8,128)(2,1)}, bf16[2,1280,240]{1,2,0:T(8,128)(2,1)}, u32[]{:S(2)}, u32[]{:S(2)}) %collective-permute-start.83) | collective-permute-done | bytes 1228832 | tf_op jit(solution)/shard_map/ppermute | solution.py:419
  858.6 7.3 collective-permute-done.85
  865.8 7.5 collective-permute-done.86
  (564 shorter events, 378.0 us)
Async XLA Ops:
  2.0 74.4 %collective-permute-start.14 = (bf16[2,1,40,240]{3,2,0,1:T(8,128)(2,1)}, bf16[2,1,40,240]{3,2,0,1:T(8,128)(2,1)}, u32[]{:S(2)}, u32[]{:S(2)}) collective-permute-start(bf16[2,1,40,240]{3,2,0,1:T(8,128)(2,1)} %fusion.53), channel_id=1, source_target_pairs={{0,2},{1,3},{2,4},{3,5},{4,6},{5,7},{6,0},{7,1},{8,10},{9,11},{10,... | collective-permute-start | bytes 115208 | tf_op jit(solution)/shard_map/ppermute | solution.py:419
  5.1 73.8 %collective-permute-start.15 = (bf16[2,1,40,240]{3,2,0,1:T(8,128)(2,1)}, bf16[2,1,40,240]{3,2,0,1:T(8,128)(2,1)}, u32[]{:S(2)}, u32[]{:S(2)}) collective-permute-start(bf16[2,1,40,240]{3,2,0,1:T(8,128)(2,1)} %fusion.53), channel_id=1, source_target_pairs={{0,4},{1,5},{2,6},{3,7},{4,0},{5,1},{6,2},{7,3},{8,12},{9,13},{10,... | collective-permute-start | bytes 115208 | tf_op jit(solution)/shard_map/ppermute | solution.py:419
  84.5 46.3 %collective-permute-start.40 = (bf16[2,1,320,240]{3,2,0,1:T(8,128)(2,1)}, bf16[2,1,320,240]{3,2,0,1:T(8,128)(2,1)S(1)}, u32[]{:S(2)}, u32[]{:S(2)}) collective-permute-start(bf16[2,1,320,240]{3,2,0,1:T(8,128)(2,1)} %fusion.43), channel_id=1, source_target_pairs={{0,6},{1,7},{2,0},{3,1},{4,2},{5,3},{6,4},{7,5},{8,14},{9,15},{10,... | collective-permute-start | bytes 921608 | tf_op jit(solution)/shard_map/ppermute | solution.py:419
  143.9 54.2 %collective-permute-start.53 = (bf16[1280,240]{0,1:T(8,128)(2,1)}, bf16[1280,240]{0,1:T(8,128)(2,1)S(1)}, u32[]{:S(2)}, u32[]{:S(2)}) collective-permute-start(bf16[1280,240]{0,1:T(8,128)(2,1)} %copy.264), channel_id=1, source_target_pairs={{0,2},{1,3},{2,4},{3,5},{4,6},{5,7},{6,0},{7,1},{8,10},{9,11},{10,... | collective-permute-start | bytes 1843208 | tf_op jit(solution)/shard_map/ppermute | solution.py:419
  147.1 52.8 %collective-permute-start.55 = (bf16[1280,240]{0,1:T(8,128)(2,1)}, bf16[1280,240]{0,1:T(8,128)(2,1)S(1)}, u32[]{:S(2)}, u32[]{:S(2)}) collective-permute-start(bf16[1280,240]{0,1:T(8,128)(2,1)} %copy.264), channel_id=1, source_target_pairs={{0,4},{1,5},{2,6},{3,7},{4,0},{5,1},{6,2},{7,3},{8,12},{9,13},{10,... | collective-permute-start | bytes 1843208 | tf_op jit(solution)/shard_map/ppermute | solution.py:419
  147.7 52.2 %collective-permute-start.57 = (bf16[1280,240]{0,1:T(8,128)(2,1)}, bf16[1280,240]{0,1:T(8,128)(2,1)S(1)}, u32[]{:S(2)}, u32[]{:S(2)}) collective-permute-start(bf16[1280,240]{0,1:T(8,128)(2,1)} %copy.264), channel_id=1, source_target_pairs={{0,6},{1,7},{2,0},{3,1},{4,2},{5,3},{6,4},{7,5},{8,14},{9,15},{10,... | collective-permute-start | bytes 1843208 | tf_op jit(solution)/shard_map/ppermute | solution.py:419
  151.6 66.1 %collective-permute-start.52 = (bf16[1280,240]{0,1:T(8,128)(2,1)}, bf16[1280,240]{0,1:T(8,128)(2,1)S(1)}, u32[]{:S(2)}, u32[]{:S(2)}) collective-permute-start(bf16[1280,240]{0,1:T(8,128)(2,1)} %copy.264), channel_id=1, source_target_pairs={{0,1},{1,0},{2,3},{3,2},{4,5},{5,4},{6,7},{7,6},{8,9},{9,8},{10,11... | collective-permute-start | bytes 1843208 | tf_op jit(solution)/shard_map/ppermute | solution.py:419
  151.6 45.8 %collective-permute-start.32 = (bf16[1,1,256,640]{3,2,1,0:T(8,128)(2,1)S(1)}, bf16[1,1,256,640]{3,2,1,0:T(8,128)(2,1)}, u32[]{:S(2)}, u32[]{:S(2)}) collective-permute-start(bf16[1,1,256,640]{3,2,1,0:T(8,128)(2,1)S(1)} %get-tuple-element.166), channel_id=1, source_target_pairs={{0,2},{1,3},{2,4},{3,5},{4,6},{5,7},{8,10},{9,11},{10,12},{11,13},... | collective-permute-start | bytes 983048 | tf_op jit(solution)/shard_map/ppermute | solution.py:419
  260.9 55.0 %collective-permute-start.44 = (bf16[2,1280,240]{1,2,0:T(8,128)(2,1)}, bf16[2,1280,240]{1,2,0:T(8,128)(2,1)}, u32[]{:S(2)}, u32[]{:S(2)}) collective-permute-start(bf16[2,1280,240]{1,2,0:T(8,128)(2,1)} %copy.257), channel_id=1, source_target_pairs={{0,16},{1,17},{2,18},{3,19},{4,20},{5,21},{6,22},{7,23},{8,24},{9,... | collective-permute-start | bytes 3686408 | tf_op jit(solution)/shard_map/ppermute | solution.py:419
  263.6 54.8 %collective-permute-start.46 = (bf16[2,1280,240]{1,2,0:T(8,128)(2,1)}, bf16[2,1280,240]{1,2,0:T(8,128)(2,1)}, u32[]{:S(2)}, u32[]{:S(2)}) collective-permute-start(bf16[2,1280,240]{1,2,0:T(8,128)(2,1)} %copy.257), channel_id=1, source_target_pairs={{0,24},{1,25},{2,26},{3,27},{4,28},{5,29},{6,30},{7,31},{8,16},{9,... | collective-permute-start | bytes 3686408 | tf_op jit(solution)/shard_map/ppermute | solution.py:419
  265.0 56.2 %collective-permute-start.41 = (bf16[2,1280,240]{1,2,0:T(8,128)(2,1)}, bf16[2,1280,240]{1,2,0:T(8,128)(2,1)}, u32[]{:S(2)}, u32[]{:S(2)}) collective-permute-start(bf16[2,1280,240]{1,2,0:T(8,128)(2,1)} %copy.257), channel_id=1, source_target_pairs={{0,1},{1,0},{2,3},{3,2},{4,5},{5,4},{6,7},{7,6},{8,9},{9,8},{10,11... | collective-permute-start | bytes 3686408 | tf_op jit(solution)/shard_map/ppermute | solution.py:419
  277.2 46.5 %collective-permute-start.30 = (bf16[1,1,256,640]{3,2,1,0:T(8,128)(2,1)}, bf16[1,1,256,640]{3,2,1,0:T(8,128)(2,1)}, u32[]{:S(2)}, u32[]{:S(2)}) collective-permute-start(bf16[1,1,256,640]{3,2,1,0:T(8,128)(2,1)} %collective-permute-done.29), channel_id=1, source_target_pairs={{0,1},{1,0},{2,3},{3,2},{4,5},{5,4},{6,7},{7,6},{8,9},{9,8},{10,11... | collective-permute-start | bytes 983048 | tf_op jit(solution)/shard_map/ppermute | solution.py:419
  277.2 46.5 %collective-permute-start.37 = (bf16[1,1,256,640]{3,2,1,0:T(8,128)(2,1)}, bf16[1,1,256,640]{3,2,1,0:T(8,128)(2,1)}, u32[]{:S(2)}, u32[]{:S(2)}) collective-permute-start(bf16[1,1,256,640]{3,2,1,0:T(8,128)(2,1)} %collective-permute-done.36), channel_id=1, source_target_pairs={{0,1},{1,0},{2,3},{3,2},{4,5},{5,4},{6,7},{7,6},{8,9},{9,8},{10,11... | collective-permute-start | bytes 983048 | tf_op jit(solution)/shard_map/ppermute | solution.py:419
  315.9 64.6 %collective-permute-start.43 = (bf16[2,1280,240]{1,2,0:T(8,128)(2,1)}, bf16[2,1280,240]{1,2,0:T(8,128)(2,1)}, u32[]{:S(2)}, u32[]{:S(2)}) collective-permute-start(bf16[2,1280,240]{1,2,0:T(8,128)(2,1)} %copy-done.31), channel_id=1, source_target_pairs={{0,1},{1,0},{2,3},{3,2},{4,5},{5,4},{6,7},{7,6},{8,9},{9,8},{10,11... | collective-permute-start | bytes 3686408 | tf_op jit(solution)/shard_map/ppermute | solution.py:419
  318.3 64.6 %collective-permute-start.45 = (bf16[2,1280,240]{1,2,0:T(8,128)(2,1)}, bf16[2,1280,240]{1,2,0:T(8,128)(2,1)}, u32[]{:S(2)}, u32[]{:S(2)}) collective-permute-start(bf16[2,1280,240]{1,2,0:T(8,128)(2,1)} %collective-permute-done.44), channel_id=1, source_target_pairs={{0,1},{1,0},{2,3},{3,2},{4,5},{5,4},{6,7},{7,6},{8,9},{9,8},{10,11... | collective-permute-start | bytes 3686408 | tf_op jit(solution)/shard_map/ppermute | solution.py:419
  321.3 64.1 %collective-permute-start.47 = (bf16[2,1280,240]{1,2,0:T(8,128)(2,1)}, bf16[2,1280,240]{1,2,0:T(8,128)(2,1)}, u32[]{:S(2)}, u32[]{:S(2)}) collective-permute-start(bf16[2,1280,240]{1,2,0:T(8,128)(2,1)} %collective-permute-done.46), channel_id=1, source_target_pairs={{0,1},{1,0},{2,3},{3,2},{4,5},{5,4},{6,7},{7,6},{8,9},{9,8},{10,11... | collective-permute-start | bytes 3686408 | tf_op jit(solution)/shard_map/ppermute | solution.py:419
  462.1 124.5 %collective-permute-start.59 = (bf16[4,256,640]{2,1,0:T(8,128)(2,1)}, bf16[4,256,640]{2,1,0:T(8,128)(2,1)}, u32[]{:S(2)}, u32[]{:S(2)}) collective-permute-start(bf16[4,256,640]{2,1,0:T(8,128)(2,1)} %dynamic-slice_bitcast_fusion.1), channel_id=1, source_target_pairs={{0,1},{1,0},{2,3},{3,2},{4,5},{5,4},{6,7},{7,6},{8,9},{9,8},{10,11... | collective-permute-start | bytes 3932168 | tf_op jit(solution)/shard_map/ppermute | solution.py:419
  478.8 111.0 %collective-permute-start.63 = (bf16[4,256,640]{2,1,0:T(8,128)(2,1)}, bf16[4,256,640]{2,1,0:T(8,128)(2,1)}, u32[]{:S(2)}, u32[]{:S(2)}) collective-permute-start(bf16[4,256,640]{2,1,0:T(8,128)(2,1)} %dynamic-slice_bitcast_fusion), channel_id=1, source_target_pairs={{0,1},{1,0},{2,3},{3,2},{4,5},{5,4},{6,7},{7,6},{8,9},{9,8},{10,11... | collective-permute-start | bytes 3932168 | tf_op jit(solution)/shard_map/ppermute | solution.py:419
  511.8 81.0 %collective-permute-start.78 = (bf16[120,240]{0,1:T(8,128)(2,1)S(1)}, bf16[120,240]{0,1:T(8,128)(2,1)S(1)}, u32[]{:S(2)}, u32[]{:S(2)}) collective-permute-start(bf16[120,240]{0,1:T(8,128)(2,1)S(1)} %get-tuple-element.186), channel_id=1, source_target_pairs={{0,2},{1,3},{2,4},{3,5},{4,6},{5,7},{6,0},{7,1},{8,10},{9,11},{10,... | collective-permute-start | bytes 172808 | tf_op jit(solution)/shard_map/ppermute | solution.py:419
  536.5 57.7 %collective-permute-start.79 = (bf16[120,240]{0,1:T(8,128)(2,1)S(1)}, bf16[120,240]{0,1:T(8,128)(2,1)S(1)}, u32[]{:S(2)}, u32[]{:S(2)}) collective-permute-start(bf16[120,240]{0,1:T(8,128)(2,1)S(1)} %get-tuple-element.188), channel_id=1, source_target_pairs={{0,4},{1,5},{2,6},{3,7},{4,0},{5,1},{6,2},{7,3},{8,12},{9,13},{10,... | collective-permute-start | bytes 172808 | tf_op jit(solution)/shard_map/ppermute | solution.py:419
  589.8 44.2 %collective-permute-start.61 = (bf16[256,640]{1,0:T(8,128)(2,1)S(1)}, bf16[256,640]{1,0:T(8,128)(2,1)S(1)}, u32[]{:S(2)}, u32[]{:S(2)}) collective-permute-start(bf16[256,640]{1,0:T(8,128)(2,1)S(1)} %get-tuple-element.133), channel_id=1, source_target_pairs={{4,0},{5,1},{6,2},{7,3},{12,8},{13,9},{14,10},{15,11},{20,16},{21,... | collective-permute-start | bytes 983048 | tf_op jit(solution)/shard_map/ppermute | solution.py:419
  592.8 43.2 %collective-permute-start.62 = (bf16[256,640]{1,0:T(8,128)(2,1)S(1)}, bf16[256,640]{1,0:T(8,128)(2,1)S(1)}, u32[]{:S(2)}, u32[]{:S(2)}) collective-permute-start(bf16[256,640]{1,0:T(8,128)(2,1)S(1)} %get-tuple-element.132), channel_id=1, source_target_pairs={{6,0},{7,1},{14,8},{15,9},{22,16},{23,17},{30,24},{31,25}} | collective-permute-start | bytes 983048 | tf_op jit(solution)/shard_map/ppermute | solution.py:419
  594.2 73.6 %collective-permute-start.88 = (bf16[4,1280,240]{1,2,0:T(8,128)(2,1)}, bf16[4,1280,240]{1,2,0:T(8,128)(2,1)}, u32[]{:S(2)}, u32[]{:S(2)}) collective-permute-start(bf16[4,1280,240]{1,2,0:T(8,128)(2,1)} %copy.318), channel_id=1, source_target_pairs={{0,1},{1,0},{2,3},{3,2},{4,5},{5,4},{6,7},{7,6},{8,9},{9,8},{10,11... | collective-permute-start | bytes 7372808 | tf_op jit(solution)/shard_map/ppermute | solution.py:419
  594.3 41.8 %collective-permute-start.64 = (bf16[256,640]{1,0:T(8,128)(2,1)S(1)}, bf16[256,640]{1,0:T(8,128)(2,1)S(1)}, u32[]{:S(2)}, u32[]{:S(2)}) collective-permute-start(bf16[256,640]{1,0:T(8,128)(2,1)S(1)} %get-tuple-element.134), channel_id=1, source_target_pairs={{2,0},{3,1},{4,2},{5,3},{6,4},{7,5},{10,8},{11,9},{12,10},{13,11},... | collective-permute-start | bytes 983048 | tf_op jit(solution)/shard_map/ppermute | solution.py:419
  599.2 49.6 %collective-permute-start.65 = (bf16[256,640]{1,0:T(8,128)(2,1)S(1)}, bf16[256,640]{1,0:T(8,128)(2,1)S(1)}, u32[]{:S(2)}, u32[]{:S(2)}) collective-permute-start(bf16[256,640]{1,0:T(8,128)(2,1)S(1)} %get-tuple-element.136), channel_id=1, source_target_pairs={{4,0},{5,1},{6,2},{7,3},{12,8},{13,9},{14,10},{15,11},{20,16},{21,... | collective-permute-start | bytes 983048 | tf_op jit(solution)/shard_map/ppermute | solution.py:419
  635.9 132.4 %collective-permute-start.81 = (bf16[4,2,1280,240]{2,3,1,0:T(8,128)(2,1)}, bf16[4,2,1280,240]{2,3,1,0:T(8,128)(2,1)}, u32[]{:S(2)}, u32[]{:S(2)}) collective-permute-start(bf16[4,2,1280,240]{2,3,1,0:T(8,128)(2,1)} %copy.309), channel_id=1, source_target_pairs={{0,1},{1,0},{2,3},{3,2},{4,5},{5,4},{6,7},{7,6},{8,9},{9,8},{10,11... | collective-permute-start | bytes 14745608 | tf_op jit(solution)/shard_map/ppermute | solution.py:419
  661.1 102.3 %collective-permute-start.67 = (bf16[4,4,200,240]{3,2,1,0:T(8,128)(2,1)}, bf16[4,4,200,240]{3,2,1,0:T(8,128)(2,1)}, u32[]{:S(2)}, u32[]{:S(2)}) collective-permute-start(bf16[4,4,200,240]{3,2,1,0:T(8,128)(2,1)} %pad_maximum_fusion), channel_id=1, source_target_pairs={{0,1},{1,0},{2,3},{3,2},{4,5},{5,4},{6,7},{7,6},{8,9},{9,8},{10,11... | collective-permute-start | bytes 4608008 | tf_op jit(solution)/shard_map/ppermute | solution.py:419
  678.0 75.3 %collective-permute-start.89 = (bf16[1280,240]{0,1:T(8,128)(2,1)}, bf16[1280,240]{0,1:T(8,128)(2,1)}, u32[]{:S(2)}, u32[]{:S(2)}) collective-permute-start(bf16[1280,240]{0,1:T(8,128)(2,1)} %copy.320), channel_id=1, source_target_pairs={{0,6},{1,7},{2,0},{3,1},{4,2},{5,3},{6,4},{7,5},{8,14},{9,15},{10,... | collective-permute-start | bytes 1843208 | tf_op jit(solution)/shard_map/ppermute | solution.py:419
  679.0 75.6 %collective-permute-start.90 = (bf16[1280,240]{0,1:T(8,128)(2,1)}, bf16[1280,240]{0,1:T(8,128)(2,1)}, u32[]{:S(2)}, u32[]{:S(2)}) collective-permute-start(bf16[1280,240]{0,1:T(8,128)(2,1)} %copy.322), channel_id=1, source_target_pairs={{0,4},{1,5},{2,6},{3,7},{4,0},{5,1},{6,2},{7,3},{8,12},{9,13},{10,... | collective-permute-start | bytes 1843208 | tf_op jit(solution)/shard_map/ppermute | solution.py:419
  680.2 75.8 %collective-permute-start.91 = (bf16[1280,240]{0,1:T(8,128)(2,1)}, bf16[1280,240]{0,1:T(8,128)(2,1)}, u32[]{:S(2)}, u32[]{:S(2)}) collective-permute-start(bf16[1280,240]{0,1:T(8,128)(2,1)} %copy.324), channel_id=1, source_target_pairs={{0,2},{1,3},{2,4},{3,5},{4,6},{5,7},{6,0},{7,1},{8,10},{9,11},{10,... | collective-permute-start | bytes 1843208 | tf_op jit(solution)/shard_map/ppermute | solution.py:419
  793.7 52.0 %collective-permute-start.83 = (bf16[2,1280,240]{1,2,0:T(8,128)(2,1)}, bf16[2,1280,240]{1,2,0:T(8,128)(2,1)}, u32[]{:S(2)}, u32[]{:S(2)}) collective-permute-start(bf16[2,1280,240]{1,2,0:T(8,128)(2,1)} %copy.313), channel_id=1, source_target_pairs={{0,16},{1,17},{2,18},{3,19},{4,20},{5,21},{6,22},{7,23},{8,24},{9,... | collective-permute-start | bytes 3686408 | tf_op jit(solution)/shard_map/ppermute | solution.py:419
  794.1 53.3 %collective-permute-start.84 = (bf16[2,1280,240]{1,2,0:T(8,128)(2,1)}, bf16[2,1280,240]{1,2,0:T(8,128)(2,1)}, u32[]{:S(2)}, u32[]{:S(2)}) collective-permute-start(bf16[2,1280,240]{1,2,0:T(8,128)(2,1)} %copy.315), channel_id=1, source_target_pairs={{0,24},{1,25},{2,26},{3,27},{4,28},{5,29},{6,30},{7,31},{8,16},{9,... | collective-permute-start | bytes 3686408 | tf_op jit(solution)/shard_map/ppermute | solution.py:419
  (133 other events, 1817.9 us)

commit v2 on v1

v2 whole, which is shorter than its diff:
```python
import functools

import jax
import jax.numpy as jnp
import numpy as np
from jax import lax
from jax.experimental import pallas as pl
from jax.experimental.layout import Layout, with_layout_constraint
from jax.experimental.pallas import tpu as pltpu
from jax.sharding import PartitionSpec as P

QUERY_HEADS = 15
KEY_VALUE_HEADS = 5
HEAD_SIZE = 64
GROUP = QUERY_HEADS // KEY_VALUE_HEADS
HALF = HEAD_SIZE // 2

epsilon = 1e-05
theta_base = 100000.0
masked_score = -1e30
lowest_top = -1e29
score_scale = 0.125
VMEM_BYTES = 56 * 1024 * 1024

BF = jnp.bfloat16
F32 = jnp.float32


def dot_nn(a, b):
    return lax.dot_general(a, b, (((1,), (0,)), ((), ())), preferred_element_type=F32)


def dot_nt(a, b):
    return lax.dot_general(a, b, (((1,), (1,)), ((), ())), preferred_element_type=F32)


def dot_tn(a, b):
    return lax.dot_general(a, b, (((0,), (0,)), ((), ())), preferred_element_type=F32)


def vmem_spec():
    return pl.BlockSpec(memory_space=pltpu.VMEM)


def smem_spec():
    return pl.BlockSpec(memory_space=pltpu.SMEM)


def params():
    return pltpu.CompilerParams(vmem_limit_bytes=VMEM_BYTES)


def cost(flops, bytes_accessed, transcendentals=0):
    part = 64
    return pl.CostEstimate(
        flops=int(flops) // part,
        bytes_accessed=int(bytes_accessed) // part,
        transcendentals=int(transcendentals) // part,
    )


def rotate(value, cosine, sine, limit=None):
    width = value.shape[1]
    lane = lax.broadcasted_iota(jnp.int32, value.shape, 1)
    ahead = pltpu.roll(value, width - HALF, 1)
    behind = pltpu.roll(value, HALF, 1)
    swapped = jnp.where(lane % HEAD_SIZE < HALF, ahead, behind)
    copies = width // 128
    cos_wide = jnp.concatenate([cosine] * copies, axis=1)
    sin_wide = jnp.concatenate([sine] * copies, axis=1)
    turned = value * cos_wide + swapped * sin_wide
    if limit is not None:
        turned = jnp.where(lane < limit, turned, value)
    return turned


def row_chunks(rows):
    size = min(128, rows)
    return [slice(start, start + size) for start in range(0, rows, size)]


def column_chunks(columns):
    return [slice(start, min(start + 256, columns)) for start in range(0, columns, 256)]


def scale_of(value):
    return lax.rsqrt(jnp.mean(value * value, axis=1, keepdims=True) + epsilon)


def call(body, operands, n_smem, outs, flops, scratch=()):
    moved = sum(o.size * o.dtype.itemsize for o in operands) + sum(
        int(np.prod(o.shape)) * o.dtype.itemsize for o in outs
    )
    return pl.pallas_call(
        body,
        out_shape=tuple(outs),
        in_specs=[smem_spec()] * n_smem + [vmem_spec()] * (len(operands) - n_smem),
        out_specs=tuple(vmem_spec() for _ in outs),
        scratch_shapes=list(scratch),
        compiler_params=params(),
        cost_estimate=cost(flops, moved),
    )(*operands)


def shape(dims, dtype):
    return jax.ShapeDtypeStruct(tuple(dims), dtype)


def block_product(x_ref, index_ref, weights, columns):
    total = None
    for m, weight in enumerate(weights):
        term = dot_nt(x_ref[index_ref[m]], weight[columns, :])
        total = term if total is None else total + term
    return total


def keys_values(hidden, gain, index, weights, cosine, sine):
    nd = len(weights)
    rows, width = hidden.shape
    depth = width // nd
    columns = weights[0].shape[0]
    turn = KEY_VALUE_HEADS * HEAD_SIZE

    def body(index_ref, hidden_ref, gain_ref, cos_ref, sin_ref, *rest):
        w, (blocks_ref, kv_ref) = rest[:nd], rest[nd:]
        for here in row_chunks(rows):
            x = hidden_ref[here, :].astype(F32)
            normed = (x * scale_of(x) * gain_ref[...]).astype(BF)
            for b in range(nd):
                blocks_ref[b, here, :] = normed[:, b * depth : (b + 1) * depth]
        for cols in column_chunks(columns):
            total = block_product(blocks_ref, index_ref, w, cols)
            if turn > cols.start:
                total = rotate(total, cos_ref[...], sin_ref[...], turn - cols.start if turn < cols.stop else None)
            kv_ref[:, cols] = total.astype(BF)

    return call(
        body,
        [index, hidden, gain, cosine, sine, *weights],
        1,
        [shape((nd, rows, depth), BF), shape((rows, columns), BF)],
        2 * rows * columns * width,
    )


def queries(blocks, index, weights, cosine, sine):
    nd, rows, depth = blocks.shape
    columns = weights[0].shape[0]

    def body(index_ref, blocks_ref, cos_ref, sin_ref, *rest):
        w, out_ref = rest[:nd], rest[nd]
        for cols in column_chunks(columns):
            total = block_product(blocks_ref, index_ref, w, cols)
            out_ref[:, cols] = rotate(total, cos_ref[...], sin_ref[...]).astype(BF)

    return call(
        body,
        [index, blocks, cosine, sine, *weights],
        1,
        [shape((rows, columns), BF)],
        2 * rows * columns * nd * depth,
    )[0]


def middle(att_parts, hidden, gain, index, weights):
    nd = len(weights)
    parts = len(att_parts)
    rows, width = hidden.shape
    depth = width // nd
    span = rows // parts

    def body(index_ref, hidden_ref, gain_ref, *rest):
        att, w = rest[:parts], rest[parts : parts + nd]
        att_ref, mid_ref, two_ref = rest[parts + nd :]
        for p in range(parts):
            for b in range(nd):
                att_ref[b, p * span : (p + 1) * span, :] = att[p][:, b * depth : (b + 1) * depth]
        for cols in column_chunks(width):
            mid_ref[:, cols] = hidden_ref[:, cols].astype(F32) + block_product(att_ref, index_ref, w, cols)
        for here in row_chunks(rows):
            x = mid_ref[here, :]
            normed = (x * scale_of(x) * gain_ref[...]).astype(BF)
            for b in range(nd):
                two_ref[b, here, :] = normed[:, b * depth : (b + 1) * depth]

    return call(
        body,
        [index, hidden, gain, *att_parts, *weights],
        1,
        [
            shape((nd, rows, depth), BF),
            shape((rows, width), F32),
            shape((nd, rows, depth), BF),
        ],
        2 * rows * width * width,
    )


def middle_back(mid, out_grad, gain, index, att_blocks, made, dn, weights):
    nd = len(weights)
    rows, width = mid.shape
    depth = width // nd

    def body(index_ref, mid_ref, grad_ref, gain_ref, att_ref, made_ref, dn_ref, *rest):
        w = rest[:nd]
        layer_ref, dmid_ref, datt_ref, dw_ref, sum_ref, low_ref, block_ref = rest[nd:]
        sums = jnp.zeros((1, width), F32)
        for here in row_chunks(rows):
            x = mid_ref[here, :]
            up = grad_ref[here, :].astype(F32)
            layer_ref[here, :] = (x + made_ref[here, :]).astype(BF)
            dn = jnp.concatenate([dn_ref[b, here, :] for b in range(nd)], axis=1)
            scale = scale_of(x)
            weighted = dn * gain_ref[...]
            sums += jnp.sum(dn * x * scale, axis=0, keepdims=True)
            inner = jnp.mean(weighted * x, axis=1, keepdims=True)
            dmid = up + scale * weighted - x * (scale * scale * scale * inner)
            dmid_ref[here, :] = dmid
            low_ref[here, :] = dmid.astype(BF)
        sum_ref[...] = sums
        for m in range(nd):
            place = index_ref[m]
            block_ref[place] = dot_nn(low_ref[...], w[m][...])
            for cols in column_chunks(width):
                dw_ref[m, cols, :] = dot_tn(low_ref[:, cols], att_ref[place]).astype(BF)
        for b in range(nd):
            datt_ref[:, b * depth : (b + 1) * depth] = block_ref[b].astype(BF)

    return call(
        body,
        [index, mid, out_grad, gain, att_blocks, made, dn, *weights],
        1,
        [
            shape((rows, width), BF),
            shape((rows, width), F32),
            shape((rows, width), BF),
            shape((nd, width, depth), BF),
            shape((1, width), F32),
        ],
        4 * rows * width * width,
        [pltpu.VMEM((rows, width), BF), pltpu.VMEM((nd, rows, depth), F32)],
    )


def queries_back(dq_parts, blocks, index, weights):
    nd, rows, depth = blocks.shape
    parts = len(dq_parts)
    span = rows // parts
    columns = weights[0].shape[0]

    def body(index_ref, blocks_ref, *rest):
        dq, w = rest[:parts], rest[parts : parts + nd]
        dx_ref, dw_ref, all_ref = rest[parts + nd :]
        for p in range(parts):
            all_ref[p * span : (p + 1) * span, :] = dq[p][...]
        for m in range(nd):
            place = index_ref[m]
            dx_ref[place] = dot_nn(all_ref[...], w[m][...])
            for cols in column_chunks(columns):
                dw_ref[m, cols, :] = dot_tn(all_ref[:, cols], blocks_ref[place]).astype(BF)

    return call(
        body,
        [index, blocks, *dq_parts, *weights],
        1,
        [shape((nd, rows, depth), F32), shape((nd, columns, depth), BF)],
        4 * rows * columns * nd * depth,
        [pltpu.VMEM((rows, columns), BF)],
    )


def keys_values_back(dkv_parts, blocks, dx_blocks, dmid, hidden, gain, index, weights, cosine, sine):
    nd, rows, depth = blocks.shape
    parts = len(dkv_parts)
    columns = weights[0].shape[0]
    width = nd * depth
    turn = KEY_VALUE_HEADS * HEAD_SIZE
    pieces = len(dkv_parts[0])
    flat = [piece for part in dkv_parts for piece in part]
    span = rows // parts

    def body(index_ref, blocks_ref, dx_ref, dmid_ref, hidden_ref, gain_ref, cos_ref, sin_ref, *rest):
        got, w = rest[: parts * pieces], rest[parts * pieces : parts * pieces + nd]
        grad_ref, dw_ref, sum_ref, low_ref, block_ref = rest[parts * pieces + nd :]
        for p in range(parts):
            here = slice(p * span, (p + 1) * span)
            for cols in column_chunks(columns):
                total = got[p * pieces][:, cols].astype(F32)
                for piece in got[p * pieces + 1 : (p + 1) * pieces]:
                    total = total + piece[:, cols].astype(F32)
                if turn > cols.start:
                    limit = turn - cols.start if turn < cols.stop else None
                    total = rotate(total, cos_ref[here, :], -sin_ref[here, :], limit)
                low_ref[here, cols] = total.astype(BF)
        for m in range(nd):
            place = index_ref[m]
            block_ref[place] = dx_ref[place] + dot_nn(low_ref[...], w[m][...])
            for cols in column_chunks(columns):
                dw_ref[m, cols, :] = dot_tn(low_ref[:, cols], blocks_ref[place]).astype(BF)
        sums = jnp.zeros((1, width), F32)
        for here in row_chunks(rows):
            x = hidden_ref[here, :].astype(F32)
            dn = jnp.concatenate([block_ref[b, here, :] for b in range(nd)], axis=1)
            scale = scale_of(x)
            weighted = dn * gain_ref[...]
            sums += jnp.sum(dn * x * scale, axis=0, keepdims=True)
            inner = jnp.mean(weighted * x, axis=1, keepdims=True)
            grad = dmid_ref[here, :] + scale * weighted - x * (scale * scale * scale * inner)
            grad_ref[here, :] = grad.astype(BF)
        sum_ref[...] = sums

    return call(
        body,
        [index, blocks, dx_blocks, dmid, hidden, gain, cosine, sine, *flat, *weights],
        1,
        [shape((rows, width), BF), shape((nd, columns, depth), BF), shape((1, width), F32)],
        4 * rows * columns * width,
        [pltpu.VMEM((rows, columns), BF), pltpu.VMEM((nd, rows, depth), F32)],
    )


def feed_forward(core, blocks, top, weights, part):
    nd, nz, _, _, depth = weights.shape
    wide = depth + -depth % 128
    rows, width = top.shape
    sub = nz // nd
    half = sub * part
    z_depth = width // nz

    def body(
        core_ref, n2_ref, top_ref, gu_own, gu_other, down_own, down_other, out_ref, dn_ref, dw_own, dw_other,
        tops, outs, w_gu, w_down, dgu, dd, sems,
    ):
        step = pl.program_id(0)

        def copies(at):
            made = []
            for h, ref in enumerate((dw_own, dw_other)):
                made.append(
                    pltpu.make_async_copy(
                        dgu.at[h], ref.at[:, pl.ds(at * sub, sub), pl.ds(0, 2)], sems.at[2 * h]
                    )
                )
                made.append(
                    pltpu.make_async_copy(dd.at[h], ref.at[at, :, pl.ds(2, 1)], sems.at[2 * h + 1])
                )
            return made

        @pl.when(step == 0)
        def _():
            dn_ref[...] = jnp.zeros_like(dn_ref)
            outs[...] = jnp.zeros_like(outs)
            dgu[...] = jnp.zeros_like(dgu)
            dd[...] = jnp.zeros_like(dd)
            for b in range(nz):
                tops[b] = top_ref[:, b * z_depth : (b + 1) * z_depth]

        for h, (gu, down) in enumerate(((gu_own, down_own), (gu_other, down_other))):
            here = slice(h * half, (h + 1) * half)
            for b in range(nd):
                for which in range(2):
                    w_gu[b, which, here, :] = gu[b, :, 0, which * part : (which + 1) * part].reshape(half, depth)
            for b in range(nz):
                for s in range(sub):
                    w_down[b, h * half + s * part : h * half + (s + 1) * part, :] = down[
                        0, b, 0, :, s * z_depth : (s + 1) * z_depth
                    ]

        gate = up = grad_hidden = None
        for b in range(nd):
            term_g = dot_nt(n2_ref[b], w_gu[b, 0])
            term_u = dot_nt(n2_ref[b], w_gu[b, 1])
            gate = term_g if gate is None else gate + term_g
            up = term_u if up is None else up + term_u
        for b in range(nz):
            term = dot_nt(tops[b], w_down[b])
            grad_hidden = term if grad_hidden is None else grad_hidden + term
        sig = jax.nn.sigmoid(gate)
        act = gate * sig
        hidden = (act * up).astype(BF)
        d_gate = (grad_hidden * up * sig * (1.0 + gate * (1.0 - sig))).astype(BF)
        d_up = (grad_hidden * act).astype(BF)

        @pl.when(step > 0)
        def _():
            for copy in copies(step - 1):
                copy.wait()

        for b in range(nz):
            outs[b] += dot_nn(hidden, w_down[b])
            grad = dot_tn(hidden, tops[b]).astype(BF)
            for h in range(2):
                for s in range(sub):
                    start = h * half + s * part
                    dd[h, b, 0, :, s * z_depth : (s + 1) * z_depth] = grad[start : start + part]
        for b in range(nd):
            dn_ref[b] += dot_nn(d_gate, w_gu[b, 0]) + dot_nn(d_up, w_gu[b, 1])
            for which, value in ((0, d_gate), (1, d_up)):
                grad = dot_tn(value, n2_ref[b]).astype(BF)
                for h in range(2):
                    dgu[h, b, :, which, :, :depth] = grad[h * half : (h + 1) * half].reshape(sub, part, depth)
        for copy in copies(step):
            copy.start()

        @pl.when(step == nd - 1)
        def _():
            for b in range(nz):
                out_ref[:, b * z_depth : (b + 1) * z_depth] = outs[b]
            for copy in copies(step):
                copy.wait()

    def gu_spec(other):
        return pl.BlockSpec(
            (nd, sub, 1, 2 * part, depth),
            lambda i, core: (0, i, 1 - core[0] if other else core[0], 0, 0),
        )

    def down_spec(other):
        return pl.BlockSpec(
            (1, nz, 1, part, depth),
            lambda i, core: (i, 0, 1 - core[0] if other else core[0], 2, 0),
        )

    grad = shape((nd, nz, 3, part, wide), BF)
    return pl.pallas_call(
        body,
        grid_spec=pltpu.PrefetchScalarGridSpec(
            num_scalar_prefetch=1,
            grid=(nd,),
            in_specs=[
                pl.BlockSpec(blocks.shape, lambda i, core: (0, 0, 0)),
                pl.BlockSpec(top.shape, lambda i, core: (0, 0)),
                gu_spec(False),
                gu_spec(True),
                down_spec(False),
                down_spec(True),
            ],
            out_specs=(
                pl.BlockSpec((rows, width), lambda i, core: (0, 0)),
                pl.BlockSpec(blocks.shape, lambda i, core: (0, 0, 0)),
                pl.BlockSpec(memory_space=pl.ANY),
                pl.BlockSpec(memory_space=pl.ANY),
            ),
            scratch_shapes=[
                pltpu.VMEM((nz, rows, z_depth), BF),
                pltpu.VMEM((nz, rows, z_depth), F32),
                pltpu.VMEM((nd, 2, 2 * half, depth), BF),
                pltpu.VMEM((nz, 2 * half, z_depth), BF),
                pltpu.VMEM((2, nd, sub, 2, part, wide), BF),
                pltpu.VMEM((2, nz, 1, part, wide), BF),
                pltpu.SemaphoreType.DMA((4,)),
            ],
        ),
        out_shape=(shape((rows, width), F32), shape(blocks.shape, F32), grad, grad),
        compiler_params=params(),
        cost_estimate=cost(36 * rows * half * nd * width, 24 * half * nd * width, 2 * rows * half * nd),
    )(core, blocks, top, weights, weights, weights, weights)


def group_rows(ref, g):
    return jnp.concatenate(
        [ref[:, (g * GROUP + i) * HEAD_SIZE : (g * GROUP + i + 1) * HEAD_SIZE] for i in range(GROUP)],
        axis=0,
    )


def bias_of(start_ref, first_query, first_key, span, size):
    key = first_key + lax.broadcasted_iota(jnp.int32, (size, span), 0)
    query = first_query + lax.broadcasted_iota(jnp.int32, (size, span), 1)
    allowed = (key <= query) & (key >= start_ref[...])
    return jnp.concatenate([jnp.where(allowed, 0.0, masked_score)] * GROUP, axis=1)


def attend_kernel(
    span, size, pieces, info_ref, start_ref, q_ref, own, other, kv_ref, att_ref, lse_ref, acc, top, total, q_rows
):
    first_query = info_ref[0]
    for s in range(pieces):
        place = info_ref[4 + s]
        for ref, core in ((own, info_ref[3]), (other, 1 - info_ref[3])):
            kv_ref[pl.ds(pl.multiple_of((2 * place + core) * span, span), span), :] = ref[s]
    top[...] = jnp.full_like(top, lowest_top)
    total[...] = jnp.zeros_like(total)
    acc[...] = jnp.zeros_like(acc)
    value_at = KEY_VALUE_HEADS * HEAD_SIZE
    for g in range(KEY_VALUE_HEADS):
        q_rows[g] = group_rows(q_ref, g) * BF(score_scale)

    def one_block(block, carry):
        first_key = pl.multiple_of(block * size, size)
        bias = bias_of(start_ref, first_query, first_key, span, size)
        for g in range(KEY_VALUE_HEADS):
            k_at, v_at = g * HEAD_SIZE, value_at + g * HEAD_SIZE
            keys = kv_ref[pl.ds(first_key, size), k_at : k_at + HEAD_SIZE]
            values = kv_ref[pl.ds(first_key, size), v_at : v_at + HEAD_SIZE]
            scores = dot_nt(keys, q_rows[g]) + bias
            old_top = top[g]
            new_top = jnp.maximum(old_top, jnp.max(scores, axis=0, keepdims=True))
            rescale = jnp.exp(old_top - new_top)
            expo = jnp.exp(scores - new_top)
            total[g] = total[g] * rescale + jnp.sum(expo, axis=0, keepdims=True)
            acc[g] = acc[g] * rescale + dot_tn(values, expo.astype(BF))
            top[g] = new_top
        return carry

    lax.fori_loop(info_ref[1], info_ref[2], one_block, 0)
    for g in range(KEY_VALUE_HEADS):
        whole = total[g]
        result = (acc[g] * (1.0 / whole)).T.astype(BF)
        lse_ref[g] = top[g] + jnp.log(whole)
        for i in range(GROUP):
            h = g * GROUP + i
            att_ref[:, h * HEAD_SIZE : (h + 1) * HEAD_SIZE] = result[i * span : (i + 1) * span]


def attend(info, start, q, own, other, size):
    span = q.shape[0]
    rows = GROUP * span
    pieces = own.shape[0]
    length = 2 * pieces * span
    return pl.pallas_call(
        functools.partial(attend_kernel, span, size, pieces),
        out_shape=(
            jax.ShapeDtypeStruct((length, 2 * KEY_VALUE_HEADS * HEAD_SIZE), BF),
            jax.ShapeDtypeStruct((span, QUERY_HEADS * HEAD_SIZE), BF),
            jax.ShapeDtypeStruct((KEY_VALUE_HEADS, 1, rows), F32),
        ),
        in_specs=[smem_spec()] + [vmem_spec()] * 4,
        out_specs=(vmem_spec(), vmem_spec(), vmem_spec()),
        scratch_shapes=[
            pltpu.VMEM((KEY_VALUE_HEADS, HEAD_SIZE, rows), F32),
            pltpu.VMEM((KEY_VALUE_HEADS, 1, rows), F32),
            pltpu.VMEM((KEY_VALUE_HEADS, 1, rows), F32),
            pltpu.VMEM((KEY_VALUE_HEADS, rows, HEAD_SIZE), BF),
        ],
        compiler_params=params(),
        cost_estimate=cost(
            16 * QUERY_HEADS * HEAD_SIZE * span * length,
            4 * length * KEY_VALUE_HEADS * HEAD_SIZE,
            QUERY_HEADS * span * length,
        ),
    )(info, start, q, own, other)


def attend_back_kernel(
    span, size, info_ref, start_ref, q_ref, kv_ref, att_ref, datt_ref, lse_ref, cos_ref, sin_ref,
    dq_ref, dkv_ref, dq_acc, q_rows, d_rows, dot_rows,
):
    first_query = info_ref[0]
    value_at = KEY_VALUE_HEADS * HEAD_SIZE
    dq_acc[...] = jnp.zeros_like(dq_acc)
    dkv_ref[...] = jnp.zeros_like(dkv_ref)
    for g in range(KEY_VALUE_HEADS):
        grads = group_rows(datt_ref, g)
        q_rows[g] = group_rows(q_ref, g) * BF(score_scale)
        d_rows[g] = grads
        products = grads.astype(F32) * group_rows(att_ref, g).astype(F32)
        dot_rows[g] = jnp.sum(products.T, axis=0, keepdims=True)

    def one_block(block, carry):
        first_key = pl.multiple_of(block * size, size)
        bias = bias_of(start_ref, first_query, first_key, span, size)
        for g in range(KEY_VALUE_HEADS):
            k_at, v_at = g * HEAD_SIZE, value_at + g * HEAD_SIZE
            rows = q_rows[g]
            grads = d_rows[g]
            keys = kv_ref[pl.ds(first_key, size), k_at : k_at + HEAD_SIZE]
            values = kv_ref[pl.ds(first_key, size), v_at : v_at + HEAD_SIZE]
            probs = jnp.exp((dot_nt(keys, rows) + bias) - lse_ref[g])
            d_probs = dot_nt(values, grads)
            d_scores = (probs * (d_probs - dot_rows[g])).astype(BF)
            dkv_ref[pl.ds(first_key, size), v_at : v_at + HEAD_SIZE] = dot_nn(
                probs.astype(BF), grads
            ).astype(BF)
            dkv_ref[pl.ds(first_key, size), k_at : k_at + HEAD_SIZE] = dot_nn(d_scores, rows).astype(BF)
            dq_acc[g] += dot_tn(keys, d_scores)
        return carry

    lax.fori_loop(info_ref[1], info_ref[2], one_block, 0)
    cosine, sine = cos_ref[...], -sin_ref[...]
    for start in range(0, QUERY_HEADS + 1, 2):
        parts = []
        for h in (start, start + 1):
            if h < QUERY_HEADS:
                g, i = h // GROUP, h % GROUP
                parts.append(dq_acc[g, :, i * span : (i + 1) * span] * score_scale)
            else:
                parts.append(jnp.zeros((HEAD_SIZE, span), F32))
        pair = jnp.concatenate(parts, axis=0).T
        dq_ref[:, start * HEAD_SIZE : (start + 2) * HEAD_SIZE] = rotate(pair, cosine, sine).astype(BF)


def attend_back(info, start, q, kv, att, datt, lse, cosine, sine, size):
    span = q.shape[0]
    rows = GROUP * span
    length = kv.shape[0]
    per_head = (KEY_VALUE_HEADS, rows, HEAD_SIZE)
    per_row = (KEY_VALUE_HEADS, 1, rows)
    return pl.pallas_call(
        functools.partial(attend_back_kernel, span, size),
        out_shape=(
            jax.ShapeDtypeStruct((span, q.shape[1]), BF),
            jax.ShapeDtypeStruct(kv.shape, BF),
        ),
        in_specs=[smem_spec()] + [vmem_spec()] * 8,
        out_specs=(vmem_spec(), vmem_spec()),
        scratch_shapes=[
            pltpu.VMEM((KEY_VALUE_HEADS, HEAD_SIZE, rows), F32),
            pltpu.VMEM(per_head, BF),
            pltpu.VMEM(per_head, BF),
            pltpu.VMEM(per_row, F32),
        ],
        compiler_params=params(),
        cost_estimate=cost(
            40 * QUERY_HEADS * HEAD_SIZE * span * length,
            8 * length * KEY_VALUE_HEADS * HEAD_SIZE,
            QUERY_HEADS * span * length,
        ),
    )(info, start, q, kv, att, datt, lse, cosine, sine)


def in_rows(value):
    return with_layout_constraint(value, Layout(tuple(range(value.ndim))))


def after(value, *others):
    return lax.optimization_barrier((value, *others))[0]


def on_device(
    hidden_in,
    positions,
    attn_gain,
    w_query,
    key_projection_weight,
    w_value,
    w_out,
    ffn_gain,
    w_gate,
    w_up,
    w_down,
    out_grad,
):
    nd, nz = lax.axis_size("dp"), lax.axis_size("z")
    nc = 2 * nz
    seqs, span, width = hidden_in.shape
    rows = seqs * span
    length = span * nc
    d, z, c = lax.axis_index("dp"), lax.axis_index("z"), lax.axis_index("core")
    rank = 2 * z + c
    first = c == 0
    block_size = min(512, length)

    def send(value, to):
        pairs = []
        for di in range(nd):
            for zi in range(nz):
                for ci in range(2):
                    target = to(di, zi, ci)
                    if target is not None:
                        dt, zt, ct = target
                        pairs.append((di * nc + zi * 2 + ci, dt * nc + zt * 2 + ct))
        return lax.ppermute(value, ("dp", "z", "core"), pairs)

    def z_shift(value, s):
        return send(value, lambda di, zi, ci: (di, (zi + s) % nz, ci))

    def z_up(value, s):
        return send(value, lambda di, zi, ci: (di, zi + s, ci) if zi + s < nz else None)

    def z_down(value, s):
        return send(value, lambda di, zi, ci: (di, zi - s, ci) if zi >= s else None)

    def dp_xor(value, m):
        return send(value, lambda di, zi, ci: (di ^ m, zi, ci))

    def core_swap(value):
        return send(value, lambda di, zi, ci: (di, zi, 1 - ci))

    def put(buffer, piece, axis, place):
        return lax.dynamic_update_slice_in_dim(buffer, piece, place, axis)

    def take(value, axis, place):
        return lax.dynamic_index_in_dim(value, place, axis, keepdims=False)

    def in_core_order(own, other, axis):
        return jnp.stack([jnp.where(first, own, other), jnp.where(first, other, own)], axis=axis)

    dp_index = jnp.bitwise_xor(d, jnp.arange(nd, dtype=jnp.int32))
    z_index = (z - jnp.arange(nz, dtype=jnp.int32)) % nz

    def pair(left, right):
        return in_rows(jnp.stack([left.T, right.T]))

    dl = w_query.shape[0]
    own_rows = key_projection_weight.shape[1]
    early = 2 * own_rows + 8
    gain_row = jnp.concatenate([attn_gain, ffn_gain])[None]
    gain_row = jnp.pad(gain_row, ((0, 7), (0, dl - gain_row.shape[1])))
    local = [pair(key_projection_weight, w_value).reshape(-1, dl), gain_row, in_rows(w_query.T)]
    kvq_z = lax.all_gather(in_rows(jnp.concatenate(local)), "z")
    kv_own = lax.all_gather(in_rows(kvq_z[:, :early]), "dp")
    q_z = in_rows(kvq_z[:, early:])
    q_own = [q_z] + [dp_xor(after(q_z, kv_own), m) for m in range(1, nd)]
    both = in_core_order(kv_own, core_swap(kv_own), 2)
    kv_weights = both[:, :, :, : 2 * own_rows].reshape(nd, nc, 2, own_rows, dl).swapaxes(1, 2)
    kv_weights = [in_rows(take(kv_weights, 0, d ^ m).reshape(-1, dl)) for m in range(nd)]
    gains = both[0, :, :, 2 * own_rows, : 2 * (width // nc)].reshape(nc, 2, -1).swapaxes(0, 1)
    gains = gains.reshape(2, 1, width).astype(F32)
    gain_attn, gain_ffn = gains[0], gains[1]

    units = w_gate.shape[1]
    down_cut = w_down.reshape(-1, 2, units, w_down.shape[1])
    down_mine, down_away = take(down_cut, 1, c), take(down_cut, 1, 1 - c)
    down_local = in_core_order(down_mine, core_swap(down_away), 2).swapaxes(0, 1).reshape(1, units, dl)
    late_local = jnp.concatenate([pair(w_gate, w_up), down_local]).reshape(-1, dl)
    late_local = in_rows(jnp.concatenate([late_local, in_rows(w_out.T)]))
    late = lax.all_gather(late_local, ("dp", "z", "core")).reshape(nd, nz, 2, -1, dl)

    lane = np.arange(128)
    frequency = jnp.power(theta_base, -jnp.asarray(lane % HALF, F32) * 2.0 / HEAD_SIZE)
    angle = positions.reshape(rows, 1).astype(F32) * frequency[None, :]
    cosine = jnp.cos(angle)
    sine = jnp.sin(angle) * jnp.asarray(np.where(lane % HEAD_SIZE < HALF, -1.0, 1.0), F32)[None, :]

    hidden_rows = hidden_in.reshape(rows, width)
    top_grad = out_grad.reshape(rows, width)
    one_blocks, kv_here = keys_values(hidden_rows, gain_attn, dp_index, kv_weights, cosine, sine)

    first_query = rank * span
    kv_up = []
    for i in range(seqs):
        piece = kv_here[i * span : (i + 1) * span]
        if i:
            piece = after(piece, kv_up[-1][1])
        kv_up.append([piece] + [z_up(piece, s) for s in range(1, nz)])

    q_own = jnp.stack([after(piece, kv_here) for piece in q_own])
    q_weights = in_core_order(q_own, core_swap(q_own), 2).reshape(nd, -1, dl)
    padding = -(QUERY_HEADS * HEAD_SIZE) % 128
    q_weights = [in_rows(jnp.pad(q_weights[m], ((0, padding), (0, 0)))) for m in range(nd)]
    one_blocks = after(one_blocks, kv_up[0][1])
    query = queries(one_blocks, dp_index, q_weights, cosine, sine)
    att_list, lse_list, kv_list, info_list, start_list = [], [], [], [], []
    for i in range(seqs):
        begin = (first_query + jnp.arange(span, dtype=jnp.int32) - positions[i]).reshape(1, span)
        info = jnp.concatenate(
            [
                jnp.stack(
                    [first_query, begin[0, 0] // block_size, (first_query + span - 1) // block_size + 1, c]
                ),
                z_index,
            ]
        ).astype(jnp.int32)
        own = kv_up[i] if i == 0 else [after(piece, att_list[-1]) for piece in kv_up[i]]
        own = jnp.stack(own)
        kv, att, lse = attend(info, begin, query[i * span : (i + 1) * span], own, core_swap(own), block_size)
        att_list.append(att)
        lse_list.append(lse)
        kv_list.append(kv)
        info_list.append(info)
        start_list.append(begin)
    late = after(late, att_list[0])
    o_weights = late[:, :, :, 3 * units :].reshape(nd, width, dl)
    o_weights = [in_rows(take(o_weights, 0, d ^ m)) for m in range(nd)]
    att_blocks, mid, two_blocks = middle(att_list, hidden_rows, gain_ffn, dp_index, o_weights)

    made, dn, ffn_grad, ffn_away = feed_forward(
        c.reshape(1).astype(jnp.int32), two_blocks, top_grad, late, units
    )
    layer_out, grad_mid, grad_att, do, ffn_sum = middle_back(
        mid, top_grad, gain_ffn, dp_index, att_blocks, made, dn, o_weights
    )

    def add(*values):
        total = values[0].astype(F32)
        for value in values[1:]:
            total = total + value.astype(F32)
        return total

    def over_dp(value):
        return add(value[0], *[dp_xor(value[m], m) for m in range(1, nd)])

    def over_z(value, axis):
        return add(take(value, axis, z), *[z_shift(take(value, axis, (z + s) % nz), s) for s in range(1, nz)])

    def rows_of(value, parts):
        cut = value.reshape(nd, parts, nz, 2, -1, value.shape[-1])

        def half(which):
            return take(cut, 3, which).transpose(0, 2, 1, 3, 4).reshape(nd, nz, -1, value.shape[-1])

        return half(c), half(1 - c)

    def finish(value):
        return in_rows(over_z(value.reshape(nz, -1, value.shape[-1]), 0)).T

    ffn_grad = add(ffn_grad, after(core_swap(ffn_away), grad_att)).astype(BF)
    grad_att = after(grad_att, ffn_grad)
    ffn_grad = in_rows(ffn_grad.reshape(nd, -1, ffn_grad.shape[-1]))
    ffn_scattered = in_rows(lax.psum_scatter(ffn_grad, "dp", scatter_dimension=0, tiled=True))
    ffn_grad = over_z(ffn_scattered.reshape(nz, 3, units, -1), 0)
    ffn_grad = in_rows(ffn_grad[:, :, :dl])
    w_gate_grad, w_up_grad = ffn_grad[0].T, ffn_grad[1].T
    down_cut = ffn_grad[2].reshape(units, -1, 2, w_down.shape[1]).swapaxes(0, 1)
    down_from = core_swap(take(down_cut, 2, 1 - c))
    w_down_grad = in_core_order(take(down_cut, 2, c), down_from, 1).reshape(w_down.shape)

    dq_list, dkv_list = [], []
    for i in range(seqs):
        here = slice(i * span, (i + 1) * span)
        grad_here = grad_att[here]
        if i:
            grad_here = after(grad_here, mine)
        dq, dkv = attend_back(
            info_list[i], start_list[i], query[here], kv_list[i], att_list[i], grad_here, lse_list[i],
            cosine[here], sine[here], block_size,
        )
        if i:
            dkv = after(dkv, *dkv_list[-1])
        cut = dkv.reshape(nz, 2, span, dkv.shape[-1])
        mine = add(take(cut, 1, c), core_swap(take(cut, 1, 1 - c))).astype(BF)
        dkv_list.append(
            [take(mine, 0, z)] + [z_down(take(mine, 0, (z - s) % nz), s) for s in range(1, nz)]
        )
        dq_list.append(dq)
    dx_blocks, dq_w = queries_back([after(dq, mine) for dq in dq_list], one_blocks, dp_index, q_weights)
    do_mine, do_other = rows_of(do, 1)
    q_mine, q_other = rows_of(dq_w[:, : QUERY_HEADS * HEAD_SIZE], 1)
    dqo = core_swap(after(jnp.concatenate([q_other, do_other], axis=2), *dkv_list[-1]))
    dqo = add(jnp.concatenate([q_mine, do_mine], axis=2), dqo).astype(BF)
    dqo = finish(over_dp(dqo).astype(BF))
    w_query_grad, w_out_grad = jnp.split(dqo, 2, axis=1)

    input_grad, dkv_w, attn_sum = keys_values_back(
        dkv_list, one_blocks, dx_blocks, grad_mid, hidden_rows, gain_attn, dp_index, kv_weights, cosine, sine
    )
    kv_mine, kv_other = rows_of(dkv_w, 2)
    sums = jnp.concatenate([attn_sum, ffn_sum]).reshape(2, nz, 2, -1).transpose(2, 1, 0, 3).reshape(2, nz, 1, -1)
    sums = jnp.pad(sums, ((0, 0), (0, 0), (0, 7), (0, dl - sums.shape[3]))).astype(BF)

    def with_sums(value, which):
        more = jnp.broadcast_to(take(sums, 0, which)[None], (nd,) + sums.shape[1:])
        return jnp.concatenate([value, more], axis=2)

    dkv_from = after(core_swap(with_sums(kv_other, 1 - c)), ffn_scattered)
    dkv_w = add(with_sums(kv_mine, c), dkv_from).astype(BF)
    dkv_w = in_rows(over_z(over_dp(dkv_w).astype(BF), 0))
    w_key_grad, w_value_grad = dkv_w[:own_rows].T, dkv_w[own_rows : 2 * own_rows].T
    gain_own = dkv_w[2 * own_rows, : 2 * (width // nc)].reshape(2, -1)
    return (
        layer_out.reshape(seqs, span, width),
        input_grad.reshape(seqs, span, width),
        gain_own[0],
        w_query_grad,
        w_key_grad,
        w_value_grad,
        w_out_grad,
        gain_own[1],
        w_gate_grad,
        w_up_grad,
        w_down_grad,
    )


def solution(mesh):
    mesh = jax.sharding.Mesh(
        mesh.devices.reshape(mesh.shape["dp"], mesh.shape["ctx"] // 2, 2), ("dp", "z", "core")
    )
    placed = (
        P("dp", ("z", "core"), None),
        P("dp", ("z", "core")),
        P(("z", "core")),
        P("dp", ("z", "core")),
        P("dp", ("z", "core")),
        P("dp", ("z", "core")),
        P("dp", ("z", "core")),
        P(("z", "core")),
        P("dp", ("z", "core")),
        P("dp", ("z", "core")),
        P("dp", ("z", "core")),
        P("dp", ("z", "core"), None),
    )
    return jax.shard_map(
        on_device,
        mesh=mesh,
        in_specs=placed,
        out_specs=(
            P("dp", ("z", "core"), None),
            P("dp", ("z", "core"), None),
            P(("z", "core")),
            P("dp", ("z", "core")),
            P("dp", ("z", "core")),
            P("dp", ("z", "core")),
            P("dp", ("z", "core")),
            P(("z", "core")),
            P("dp", ("z", "core")),
            P("dp", ("z", "core")),
            P("dp", ("z", "core")),
        ),
        check_vma=False,
    )
```

time: 879 us -> 510 us (0.58)
  local copies, waits for them, and re-layouts: 213 us -> 55.4 us
  starting transfers between devices: 192 us -> 54 us
  other arithmetic: 73.4 us -> 33.5 us
  blocking collectives: 65.2 us -> 29.7 us
  waiting for transfers between devices: 208 us -> 186 us
  between operations: 7.98 us -> 20.6 us
    ppermute x96 -> x41, starting transfers between devices: 192 us -> 53.9 us  [send(): return lax.ppermute(value, ('dp', 'z', 'core'), pairs)]
    psum x1 -> x0, blocking collectives: 65.2 us -> none  [on_device(): gain_sums = lax.psum(jnp.stack([attn_sum, ffn_sum]), ('dp', 'ctx'))]
    ppermute x28 -> x0, local copies, waits for them, and re-layouts: 55 us -> none  [send(): return lax.ppermute(value, ('dp', 'ctx'), pairs)]
    all_gather x0 -> x2, blocking collectives: none -> 29.7 us  [the longest x1 17.7 us: on_device(): kvq_z = lax.all_gather(in_rows(jnp.concatenate(local)), 'z')]
    dynamic_update_slice x33 -> x0, local copies, waits for them, and re-layouts: 23.9 us -> none  [the longest x18 12.7 us: put(): return lax.dynamic_update_slice_in_dim(buffer, piece, place, axis)]
    ppermute x96 -> x41, waiting for transfers between devices: 208 us -> 185 us  [send(): return lax.ppermute(value, ('dp', 'z', 'core'), pairs)]
    reshape x11 -> x3, local copies, waits for them, and re-layouts: 17.5 us -> 0.18 us  [on_device(): jnp.concatenate([attn_sum, ffn_sum]).reshape(2, nz, 2, -1)]
    pallas_call x2 -> x0, local copies, waits for them, and re-layouts: 12.1 us -> none  [feed_forward(): pl.pallas_call(functools.partial(ffn_kernel, nd, nz), grid=(units // chun...]
  transfers between devices with their start and end apart: 96 -> 43, of which waited for: 20 -> 19; matrix products, arithmetic and copies ran while one was open for 27% -> 13% of each run, Pallas kernels for 11% -> 15%
where the time goes in v2:
time: 510 us; the launch traced here: 504 us
  waiting for transfers between devices  186 us (36%)
  Pallas kernels  124 us (24%)
  local copies, waits for them, and re-layouts  55.4 us (11%)
  starting transfers between devices  54 us (11%)
  other arithmetic  33.5 us (7%)
  blocking collectives  29.7 us (6%)
  between operations  20.6 us (4%)
    ppermute x41, waiting for transfers between devices, send(): return lax.ppermute(value, ('dp', 'z', 'core'), pairs)  185 us
    ppermute x41, starting transfers between devices, send(): return lax.ppermute(value, ('dp', 'z', 'core'), pairs)  53.9 us
    pallas_call x6, Pallas kernels, call(): pl.pallas_call(body, out_shape=tuple(outs), in_specs=[smem_spec()] * n_sm...  41.5 us
    pallas_call x1, Pallas kernels, feed_forward(): pl.pallas_call(body, grid_spec=pltpu.PrefetchScalarGridSpec(num_scalar_pr...  40.9 us
    pallas_call x2, Pallas kernels, attend_back(): pl.pallas_call(functools.partial(attend_back_kernel, span, size), out_sha...  23.7 us
    pallas_call x2, Pallas kernels, attend(): pl.pallas_call(functools.partial(attend_kernel, span, size, pieces), out_...  18.4 us
    all_gather x1, blocking collectives, on_device(): kvq_z = lax.all_gather(in_rows(jnp.concatenate(local)), 'z')  17.7 us
    unnamed x79, local copies, waits for them, and re-layouts  17.4 us
  transfers between devices with their start and end apart: 43, of which 19 were waited for; matrix products, arithmetic and copies ran while one was open for 13% of the time, Pallas kernels for 15%

profile of v2, /device:TPU:0, one launch (start us, length us, event | category | flops | bytes accessed | tf_op | source)
XLA Modules:
  0.0 503.9 jit_solution(2484572656439719029)
XLA Ops:
  11.7 17.7 %all-gather = bf16[832,240]{1,0:T(8,128)(2,1)S(1)} all-gather(bf16[208,240]{1,0:T(8,128)(2,1)S(1)} %fusion.20), channel_id=2, replica_groups=mesh['dp'=4,'z'=4,'core'=2] {'z'}, dimensions={0}, use_global_device_ids=true | all-gather | bytes 499200 | tf_op jit(solution)/shard_map/all_gather | solution.py:701
  29.5 11.9 %all-gather.1 = bf16[16,88,240]{2,1,0:T(8,128)(2,1)S(1)} all-gather(bf16[4,88,240]{2,1,0:T(8,128)(2,1)S(1)} %slice.184), channel_id=3, replica_groups=mesh['dp'=4,'z'=4,'core'=2] {'dp'}, dimensions={0}, use_global_device_ids=true | all-gather | bytes 844800 | tf_op jit(solution)/shard_map/all_gather | solution.py:702
  54.1 4.8 shard_map.221
  60.0 3.4 collective-permute-start.1
  63.4 3.2 collective-permute-start.7
  70.8 7.1 %collective-permute-done.1 = bf16[256,640]{1,0:T(8,128)(2,1)S(1)} collective-permute-done((bf16[256,640]{1,0:T(8,128)(2,1)S(1)}, bf16[256,640]{1,0:T(8,128)(2,1)S(1)}, u32[]{:S(2)}, u32[]{:S(2)}) %collective-permute-start.1) | collective-permute-done | bytes 327712 | tf_op jit(solution)/shard_map/ppermute | solution.py:663
  77.9 12.5 %collective-permute-done.7 = bf16[256,640]{1,0:T(8,128)(2,1)S(1)} collective-permute-done((bf16[256,640]{1,0:T(8,128)(2,1)S(1)}, bf16[256,640]{1,0:T(8,128)(2,1)S(1)}, u32[]{:S(2)}, u32[]{:S(2)}) %collective-permute-start.7) | collective-permute-done | bytes 327712 | tf_op jit(solution)/shard_map/ppermute | solution.py:663
  90.4 5.7 %collective-permute-done.6 = bf16[256,640]{1,0:T(8,128)(2,1)S(1)} collective-permute-done((bf16[256,640]{1,0:T(8,128)(2,1)S(1)}, bf16[256,640]{1,0:T(8,128)(2,1)S(1)}, u32[]{:S(2)}, u32[]{:S(2)}) %collective-permute-start.6) | collective-permute-done | bytes 327712 | tf_op jit(solution)/shard_map/ppermute | solution.py:663
  100.3 12.1 %collective-permute-start.11 = (bf16[256,640]{1,0:T(8,128)(2,1)S(1)}, bf16[256,640]{1,0:T(8,128)(2,1)S(1)}, u32[]{:S(2)}, u32[]{:S(2)}) collective-permute-start(bf16[256,640]{1,0:T(8,128)(2,1)S(1)} %get-tuple-element.70), channel_id=1, source_target_pairs={{0,6},{1,7},{8,14},{9,15},{16,22},{17,23},{24,30},{25,31}} | collective-permute-start | bytes 983048 | tf_op jit(solution)/shard_map/ppermute | solution.py:663
  122.0 4.7 shard_map.222
  129.0 9.1 %shard_map.223 = (bf16[2048,640]{1,0:T(8,128)(2,1)}, bf16[256,960]{1,0:T(8,128)(2,1)}, f32[5,1,768]{2,1,0:T(1,128)}) custom-call(s32[8]{0:T(128)} %concatenate.36.info_ref, s32[1,256]{1,0:T(1,128)} %copy-done.27, bf16[256,1024]{1,0:T(8,128)(2,1)} %get-tuple-element.194.q_ref, bf16[4,256,640]{2,1,0:T(8,128)(2,1)} %copy-done.2, ...), custom_call_target="tpu_custom_call" | custom-call | flops 125829120 | bytes 40960 | tf_op jit(solution)/shard_map/pallas_call | solution.py:521
  138.2 3.3 collective-permute-done.10
  141.4 13.8 %collective-permute-done.9 = bf16[256,640]{1,0:T(8,128)(2,1)S(1)} collective-permute-done((bf16[256,640]{1,0:T(8,128)(2,1)S(1)}, bf16[256,640]{1,0:T(8,128)(2,1)S(1)}, u32[]{:S(2)}, u32[]{:S(2)}) %collective-permute-start.9) | collective-permute-done | bytes 327712 | tf_op jit(solution)/shard_map/ppermute | solution.py:663
  163.4 9.3 %shard_map.224 = (bf16[2048,640]{1,0:T(8,128)(2,1)}, bf16[256,960]{1,0:T(8,128)(2,1)}, f32[5,1,768]{2,1,0:T(1,128)}) custom-call(s32[8]{0:T(128)} %concatenate.37.info_ref, s32[1,256]{1,0:T(1,128)} %copy-done.26, bf16[256,1024]{1,0:T(8,128)(2,1)} %get-tuple-element.193.q_ref, bf16[4,256,640]{2,1,0:T(8,128)(2,1)} %copy-done.3, bf16[4,256,640]{2,1,0:T(8,128)(2,1)} %copy-done.9), custom_call_target="tpu_custom_call" | custom-call | flops 125829120 | bytes 40960 | tf_op jit(solution)/shard_map/pallas_call | solution.py:521
  177.2 6.2 %shard_map.225 = (bf16[4,512,240]{2,1,0:T(8,128)(2,1)}, f32[512,960]{1,0:T(8,128)}, bf16[4,512,240]{2,1,0:T(8,128)(2,1)}) custom-call(s32[4]{0:T(128)} %iota_xor_fusion.index_ref, bf16[512,960]{1,0:T(8,128)(2,1)} %bitcast.251, f32[1,960]{1,0:T(1,128)} %squeeze.172.gain_ref, bf16[256,960]{1,0:T(8,128)(2,1)} %get-tuple-element.68.rest_0_.att_ref, ...), custom_call_target="tpu_custom_call" | custom-call | flops 14745600 | bytes 121020 | tf_op jit(solution)/shard_map/pallas_call | solution.py:94
  183.4 40.9 %shard_map.226 = (f32[512,960]{1,0:T(8,128)}, f32[4,512,240]{2,1,0:T(8,128)}, bf16[4,4,3,320,256]{4,3,2,1,0:T(8,128)(2,1)}, bf16[4,4,3,320,256]{4,3,2,1,0:T(8,128)(2,1)}) custom-call(s32[1]{0:T(128)} %bitcast.17.core_ref, bf16[4,512,240]{2,1,0:T(8,128)(2,1)} %get-tuple-element.78.n2_ref, bf16[512,960]{1,0:T(8,128)(2,1)} %bitcast.253, ...), custom_call_target="tpu_custom_call" | custom-call | flops 353894400 | bytes 460800 | tf_op jit(solution)/shard_map/pallas_call | solution.py:425
  224.4 10.5 %shard_map.227 = (bf16[512,960]{1,0:T(8,128)(2,1)}, f32[512,960]{1,0:T(8,128)}, bf16[512,960]{1,0:T(8,128)(2,1)}, bf16[4,960,240]{2,1,0:T(8,128)(2,1)}, f32[1,960]{1,0:T(1,128)}) custom-call(s32[4]{0:T(128)} %iota_xor_fusion.index_ref, f32[512,960]{1,0:T(8,128)} %get-tuple-element.76.mid_ref, bf16[512,960]{1,0:T(8,128)(2,1)} %bitcast.254, ...), custom_call_target="tpu_custom_call" | custom-call | flops 29491200 | bytes 242040 | tf_op jit(solution)/shard_map/pallas_call | solution.py:94
  237.2 12.2 %add_convert_fusion = bf16[4,4,3,320,256]{4,3,2,1,0:T(8,128)(2,1)} fusion(bf16[4,4,3,320,256]{4,3,2,1,0:T(8,128)(2,1)} %collective-permute-done.14, bf16[4,4,3,320,256]{4,3,2,1,0:T(8,128)(2,1)} %get-tuple-element.84), kind=kLoop, calls=%fused_computation | loop fusion | flops 15728640 | bytes 23592960 | tf_op jit(solution)/shard_map/convert_element_type | solution.py:798
  252.2 11.8 %shard_map.228 = (bf16[256,1024]{1,0:T(8,128)(2,1)}, bf16[2048,640]{1,0:T(8,128)(2,1)}) custom-call(s32[8]{0:T(128)} %concatenate.36.info_ref, s32[1,256]{1,0:T(1,128)} %copy-done.27, bf16[256,1024]{1,0:T(8,128)(2,1)} %get-tuple-element.194.q_ref, bf16[2048,640]{1,0:T(8,128)(2,1)} %get-tuple-element.82.kv_ref, ...), custom_call_target="tpu_custom_call" | custom-call | flops 314572800 | bytes 81920 | tf_op jit(solution)/shard_map/pallas_call | solution.py:599
  264.1 2.7 dynamic-slice_bitcast_fusion.1
  266.9 3.2 collective-permute-done.15
  276.6 11.9 %shard_map.229 = (bf16[256,1024]{1,0:T(8,128)(2,1)}, bf16[2048,640]{1,0:T(8,128)(2,1)}) custom-call(s32[8]{0:T(128)} %concatenate.37.info_ref, s32[1,256]{1,0:T(1,128)} %copy-done.26, bf16[256,1024]{1,0:T(8,128)(2,1)} %get-tuple-element.193.q_ref, bf16[2048,640]{1,0:T(8,128)(2,1)} %get-tuple-element.90.kv_ref, ...), custom_call_target="tpu_custom_call" | custom-call | flops 314572800 | bytes 81920 | tf_op jit(solution)/shard_map/pallas_call | solution.py:599
  288.5 23.9 %collective-permute-done.16.rest_1_ = bf16[256,640]{1,0:T(8,128)(2,1)S(1)} collective-permute-done((bf16[256,640]{1,0:T(8,128)(2,1)S(1)}, bf16[256,640]{1,0:T(8,128)(2,1)S(1)}, u32[]{:S(2)}, u32[]{:S(2)}) %collective-permute-start.16) | collective-permute-done | bytes 327712 | tf_op jit(solution)/shard_map/ppermute | solution.py:663
  312.4 32.7 %collective-permute-done.17.rest_2_ = bf16[256,640]{1,0:T(8,128)(2,1)S(1)} collective-permute-done((bf16[256,640]{1,0:T(8,128)(2,1)S(1)}, bf16[256,640]{1,0:T(8,128)(2,1)S(1)}, u32[]{:S(2)}, u32[]{:S(2)}) %collective-permute-start.17) | collective-permute-done | bytes 327712 | tf_op jit(solution)/shard_map/ppermute | solution.py:663
  346.9 3.0 collective-permute-done.19
  355.5 6.6 %shard_map.230 = (f32[4,512,240]{2,1,0:T(8,128)}, bf16[4,1024,240]{2,1,0:T(8,128)(2,1)}) custom-call(s32[4]{0:T(128)} %iota_xor_fusion.index_ref, bf16[4,512,240]{2,1,0:T(8,128)(2,1)} %get-tuple-element.62.blocks_ref, bf16[256,1024]{1,0:T(8,128)(2,1)} %get-tuple-element.96.rest_0_, bf16[256,1024]{1,0:T(8,128)(2,1)} %get-tuple-element.98.rest_1_, ...), custom_call_target="tpu_custom_call" | custom-call | flops 31457280 | bytes 123904 | tf_op jit(solution)/shard_map/pallas_call | solution.py:94
  365.2 16.5 %collective-permute-done.21.rest_6_ = bf16[256,640]{1,0:T(8,128)(2,1)S(1)} collective-permute-done((bf16[256,640]{1,0:T(8,128)(2,1)S(1)}, bf16[256,640]{1,0:T(8,128)(2,1)S(1)}, u32[]{:S(2)}, u32[]{:S(2)}) %collective-permute-start.21) | collective-permute-done | bytes 327712 | tf_op jit(solution)/shard_map/ppermute | solution.py:663
  382.5 8.7 %shard_map.231 = (bf16[512,960]{1,0:T(8,128)(2,1)}, bf16[4,640,240]{2,1,0:T(8,128)(2,1)}, f32[1,960]{1,0:T(1,128)}) custom-call(s32[4]{0:T(128)} %iota_xor_fusion.index_ref, bf16[4,512,240]{2,1,0:T(8,128)(2,1)} %get-tuple-element.62.blocks_ref, f32[4,512,240]{2,1,0:T(8,128)} %get-tuple-element.99.dx_ref, f32[512,960]{1,0:T(8,128)} %get-tuple-element.100.dmid_ref, ...), custom_call_target="tpu_custom_call" | custom-call | flops 19660800 | bytes 195192 | tf_op jit(solution)/shard_map/pallas_call | solution.py:94
  407.0 6.2 %collective-permute-done.33 = bf16[4,240,240]{2,1,0:T(8,128)(2,1)} collective-permute-done((bf16[4,240,240]{2,1,0:T(8,128)(2,1)}, bf16[4,240,240]{2,1,0:T(8,128)(2,1)}, u32[]{:S(2)}, u32[]{:S(2)}) %collective-permute-start.33) | collective-permute-done | bytes 460832 | tf_op jit(solution)/shard_map/ppermute | solution.py:663
  413.2 9.3 %collective-permute-done.32 = bf16[4,240,240]{2,1,0:T(8,128)(2,1)} collective-permute-done((bf16[4,240,240]{2,1,0:T(8,128)(2,1)}, bf16[4,240,240]{2,1,0:T(8,128)(2,1)}, u32[]{:S(2)}, u32[]{:S(2)}) %collective-permute-start.32) | collective-permute-done | bytes 460832 | tf_op jit(solution)/shard_map/ppermute | solution.py:663
  432.5 4.0 collective-permute-done.35
  452.4 37.6 %collective-permute-done.28 = bf16[88,240]{1,0:T(8,128)(2,1)} collective-permute-done((bf16[88,240]{1,0:T(8,128)(2,1)}, bf16[88,240]{1,0:T(8,128)(2,1)}, u32[]{:S(2)}, u32[]{:S(2)}) %collective-permute-start.28) | collective-permute-done | bytes 42272 | tf_op jit(solution)/shard_map/ppermute | solution.py:663
  (247 shorter events, 116.8 us)
Async XLA Ops:
  7.2 167.0 %all-gather.5.cloned.1.call-start = ((), (), s32[]{:S(2)}) async-start(), calls=%async_computation.1 | async-start | bytes 18247680 | tf_op jit(solution)/shard_map/all_gather | solution.py:718
  11.4 415.4 %reduce-scatter.4.cloned.1.call-start = ((), (), s32[]{:S(2)}) async-start(), calls=%async_computation.2 | async-start | bytes 9830400
  41.5 25.1 %collective-permute-start.4 = (bf16[4,120,240]{2,1,0:T(8,128)(2,1)S(1)}, bf16[4,120,240]{2,1,0:T(8,128)(2,1)S(1)}, u32[]{:S(2)}, u32[]{:S(2)}) collective-permute-start(bf16[4,120,240]{2,1,0:T(8,128)(2,1)S(1)} %slice.188), channel_id=1, source_target_pairs={{0,24},{1,25},{2,26},{3,27},{4,28},{5,29},{6,30},{7,31},{8,16},{9,... | collective-permute-start | bytes 691208 | tf_op jit(solution)/shard_map/ppermute | solution.py:663
  43.0 25.5 %collective-permute-start.3 = (bf16[4,120,240]{2,1,0:T(8,128)(2,1)S(1)}, bf16[4,120,240]{2,1,0:T(8,128)(2,1)S(1)}, u32[]{:S(2)}, u32[]{:S(2)}) collective-permute-start(bf16[4,120,240]{2,1,0:T(8,128)(2,1)S(1)} %slice.188), channel_id=1, source_target_pairs={{0,16},{1,17},{2,18},{3,19},{4,20},{5,21},{6,22},{7,23},{8,24},{9,... | collective-permute-start | bytes 691208 | tf_op jit(solution)/shard_map/ppermute | solution.py:663
  44.4 24.1 %collective-permute-start.2 = (bf16[4,120,240]{2,1,0:T(8,128)(2,1)S(1)}, bf16[4,120,240]{2,1,0:T(8,128)(2,1)S(1)}, u32[]{:S(2)}, u32[]{:S(2)}) collective-permute-start(bf16[4,120,240]{2,1,0:T(8,128)(2,1)S(1)} %slice.188), channel_id=1, source_target_pairs={{0,8},{1,9},{2,10},{3,11},{4,12},{5,13},{6,14},{7,15},{8,0},{9,1},... | collective-permute-start | bytes 691208 | tf_op jit(solution)/shard_map/ppermute | solution.py:663
  60.0 17.9 %collective-permute-start.1 = (bf16[256,640]{1,0:T(8,128)(2,1)S(1)}, bf16[256,640]{1,0:T(8,128)(2,1)S(1)}, u32[]{:S(2)}, u32[]{:S(2)}) collective-permute-start(bf16[256,640]{1,0:T(8,128)(2,1)S(1)} %get-tuple-element.203), channel_id=1, source_target_pairs={{0,2},{1,3},{2,4},{3,5},{4,6},{5,7},{8,10},{9,11},{10,12},{11,13},... | collective-permute-start | bytes 983048 | tf_op jit(solution)/shard_map/ppermute | solution.py:663
  63.4 27.0 %collective-permute-start.7 = (bf16[256,640]{1,0:T(8,128)(2,1)S(1)}, bf16[256,640]{1,0:T(8,128)(2,1)S(1)}, u32[]{:S(2)}, u32[]{:S(2)}) collective-permute-start(bf16[256,640]{1,0:T(8,128)(2,1)S(1)} %get-tuple-element.203), channel_id=1, source_target_pairs={{0,6},{1,7},{8,14},{9,15},{16,22},{17,23},{24,30},{25,31}} | collective-permute-start | bytes 983048 | tf_op jit(solution)/shard_map/ppermute | solution.py:663
  66.6 29.5 %collective-permute-start.6 = (bf16[256,640]{1,0:T(8,128)(2,1)S(1)}, bf16[256,640]{1,0:T(8,128)(2,1)S(1)}, u32[]{:S(2)}, u32[]{:S(2)}) collective-permute-start(bf16[256,640]{1,0:T(8,128)(2,1)S(1)} %get-tuple-element.203), channel_id=1, source_target_pairs={{0,4},{1,5},{2,6},{3,7},{8,12},{9,13},{10,14},{11,15},{16,20},{17,... | collective-permute-start | bytes 983048 | tf_op jit(solution)/shard_map/ppermute | solution.py:663
  70.7 45.5 %collective-permute-start.5 = (bf16[4,4,120,240]{3,2,1,0:T(8,128)(2,1)S(1)}, bf16[4,4,120,240]{3,2,1,0:T(8,128)(2,1)}, u32[]{:S(2)}, u32[]{:S(2)}) collective-permute-start(bf16[4,4,120,240]{3,2,1,0:T(8,128)(2,1)S(1)} %pad_maximum_fusion.4), channel_id=1, source_target_pairs={{0,1},{1,0},{2,3},{3,2},{4,5},{5,4},{6,7},{7,6},{8,9},{9,8},{10,11... | collective-permute-start | bytes 2764808 | tf_op jit(solution)/shard_map/ppermute | solution.py:663
  96.3 32.8 %collective-permute-start.8 = (bf16[4,256,640]{2,1,0:T(8,128)(2,1)S(1)}, bf16[4,256,640]{2,1,0:T(8,128)(2,1)}, u32[]{:S(2)}, u32[]{:S(2)}) collective-permute-start(bf16[4,256,640]{2,1,0:T(8,128)(2,1)S(1)} %pad_maximum_fusion.2.own), channel_id=1, source_target_pairs={{0,1},{1,0},{2,3},{3,2},{4,5},{5,4},{6,7},{7,6},{8,9},{9,8},{10,11... | collective-permute-start | bytes 3932168 | tf_op jit(solution)/shard_map/ppermute | solution.py:663
  100.3 37.9 %collective-permute-start.11 = (bf16[256,640]{1,0:T(8,128)(2,1)S(1)}, bf16[256,640]{1,0:T(8,128)(2,1)S(1)}, u32[]{:S(2)}, u32[]{:S(2)}) collective-permute-start(bf16[256,640]{1,0:T(8,128)(2,1)S(1)} %get-tuple-element.70), channel_id=1, source_target_pairs={{0,6},{1,7},{8,14},{9,15},{16,22},{17,23},{24,30},{25,31}} | collective-permute-start | bytes 983048 | tf_op jit(solution)/shard_map/ppermute | solution.py:663
  112.4 29.1 %collective-permute-start.10 = (bf16[256,640]{1,0:T(8,128)(2,1)S(1)}, bf16[256,640]{1,0:T(8,128)(2,1)S(1)}, u32[]{:S(2)}, u32[]{:S(2)}) collective-permute-start(bf16[256,640]{1,0:T(8,128)(2,1)S(1)} %get-tuple-element.70), channel_id=1, source_target_pairs={{0,4},{1,5},{2,6},{3,7},{8,12},{9,13},{10,14},{11,15},{16,20},{17,... | collective-permute-start | bytes 983048 | tf_op jit(solution)/shard_map/ppermute | solution.py:663
  113.7 41.6 %collective-permute-start.9 = (bf16[256,640]{1,0:T(8,128)(2,1)S(1)}, bf16[256,640]{1,0:T(8,128)(2,1)S(1)}, u32[]{:S(2)}, u32[]{:S(2)}) collective-permute-start(bf16[256,640]{1,0:T(8,128)(2,1)S(1)} %get-tuple-element.70), channel_id=1, source_target_pairs={{0,2},{1,3},{2,4},{3,5},{4,6},{5,7},{8,10},{9,11},{10,12},{11,13},... | collective-permute-start | bytes 983048 | tf_op jit(solution)/shard_map/ppermute | solution.py:663
  224.3 12.8 %collective-permute-start.14 = (bf16[4,4,3,320,256]{4,3,2,1,0:T(8,128)(2,1)}, bf16[4,4,3,320,256]{4,3,2,1,0:T(8,128)(2,1)}, u32[]{:S(2)}, u32[]{:S(2)}) collective-permute-start(bf16[4,4,3,320,256]{4,3,2,1,0:T(8,128)(2,1)} %get-tuple-element.85), channel_id=1, source_target_pairs={{0,1},{1,0},{2,3},{3,2},{4,5},{5,4},{6,7},{7,6},{8,9},{9,8},{10,11... | collective-permute-start | bytes 23592968 | tf_op jit(solution)/shard_map/ppermute | solution.py:663
  272.7 39.7 %collective-permute-start.16 = (bf16[256,640]{1,0:T(8,128)(2,1)S(1)}, bf16[256,640]{1,0:T(8,128)(2,1)S(1)}, u32[]{:S(2)}, u32[]{:S(2)}) collective-permute-start(bf16[256,640]{1,0:T(8,128)(2,1)S(1)} %get-tuple-element.185), channel_id=1, source_target_pairs={{2,0},{3,1},{4,2},{5,3},{6,4},{7,5},{10,8},{11,9},{12,10},{13,11},... | collective-permute-start | bytes 983048 | tf_op jit(solution)/shard_map/ppermute | solution.py:663
  274.0 71.2 %collective-permute-start.17 = (bf16[256,640]{1,0:T(8,128)(2,1)S(1)}, bf16[256,640]{1,0:T(8,128)(2,1)S(1)}, u32[]{:S(2)}, u32[]{:S(2)}) collective-permute-start(bf16[256,640]{1,0:T(8,128)(2,1)S(1)} %get-tuple-element.184), channel_id=1, source_target_pairs={{4,0},{5,1},{6,2},{7,3},{12,8},{13,9},{14,10},{15,11},{20,16},{21,... | collective-permute-start | bytes 983048 | tf_op jit(solution)/shard_map/ppermute | solution.py:663
  275.3 69.9 %collective-permute-start.18 = (bf16[256,640]{1,0:T(8,128)(2,1)S(1)}, bf16[256,640]{1,0:T(8,128)(2,1)S(1)}, u32[]{:S(2)}, u32[]{:S(2)}) collective-permute-start(bf16[256,640]{1,0:T(8,128)(2,1)S(1)} %get-tuple-element.183), channel_id=1, source_target_pairs={{6,0},{7,1},{14,8},{15,9},{22,16},{23,17},{30,24},{31,25}} | collective-permute-start | bytes 983048 | tf_op jit(solution)/shard_map/ppermute | solution.py:663
  351.2 14.0 %collective-permute-start.20 = (bf16[256,640]{1,0:T(8,128)(2,1)S(1)}, bf16[256,640]{1,0:T(8,128)(2,1)S(1)}, u32[]{:S(2)}, u32[]{:S(2)}) collective-permute-start(bf16[256,640]{1,0:T(8,128)(2,1)S(1)} %get-tuple-element.181), channel_id=1, source_target_pairs={{2,0},{3,1},{4,2},{5,3},{6,4},{7,5},{10,8},{11,9},{12,10},{13,11},... | collective-permute-start | bytes 983048 | tf_op jit(solution)/shard_map/ppermute | solution.py:663
  352.5 29.2 %collective-permute-start.21 = (bf16[256,640]{1,0:T(8,128)(2,1)S(1)}, bf16[256,640]{1,0:T(8,128)(2,1)S(1)}, u32[]{:S(2)}, u32[]{:S(2)}) collective-permute-start(bf16[256,640]{1,0:T(8,128)(2,1)S(1)} %get-tuple-element.180), channel_id=1, source_target_pairs={{4,0},{5,1},{6,2},{7,3},{12,8},{13,9},{14,10},{15,11},{20,16},{21,... | collective-permute-start | bytes 983048 | tf_op jit(solution)/shard_map/ppermute | solution.py:663
  353.8 27.9 %collective-permute-start.22 = (bf16[256,640]{1,0:T(8,128)(2,1)S(1)}, bf16[256,640]{1,0:T(8,128)(2,1)S(1)}, u32[]{:S(2)}, u32[]{:S(2)}) collective-permute-start(bf16[256,640]{1,0:T(8,128)(2,1)S(1)} %get-tuple-element.179), channel_id=1, source_target_pairs={{6,0},{7,1},{14,8},{15,9},{22,16},{23,17},{30,24},{31,25}} | collective-permute-start | bytes 983048 | tf_op jit(solution)/shard_map/ppermute | solution.py:663
  381.7 12.6 %collective-permute-start.30 = (bf16[4,4,240,240]{3,2,1,0:T(8,128)(2,1)S(1)}, bf16[4,4,240,240]{3,2,1,0:T(8,128)(2,1)}, u32[]{:S(2)}, u32[]{:S(2)}) collective-permute-start(bf16[4,4,240,240]{3,2,1,0:T(8,128)(2,1)S(1)} %pad_maximum_fusion), channel_id=1, source_target_pairs={{0,1},{1,0},{2,3},{3,2},{4,5},{5,4},{6,7},{7,6},{8,9},{9,8},{10,11... | collective-permute-start | bytes 5529608 | tf_op jit(solution)/shard_map/ppermute | solution.py:663
  397.8 15.4 %collective-permute-start.33 = (bf16[4,240,240]{2,1,0:T(8,128)(2,1)}, bf16[4,240,240]{2,1,0:T(8,128)(2,1)}, u32[]{:S(2)}, u32[]{:S(2)}) collective-permute-start(bf16[4,240,240]{2,1,0:T(8,128)(2,1)} %get-tuple-element.159), channel_id=1, source_target_pairs={{0,24},{1,25},{2,26},{3,27},{4,28},{5,29},{6,30},{7,31},{8,16},{9,... | collective-permute-start | bytes 1382408 | tf_op jit(solution)/shard_map/ppermute | solution.py:663
  399.4 23.1 %collective-permute-start.32 = (bf16[4,240,240]{2,1,0:T(8,128)(2,1)}, bf16[4,240,240]{2,1,0:T(8,128)(2,1)}, u32[]{:S(2)}, u32[]{:S(2)}) collective-permute-start(bf16[4,240,240]{2,1,0:T(8,128)(2,1)} %get-tuple-element.160), channel_id=1, source_target_pairs={{0,16},{1,17},{2,18},{3,19},{4,20},{5,21},{6,22},{7,23},{8,24},{9,... | collective-permute-start | bytes 1382408 | tf_op jit(solution)/shard_map/ppermute | solution.py:663
  400.5 22.0 %collective-permute-start.31 = (bf16[4,240,240]{2,1,0:T(8,128)(2,1)}, bf16[4,240,240]{2,1,0:T(8,128)(2,1)}, u32[]{:S(2)}, u32[]{:S(2)}) collective-permute-start(bf16[4,240,240]{2,1,0:T(8,128)(2,1)} %get-tuple-element.158), channel_id=1, source_target_pairs={{0,8},{1,9},{2,10},{3,11},{4,12},{5,13},{6,14},{7,15},{8,0},{9,1},... | collective-permute-start | bytes 1382408 | tf_op jit(solution)/shard_map/ppermute | solution.py:663
  402.4 24.4 %collective-permute-start.23 = (bf16[4,4,88,240]{3,2,1,0:T(8,128)(2,1)}, bf16[4,4,88,240]{3,2,1,0:T(8,128)(2,1)}, u32[]{:S(2)}, u32[]{:S(2)}) collective-permute-start(bf16[4,4,88,240]{3,2,1,0:T(8,128)(2,1)} %pad_maximum_fusion.5), channel_id=1, source_target_pairs={{0,1},{1,0},{2,3},{3,2},{4,5},{5,4},{6,7},{7,6},{8,9},{9,8},{10,11... | collective-permute-start | bytes 2027528 | tf_op jit(solution)/shard_map/ppermute | solution.py:663
  424.8 11.7 %collective-permute-start.35 = (bf16[240,240]{1,0:T(8,128)(2,1)}, bf16[240,240]{1,0:T(8,128)(2,1)S(1)}, u32[]{:S(2)}, u32[]{:S(2)}) collective-permute-start(bf16[240,240]{1,0:T(8,128)(2,1)} %get-tuple-element.206), channel_id=1, source_target_pairs={{0,4},{1,5},{2,6},{3,7},{4,0},{5,1},{6,2},{7,3},{8,12},{9,13},{10,... | collective-permute-start | bytes 345608 | tf_op jit(solution)/shard_map/ppermute | solution.py:663
  424.8 11.7 %collective-permute-start.34 = (bf16[240,240]{1,0:T(8,128)(2,1)S(1)}, bf16[240,240]{1,0:T(8,128)(2,1)}, u32[]{:S(2)}, u32[]{:S(2)}) collective-permute-start(bf16[240,240]{1,0:T(8,128)(2,1)S(1)} %get-tuple-element.204), channel_id=1, source_target_pairs={{0,2},{1,3},{2,4},{3,5},{4,6},{5,7},{6,0},{7,1},{8,10},{9,11},{10,... | collective-permute-start | bytes 345608 | tf_op jit(solution)/shard_map/ppermute | solution.py:663
  443.2 48.3 %collective-permute-start.39 = (bf16[3,320,256]{2,1,0:T(8,128)(2,1)}, bf16[3,320,256]{2,1,0:T(8,128)(2,1)S(1)}, u32[]{:S(2)}, u32[]{:S(2)}) collective-permute-start(bf16[3,320,256]{2,1,0:T(8,128)(2,1)} %get-tuple-element.156), channel_id=1, source_target_pairs={{0,6},{1,7},{2,0},{3,1},{4,2},{5,3},{6,4},{7,5},{8,14},{9,15},{10,... | collective-permute-start | bytes 1474568 | tf_op jit(solution)/shard_map/ppermute | solution.py:663
  445.0 46.5 %collective-permute-start.38 = (bf16[3,320,256]{2,1,0:T(8,128)(2,1)}, bf16[3,320,256]{2,1,0:T(8,128)(2,1)S(1)}, u32[]{:S(2)}, u32[]{:S(2)}) collective-permute-start(bf16[3,320,256]{2,1,0:T(8,128)(2,1)} %get-tuple-element.157), channel_id=1, source_target_pairs={{0,4},{1,5},{2,6},{3,7},{4,0},{5,1},{6,2},{7,3},{8,12},{9,13},{10,... | collective-permute-start | bytes 1474568 | tf_op jit(solution)/shard_map/ppermute | solution.py:663
  445.0 46.5 %collective-permute-start.37 = (bf16[3,320,256]{2,1,0:T(8,128)(2,1)}, bf16[3,320,256]{2,1,0:T(8,128)(2,1)}, u32[]{:S(2)}, u32[]{:S(2)}) collective-permute-start(bf16[3,320,256]{2,1,0:T(8,128)(2,1)} %get-tuple-element.155), channel_id=1, source_target_pairs={{0,2},{1,3},{2,4},{3,5},{4,6},{5,7},{6,0},{7,1},{8,10},{9,11},{10,... | collective-permute-start | bytes 1474568 | tf_op jit(solution)/shard_map/ppermute | solution.py:663
  445.8 44.2 %collective-permute-start.28 = (bf16[88,240]{1,0:T(8,128)(2,1)}, bf16[88,240]{1,0:T(8,128)(2,1)}, u32[]{:S(2)}, u32[]{:S(2)}) collective-permute-start(bf16[88,240]{1,0:T(8,128)(2,1)} %get-tuple-element.221), channel_id=1, source_target_pairs={{0,4},{1,5},{2,6},{3,7},{4,0},{5,1},{6,2},{7,3},{8,12},{9,13},{10,... | collective-permute-start | bytes 126728 | tf_op jit(solution)/shard_map/ppermute | solution.py:663
  448.2 41.8 %collective-permute-start.27 = (bf16[88,240]{1,0:T(8,128)(2,1)}, bf16[88,240]{1,0:T(8,128)(2,1)}, u32[]{:S(2)}, u32[]{:S(2)}) collective-permute-start(bf16[88,240]{1,0:T(8,128)(2,1)} %get-tuple-element.219), channel_id=1, source_target_pairs={{0,2},{1,3},{2,4},{3,5},{4,6},{5,7},{6,0},{7,1},{8,10},{9,11},{10,... | collective-permute-start | bytes 126728 | tf_op jit(solution)/shard_map/ppermute | solution.py:663
  (45 other events, 457.2 us)
Sparse Core Ops, SparseCore 0:
  11.6 162.5 all-gather.4
  249.5 111.0 reduce-scatter.3

commit v3 on v2

--- a/solution.py
+++ b/solution.py
@@ -219,10 +219,11 @@
             low_ref[here, :] = dmid.astype(BF)
         sum_ref[...] = sums
         for m in range(nd):
-            place = index_ref[m]
-            block_ref[place] = dot_nn(low_ref[...], w[m][...])
-            for cols in column_chunks(width):
-                dw_ref[m, cols, :] = dot_tn(low_ref[:, cols], att_ref[place]).astype(BF)
+            block_ref[index_ref[m]] = dot_nn(low_ref[...], w[m][...])
+        for cols in column_chunks(width):
+            turned = low_ref[:, cols].T
+            for m in range(nd):
+                dw_ref[m, cols, :] = dot_nn(turned, att_ref[index_ref[m]]).astype(BF)
         for b in range(nd):
             datt_ref[:, b * depth : (b + 1) * depth] = block_ref[b].astype(BF)
 
@@ -254,10 +255,11 @@
         for p in range(parts):
             all_ref[p * span : (p + 1) * span, :] = dq[p][...]
         for m in range(nd):
-            place = index_ref[m]
-            dx_ref[place] = dot_nn(all_ref[...], w[m][...])
-            for cols in column_chunks(columns):
-                dw_ref[m, cols, :] = dot_tn(all_ref[:, cols], blocks_ref[place]).astype(BF)
+            dx_ref[index_ref[m]] = dot_nn(all_ref[...], w[m][...])
+        for cols in column_chunks(columns):
+            turned = all_ref[:, cols].T
+            for m in range(nd):
+                dw_ref[m, cols, :] = dot_nn(turned, blocks_ref[index_ref[m]]).astype(BF)
 
     return call(
         body,
@@ -295,8 +297,10 @@
         for m in range(nd):
             place = index_ref[m]
             block_ref[place] = dx_ref[place] + dot_nn(low_ref[...], w[m][...])
-            for cols in column_chunks(columns):
-                dw_ref[m, cols, :] = dot_tn(low_ref[:, cols], blocks_ref[place]).astype(BF)
+        for cols in column_chunks(columns):
+            turned = low_ref[:, cols].T
+            for m in range(nd):
+                dw_ref[m, cols, :] = dot_nn(turned, blocks_ref[index_ref[m]]).astype(BF)
         sums = jnp.zeros((1, width), F32)
         for here in row_chunks(rows):
             x = hidden_ref[here, :].astype(F32)
@@ -386,17 +390,18 @@
             for copy in copies(step - 1):
                 copy.wait()
 
+        hidden_t, d_gate_t, d_up_t = hidden.T, d_gate.T, d_up.T
         for b in range(nz):
             outs[b] += dot_nn(hidden, w_down[b])
-            grad = dot_tn(hidden, tops[b]).astype(BF)
+            grad = dot_nn(hidden_t, tops[b]).astype(BF)
             for h in range(2):
                 for s in range(sub):
                     start = h * half + s * part
                     dd[h, b, 0, :, s * z_depth : (s + 1) * z_depth] = grad[start : start + part]
         for b in range(nd):
             dn_ref[b] += dot_nn(d_gate, w_gu[b, 0]) + dot_nn(d_up, w_gu[b, 1])
-            for which, value in ((0, d_gate), (1, d_up)):
-                grad = dot_tn(value, n2_ref[b]).astype(BF)
+            for which, value in ((0, d_gate_t), (1, d_up_t)):
+                grad = dot_nn(value, n2_ref[b]).astype(BF)
                 for h in range(2):
                     dgu[h, b, :, which, :, :depth] = grad[h * half : (h + 1) * half].reshape(sub, part, depth)
         for copy in copies(step):
@@ -752,7 +757,7 @@
                 z_index,
             ]
         ).astype(jnp.int32)
-        own = kv_up[i] if i == 0 else [after(piece, att_list[-1]) for piece in kv_up[i]]
+        own = [after(piece, att_list[-1]) for piece in kv_up[i]] if i else kv_up[i]
         own = jnp.stack(own)
         kv, att, lse = attend(info, begin, query[i * span : (i + 1) * span], own, core_swap(own), block_size)
         att_list.append(att)
@@ -781,8 +786,11 @@
     def over_dp(value):
         return add(value[0], *[dp_xor(value[m], m) for m in range(1, nd)])
 
-    def over_z(value, axis):
-        return add(take(value, axis, z), *[z_shift(take(value, axis, (z + s) % nz), s) for s in range(1, nz)])
+    def z_pieces(value):
+        return [take(value, 0, z)] + [z_shift(take(value, 0, (z + s) % nz), s) for s in range(1, nz)]
+
+    def over_z(value):
+        return add(*z_pieces(value))
 
     def rows_of(value, parts):
         cut = value.reshape(nd, parts, nz, 2, -1, value.shape[-1])
@@ -793,19 +801,12 @@
         return half(c), half(1 - c)
 
     def finish(value):
-        return in_rows(over_z(value.reshape(nz, -1, value.shape[-1]), 0)).T
+        return in_rows(over_z(value.reshape(nz, -1, value.shape[-1]))).T
 
     ffn_grad = add(ffn_grad, after(core_swap(ffn_away), grad_att)).astype(BF)
     grad_att = after(grad_att, ffn_grad)
     ffn_grad = in_rows(ffn_grad.reshape(nd, -1, ffn_grad.shape[-1]))
     ffn_scattered = in_rows(lax.psum_scatter(ffn_grad, "dp", scatter_dimension=0, tiled=True))
-    ffn_grad = over_z(ffn_scattered.reshape(nz, 3, units, -1), 0)
-    ffn_grad = in_rows(ffn_grad[:, :, :dl])
-    w_gate_grad, w_up_grad = ffn_grad[0].T, ffn_grad[1].T
-    down_cut = ffn_grad[2].reshape(units, -1, 2, w_down.shape[1]).swapaxes(0, 1)
-    down_from = core_swap(take(down_cut, 2, 1 - c))
-    w_down_grad = in_core_order(take(down_cut, 2, c), down_from, 1).reshape(w_down.shape)
-
     dq_list, dkv_list = [], []
     for i in range(seqs):
         here = slice(i * span, (i + 1) * span)
@@ -829,12 +830,15 @@
     q_mine, q_other = rows_of(dq_w[:, : QUERY_HEADS * HEAD_SIZE], 1)
     dqo = core_swap(after(jnp.concatenate([q_other, do_other], axis=2), *dkv_list[-1]))
     dqo = add(jnp.concatenate([q_mine, do_mine], axis=2), dqo).astype(BF)
-    dqo = finish(over_dp(dqo).astype(BF))
+    dx_blocks = after(dx_blocks, ffn_scattered)
+    ffn_pieces = z_pieces(ffn_scattered.reshape(nz, 3, units, -1))
+    dqo = finish(after(over_dp(dqo).astype(BF), ffn_pieces[2]))
     w_query_grad, w_out_grad = jnp.split(dqo, 2, axis=1)
 
     input_grad, dkv_w, attn_sum = keys_values_back(
         dkv_list, one_blocks, dx_blocks, grad_mid, hidden_rows, gain_attn, dp_index, kv_weights, cosine, sine
     )
+    dkv_w = after(dkv_w, ffn_pieces[1], ffn_pieces[-1])
     kv_mine, kv_other = rows_of(dkv_w, 2)
     sums = jnp.concatenate([attn_sum, ffn_sum]).reshape(2, nz, 2, -1).transpose(2, 1, 0, 3).reshape(2, nz, 1, -1)
     sums = jnp.pad(sums, ((0, 0), (0, 0), (0, 7), (0, dl - sums.shape[3]))).astype(BF)
@@ -843,11 +847,17 @@
         more = jnp.broadcast_to(take(sums, 0, which)[None], (nd,) + sums.shape[1:])
         return jnp.concatenate([value, more], axis=2)
 
-    dkv_from = after(core_swap(with_sums(kv_other, 1 - c)), ffn_scattered)
+    dkv_from = core_swap(with_sums(kv_other, 1 - c))
     dkv_w = add(with_sums(kv_mine, c), dkv_from).astype(BF)
-    dkv_w = in_rows(over_z(over_dp(dkv_w).astype(BF), 0))
+    dkv_w = in_rows(over_z(over_dp(dkv_w).astype(BF)))
     w_key_grad, w_value_grad = dkv_w[:own_rows].T, dkv_w[own_rows : 2 * own_rows].T
     gain_own = dkv_w[2 * own_rows, : 2 * (width // nc)].reshape(2, -1)
+    ffn_grad = in_rows(add(*ffn_pieces)[:, :, :dl])
+    w_gate_grad, w_up_grad = ffn_grad[0].T, ffn_grad[1].T
+    down_cut = ffn_grad[2].reshape(units, -1, 2, w_down.shape[1]).swapaxes(0, 1)
+    down_from = core_swap(take(down_cut, 2, 1 - c))
+    w_down_grad = in_core_order(take(down_cut, 2, c), down_from, 1).reshape(w_down.shape)
+
     return (
         layer_out.reshape(seqs, span, width),
         input_grad.reshape(seqs, span, width),

time: 510 us -> 490 us (0.961)
  waiting for transfers between devices: 186 us -> 166 us
  starting transfers between devices: 54 us -> 59.2 us
    ppermute x41, waiting for transfers between devices: 185 us -> 164 us  [send(): return lax.ppermute(value, ('dp', 'z', 'core'), pairs)]
    ppermute x41, starting transfers between devices: 53.9 us -> 59.1 us  [send(): return lax.ppermute(value, ('dp', 'z', 'core'), pairs)]
    unnamed x79 -> x81, local copies, waits for them, and re-layouts: 17.4 us -> 16.5 us
  transfers between devices with their start and end apart: 43 -> 43, of which waited for: 19 -> 24; matrix products, arithmetic and copies ran while one was open for 13% -> 13% of each run, Pallas kernels for 15% -> 16%
where the time goes in v3:
time: 490 us; the launch traced here: 482 us
  waiting for transfers between devices  166 us (34%)
  Pallas kernels  122 us (25%)
  starting transfers between devices  59.2 us (12%)
  local copies, waits for them, and re-layouts  54.5 us (11%)
  other arithmetic  29.9 us (6%)
  blocking collectives  29.7 us (6%)
  between operations  20.6 us (4%)
    ppermute x41, waiting for transfers between devices, send(): return lax.ppermute(value, ('dp', 'z', 'core'), pairs)  164 us
    ppermute x41, starting transfers between devices, send(): return lax.ppermute(value, ('dp', 'z', 'core'), pairs)  59.1 us
    pallas_call x1, Pallas kernels, feed_forward(): pl.pallas_call(body, grid_spec=pltpu.PrefetchScalarGridSpec(num_scalar_pr...  40.8 us
    pallas_call x6, Pallas kernels, call(): pl.pallas_call(body, out_shape=tuple(outs), in_specs=[smem_spec()] * n_sm...  39.2 us
    pallas_call x2, Pallas kernels, attend_back(): pl.pallas_call(functools.partial(attend_back_kernel, span, size), out_sha...  23.7 us
    pallas_call x2, Pallas kernels, attend(): pl.pallas_call(functools.partial(attend_kernel, span, size, pieces), out_...  18.4 us
    all_gather x1, blocking collectives, on_device(): kvq_z = lax.all_gather(in_rows(jnp.concatenate(local)), 'z')  17.7 us
    unnamed x81, local copies, waits for them, and re-layouts  16.5 us
  transfers between devices with their start and end apart: 43, of which 24 were waited for; matrix products, arithmetic and copies ran while one was open for 13% of the time, Pallas kernels for 16%

profile of v3, /device:TPU:0, one launch (start us, length us, event | category | flops | bytes accessed | tf_op | source)
XLA Modules:
  0.0 481.6 jit_solution(1580077824416327165)
XLA Ops:
  11.7 17.7 %all-gather = bf16[832,240]{1,0:T(8,128)(2,1)S(1)} all-gather(bf16[208,240]{1,0:T(8,128)(2,1)S(1)} %fusion.20), channel_id=2, replica_groups=mesh['dp'=4,'z'=4,'core'=2] {'z'}, dimensions={0}, use_global_device_ids=true | all-gather | bytes 499200 | tf_op jit(solution)/shard_map/all_gather | solution.py:706
  29.5 11.9 %all-gather.1 = bf16[16,88,240]{2,1,0:T(8,128)(2,1)S(1)} all-gather(bf16[4,88,240]{2,1,0:T(8,128)(2,1)S(1)} %slice.184), channel_id=3, replica_groups=mesh['dp'=4,'z'=4,'core'=2] {'dp'}, dimensions={0}, use_global_device_ids=true | all-gather | bytes 844800 | tf_op jit(solution)/shard_map/all_gather | solution.py:707
  54.1 4.8 shard_map.221
  60.0 3.4 collective-permute-start.1
  70.7 7.2 %collective-permute-done.1 = bf16[256,640]{1,0:T(8,128)(2,1)S(1)} collective-permute-done((bf16[256,640]{1,0:T(8,128)(2,1)S(1)}, bf16[256,640]{1,0:T(8,128)(2,1)S(1)}, u32[]{:S(2)}, u32[]{:S(2)}) %collective-permute-start.1) | collective-permute-done | bytes 327712 | tf_op jit(solution)/shard_map/ppermute | solution.py:668
  77.9 12.5 %collective-permute-done.7 = bf16[256,640]{1,0:T(8,128)(2,1)S(1)} collective-permute-done((bf16[256,640]{1,0:T(8,128)(2,1)S(1)}, bf16[256,640]{1,0:T(8,128)(2,1)S(1)}, u32[]{:S(2)}, u32[]{:S(2)}) %collective-permute-start.7) | collective-permute-done | bytes 327712 | tf_op jit(solution)/shard_map/ppermute | solution.py:668
  90.4 5.7 %collective-permute-done.6 = bf16[256,640]{1,0:T(8,128)(2,1)S(1)} collective-permute-done((bf16[256,640]{1,0:T(8,128)(2,1)S(1)}, bf16[256,640]{1,0:T(8,128)(2,1)S(1)}, u32[]{:S(2)}, u32[]{:S(2)}) %collective-permute-start.6) | collective-permute-done | bytes 327712 | tf_op jit(solution)/shard_map/ppermute | solution.py:668
  100.4 12.1 %collective-permute-start.11 = (bf16[256,640]{1,0:T(8,128)(2,1)S(1)}, bf16[256,640]{1,0:T(8,128)(2,1)S(1)}, u32[]{:S(2)}, u32[]{:S(2)}) collective-permute-start(bf16[256,640]{1,0:T(8,128)(2,1)S(1)} %get-tuple-element.72), channel_id=1, source_target_pairs={{0,6},{1,7},{8,14},{9,15},{16,22},{17,23},{24,30},{25,31}} | collective-permute-start | bytes 983048 | tf_op jit(solution)/shard_map/ppermute | solution.py:668
  122.0 4.7 shard_map.222
  130.1 9.1 %shard_map.223 = (bf16[2048,640]{1,0:T(8,128)(2,1)}, bf16[256,960]{1,0:T(8,128)(2,1)}, f32[5,1,768]{2,1,0:T(1,128)}) custom-call(s32[8]{0:T(128)} %concatenate.36.info_ref, s32[1,256]{1,0:T(1,128)} %copy-done.27, bf16[256,1024]{1,0:T(8,128)(2,1)} %get-tuple-element.198.q_ref, bf16[4,256,640]{2,1,0:T(8,128)(2,1)} %copy-done.2, bf16[4,256,640]{2,1,0:T(8,128)(2,1)} %copy-done.7), custom_call_target="tpu_custom_call" | custom-call | flops 125829120 | bytes 40960 | tf_op jit(solution)/shard_map/pallas_call | solution.py:526
  141.5 13.8 %collective-permute-done.9 = bf16[256,640]{1,0:T(8,128)(2,1)S(1)} collective-permute-done((bf16[256,640]{1,0:T(8,128)(2,1)S(1)}, bf16[256,640]{1,0:T(8,128)(2,1)S(1)}, u32[]{:S(2)}, u32[]{:S(2)}) %collective-permute-start.9) | collective-permute-done | bytes 327712 | tf_op jit(solution)/shard_map/ppermute | solution.py:668
  163.6 9.3 %shard_map.224 = (bf16[2048,640]{1,0:T(8,128)(2,1)}, bf16[256,960]{1,0:T(8,128)(2,1)}, f32[5,1,768]{2,1,0:T(1,128)}) custom-call(s32[8]{0:T(128)} %concatenate.37.info_ref, s32[1,256]{1,0:T(1,128)} %copy-done.26, bf16[256,1024]{1,0:T(8,128)(2,1)} %get-tuple-element.197.q_ref, bf16[4,256,640]{2,1,0:T(8,128)(2,1)} %copy-done.3, bf16[4,256,640]{2,1,0:T(8,128)(2,1)} %copy-done.8), custom_call_target="tpu_custom_call" | custom-call | flops 125829120 | bytes 40960 | tf_op jit(solution)/shard_map/pallas_call | solution.py:526
  177.2 6.2 %shard_map.225 = (bf16[4,512,240]{2,1,0:T(8,128)(2,1)}, f32[512,960]{1,0:T(8,128)}, bf16[4,512,240]{2,1,0:T(8,128)(2,1)}) custom-call(s32[4]{0:T(128)} %iota_xor_fusion.index_ref, bf16[512,960]{1,0:T(8,128)(2,1)} %bitcast.251, f32[1,960]{1,0:T(1,128)} %squeeze.172.gain_ref, bf16[256,960]{1,0:T(8,128)(2,1)} %get-tuple-element.70.rest_0_.att_ref, ...), custom_call_target="tpu_custom_call" | custom-call | flops 14745600 | bytes 121020 | tf_op jit(solution)/shard_map/pallas_call | solution.py:94
  183.4 40.8 %shard_map.226 = (f32[512,960]{1,0:T(8,128)}, f32[4,512,240]{2,1,0:T(8,128)}, bf16[4,4,3,320,256]{4,3,2,1,0:T(8,128)(2,1)}, bf16[4,4,3,320,256]{4,3,2,1,0:T(8,128)(2,1)}) custom-call(s32[1]{0:T(128)} %bitcast.17.core_ref, bf16[4,512,240]{2,1,0:T(8,128)(2,1)} %get-tuple-element.80.n2_ref, bf16[512,960]{1,0:T(8,128)(2,1)} %bitcast.253, ...), custom_call_target="tpu_custom_call" | custom-call | flops 353894400 | bytes 460800 | tf_op jit(solution)/shard_map/pallas_call | solution.py:430
  224.4 9.4 %shard_map.227 = (bf16[512,960]{1,0:T(8,128)(2,1)}, f32[512,960]{1,0:T(8,128)}, bf16[512,960]{1,0:T(8,128)(2,1)}, bf16[4,960,240]{2,1,0:T(8,128)(2,1)}, f32[1,960]{1,0:T(1,128)}) custom-call(s32[4]{0:T(128)} %iota_xor_fusion.index_ref, f32[512,960]{1,0:T(8,128)} %get-tuple-element.78.mid_ref, bf16[512,960]{1,0:T(8,128)(2,1)} %bitcast.254, ...), custom_call_target="tpu_custom_call" | custom-call | flops 29491200 | bytes 242040 | tf_op jit(solution)/shard_map/pallas_call | solution.py:94
  233.7 3.3 collective-permute-done.14
  237.1 12.1 %add_convert_fusion = bf16[4,4,3,320,256]{4,3,2,1,0:T(8,128)(2,1)} fusion(bf16[4,4,3,320,256]{4,3,2,1,0:T(8,128)(2,1)} %collective-permute-done.14, bf16[4,4,3,320,256]{4,3,2,1,0:T(8,128)(2,1)} %get-tuple-element.86), kind=kLoop, calls=%fused_computation | loop fusion | flops 15728640 | bytes 23592960 | tf_op jit(solution)/shard_map/convert_element_type | solution.py:806
  252.0 11.8 %shard_map.228 = (bf16[256,1024]{1,0:T(8,128)(2,1)}, bf16[2048,640]{1,0:T(8,128)(2,1)}) custom-call(s32[8]{0:T(128)} %concatenate.36.info_ref, s32[1,256]{1,0:T(1,128)} %copy-done.27, bf16[256,1024]{1,0:T(8,128)(2,1)} %get-tuple-element.198.q_ref, bf16[2048,640]{1,0:T(8,128)(2,1)} %get-tuple-element.84.kv_ref, ...), custom_call_target="tpu_custom_call" | custom-call | flops 314572800 | bytes 81920 | tf_op jit(solution)/shard_map/pallas_call | solution.py:604
  266.7 3.2 collective-permute-done.15
  276.4 11.8 %shard_map.229 = (bf16[256,1024]{1,0:T(8,128)(2,1)}, bf16[2048,640]{1,0:T(8,128)(2,1)}) custom-call(s32[8]{0:T(128)} %concatenate.37.info_ref, s32[1,256]{1,0:T(1,128)} %copy-done.26, bf16[256,1024]{1,0:T(8,128)(2,1)} %get-tuple-element.197.q_ref, bf16[2048,640]{1,0:T(8,128)(2,1)} %get-tuple-element.92.kv_ref, ...), custom_call_target="tpu_custom_call" | custom-call | flops 314572800 | bytes 81920 | tf_op jit(solution)/shard_map/pallas_call | solution.py:604
  288.2 24.0 %collective-permute-done.16.rest_1_ = bf16[256,640]{1,0:T(8,128)(2,1)S(1)} collective-permute-done((bf16[256,640]{1,0:T(8,128)(2,1)S(1)}, bf16[256,640]{1,0:T(8,128)(2,1)S(1)}, u32[]{:S(2)}, u32[]{:S(2)}) %collective-permute-start.16) | collective-permute-done | bytes 327712 | tf_op jit(solution)/shard_map/ppermute | solution.py:668
  312.3 22.9 %collective-permute-done.17.rest_2_ = bf16[256,640]{1,0:T(8,128)(2,1)S(1)} collective-permute-done((bf16[256,640]{1,0:T(8,128)(2,1)S(1)}, bf16[256,640]{1,0:T(8,128)(2,1)S(1)}, u32[]{:S(2)}, u32[]{:S(2)}) %collective-permute-start.17) | collective-permute-done | bytes 327712 | tf_op jit(solution)/shard_map/ppermute | solution.py:668
  345.4 6.0 %shard_map.230 = (f32[4,512,240]{2,1,0:T(8,128)}, bf16[4,1024,240]{2,1,0:T(8,128)(2,1)}) custom-call(s32[4]{0:T(128)} %iota_xor_fusion.index_ref, bf16[4,512,240]{2,1,0:T(8,128)(2,1)} %get-tuple-element.64.blocks_ref, bf16[256,1024]{1,0:T(8,128)(2,1)} %get-tuple-element.98.rest_0_, bf16[256,1024]{1,0:T(8,128)(2,1)} %get-tuple-element.100.rest_1_, ...), custom_call_target="tpu_custom_call" | custom-call | flops 31457280 | bytes 123904 | tf_op jit(solution)/shard_map/pallas_call | solution.py:94
  354.3 17.4 %collective-permute-done.21.rest_6_ = bf16[256,640]{1,0:T(8,128)(2,1)S(1)} collective-permute-done((bf16[256,640]{1,0:T(8,128)(2,1)S(1)}, bf16[256,640]{1,0:T(8,128)(2,1)S(1)}, u32[]{:S(2)}, u32[]{:S(2)}) %collective-permute-start.21) | collective-permute-done | bytes 327712 | tf_op jit(solution)/shard_map/ppermute | solution.py:668
  373.2 4.0 collective-permute-done.32
  380.3 6.0 %collective-permute-start.34 = (bf16[4,240,240]{2,1,0:T(8,128)(2,1)}, bf16[4,240,240]{2,1,0:T(8,128)(2,1)}, u32[]{:S(2)}, u32[]{:S(2)}) collective-permute-start(bf16[4,240,240]{2,1,0:T(8,128)(2,1)} %get-tuple-element.164), channel_id=1, source_target_pairs={{0,16},{1,17},{2,18},{3,19},{4,20},{5,21},{6,22},{7,23},{8,24},{9,... | collective-permute-start | bytes 1382408 | tf_op jit(solution)/shard_map/ppermute | solution.py:668
  390.2 4.1 collective-permute-start.24
  394.3 13.1 %collective-permute-done.34 = bf16[4,240,240]{2,1,0:T(8,128)(2,1)} collective-permute-done((bf16[4,240,240]{2,1,0:T(8,128)(2,1)}, bf16[4,240,240]{2,1,0:T(8,128)(2,1)}, u32[]{:S(2)}, u32[]{:S(2)}) %collective-permute-start.34) | collective-permute-done | bytes 460832 | tf_op jit(solution)/shard_map/ppermute | solution.py:668
  409.9 8.0 %shard_map.231 = (bf16[512,960]{1,0:T(8,128)(2,1)}, bf16[4,640,240]{2,1,0:T(8,128)(2,1)}, f32[1,960]{1,0:T(1,128)}) custom-call(s32[4]{0:T(128)} %iota_xor_fusion.index_ref, bf16[4,512,240]{2,1,0:T(8,128)(2,1)} %get-tuple-element.64.blocks_ref, f32[4,512,240]{2,1,0:T(8,128)} %get-tuple-element.102.dx_ref, f32[512,960]{1,0:T(8,128)} %get-tuple-element.103.dmid_ref, ...), custom_call_target="tpu_custom_call" | custom-call | flops 19660800 | bytes 195192 | tf_op jit(solution)/shard_map/pallas_call | solution.py:94
  423.9 12.8 %collective-permute-done.36 = bf16[3,320,256]{2,1,0:T(8,128)(2,1)} collective-permute-done((bf16[3,320,256]{2,1,0:T(8,128)(2,1)}, bf16[3,320,256]{2,1,0:T(8,128)(2,1)}, u32[]{:S(2)}, u32[]{:S(2)}) %collective-permute-start.36) | collective-permute-done | bytes 491552 | tf_op jit(solution)/shard_map/ppermute | solution.py:668
  444.3 4.7 collective-permute-done.38
  459.9 3.7 collective-permute-done.27
  (249 shorter events, 123.1 us)
Async XLA Ops:
  7.2 167.0 %all-gather.5.cloned.1.call-start = ((), (), s32[]{:S(2)}) async-start(), calls=%async_computation.1 | async-start | bytes 18247680 | tf_op jit(solution)/shard_map/all_gather | solution.py:723
  11.4 376.3 %reduce-scatter.4.cloned.1.call-start = ((), (), s32[]{:S(2)}) async-start(), calls=%async_computation.2 | async-start | bytes 9830400
  41.5 25.1 %collective-permute-start.4 = (bf16[4,120,240]{2,1,0:T(8,128)(2,1)S(1)}, bf16[4,120,240]{2,1,0:T(8,128)(2,1)S(1)}, u32[]{:S(2)}, u32[]{:S(2)}) collective-permute-start(bf16[4,120,240]{2,1,0:T(8,128)(2,1)S(1)} %slice.188), channel_id=1, source_target_pairs={{0,24},{1,25},{2,26},{3,27},{4,28},{5,29},{6,30},{7,31},{8,16},{9,... | collective-permute-start | bytes 691208 | tf_op jit(solution)/shard_map/ppermute | solution.py:668
  43.0 25.5 %collective-permute-start.3 = (bf16[4,120,240]{2,1,0:T(8,128)(2,1)S(1)}, bf16[4,120,240]{2,1,0:T(8,128)(2,1)S(1)}, u32[]{:S(2)}, u32[]{:S(2)}) collective-permute-start(bf16[4,120,240]{2,1,0:T(8,128)(2,1)S(1)} %slice.188), channel_id=1, source_target_pairs={{0,16},{1,17},{2,18},{3,19},{4,20},{5,21},{6,22},{7,23},{8,24},{9,... | collective-permute-start | bytes 691208 | tf_op jit(solution)/shard_map/ppermute | solution.py:668
  44.4 24.1 %collective-permute-start.2 = (bf16[4,120,240]{2,1,0:T(8,128)(2,1)S(1)}, bf16[4,120,240]{2,1,0:T(8,128)(2,1)}, u32[]{:S(2)}, u32[]{:S(2)}) collective-permute-start(bf16[4,120,240]{2,1,0:T(8,128)(2,1)S(1)} %slice.188), channel_id=1, source_target_pairs={{0,8},{1,9},{2,10},{3,11},{4,12},{5,13},{6,14},{7,15},{8,0},{9,1},... | collective-permute-start | bytes 691208 | tf_op jit(solution)/shard_map/ppermute | solution.py:668
  60.0 17.9 %collective-permute-start.1 = (bf16[256,640]{1,0:T(8,128)(2,1)S(1)}, bf16[256,640]{1,0:T(8,128)(2,1)S(1)}, u32[]{:S(2)}, u32[]{:S(2)}) collective-permute-start(bf16[256,640]{1,0:T(8,128)(2,1)S(1)} %get-tuple-element.207), channel_id=1, source_target_pairs={{0,2},{1,3},{2,4},{3,5},{4,6},{5,7},{8,10},{9,11},{10,12},{11,13},... | collective-permute-start | bytes 983048 | tf_op jit(solution)/shard_map/ppermute | solution.py:668
  63.4 27.0 %collective-permute-start.7 = (bf16[256,640]{1,0:T(8,128)(2,1)S(1)}, bf16[256,640]{1,0:T(8,128)(2,1)S(1)}, u32[]{:S(2)}, u32[]{:S(2)}) collective-permute-start(bf16[256,640]{1,0:T(8,128)(2,1)S(1)} %get-tuple-element.207), channel_id=1, source_target_pairs={{0,6},{1,7},{8,14},{9,15},{16,22},{17,23},{24,30},{25,31}} | collective-permute-start | bytes 983048 | tf_op jit(solution)/shard_map/ppermute | solution.py:668
  66.6 29.5 %collective-permute-start.6 = (bf16[256,640]{1,0:T(8,128)(2,1)S(1)}, bf16[256,640]{1,0:T(8,128)(2,1)S(1)}, u32[]{:S(2)}, u32[]{:S(2)}) collective-permute-start(bf16[256,640]{1,0:T(8,128)(2,1)S(1)} %get-tuple-element.207), channel_id=1, source_target_pairs={{0,4},{1,5},{2,6},{3,7},{8,12},{9,13},{10,14},{11,15},{16,20},{17,... | collective-permute-start | bytes 983048 | tf_op jit(solution)/shard_map/ppermute | solution.py:668
  70.7 45.5 %collective-permute-start.5 = (bf16[4,4,120,240]{3,2,1,0:T(8,128)(2,1)}, bf16[4,4,120,240]{3,2,1,0:T(8,128)(2,1)}, u32[]{:S(2)}, u32[]{:S(2)}) collective-permute-start(bf16[4,4,120,240]{3,2,1,0:T(8,128)(2,1)} %pad_maximum_fusion.4), channel_id=1, source_target_pairs={{0,1},{1,0},{2,3},{3,2},{4,5},{5,4},{6,7},{7,6},{8,9},{9,8},{10,11... | collective-permute-start | bytes 2764808 | tf_op jit(solution)/shard_map/ppermute | solution.py:668
  96.3 32.8 %collective-permute-start.8 = (bf16[4,256,640]{2,1,0:T(8,128)(2,1)S(1)}, bf16[4,256,640]{2,1,0:T(8,128)(2,1)S(1)}, u32[]{:S(2)}, u32[]{:S(2)}) collective-permute-start(bf16[4,256,640]{2,1,0:T(8,128)(2,1)S(1)} %pad_maximum_fusion.2.own), channel_id=1, source_target_pairs={{0,1},{1,0},{2,3},{3,2},{4,5},{5,4},{6,7},{7,6},{8,9},{9,8},{10,11... | collective-permute-start | bytes 3932168 | tf_op jit(solution)/shard_map/ppermute | solution.py:668
  100.4 38.9 %collective-permute-start.11 = (bf16[256,640]{1,0:T(8,128)(2,1)S(1)}, bf16[256,640]{1,0:T(8,128)(2,1)S(1)}, u32[]{:S(2)}, u32[]{:S(2)}) collective-permute-start(bf16[256,640]{1,0:T(8,128)(2,1)S(1)} %get-tuple-element.72), channel_id=1, source_target_pairs={{0,6},{1,7},{8,14},{9,15},{16,22},{17,23},{24,30},{25,31}} | collective-permute-start | bytes 983048 | tf_op jit(solution)/shard_map/ppermute | solution.py:668
  112.4 29.1 %collective-permute-start.10 = (bf16[256,640]{1,0:T(8,128)(2,1)S(1)}, bf16[256,640]{1,0:T(8,128)(2,1)S(1)}, u32[]{:S(2)}, u32[]{:S(2)}) collective-permute-start(bf16[256,640]{1,0:T(8,128)(2,1)S(1)} %get-tuple-element.72), channel_id=1, source_target_pairs={{0,4},{1,5},{2,6},{3,7},{8,12},{9,13},{10,14},{11,15},{16,20},{17,... | collective-permute-start | bytes 983048 | tf_op jit(solution)/shard_map/ppermute | solution.py:668
  113.8 41.6 %collective-permute-start.9 = (bf16[256,640]{1,0:T(8,128)(2,1)S(1)}, bf16[256,640]{1,0:T(8,128)(2,1)S(1)}, u32[]{:S(2)}, u32[]{:S(2)}) collective-permute-start(bf16[256,640]{1,0:T(8,128)(2,1)S(1)} %get-tuple-element.72), channel_id=1, source_target_pairs={{0,2},{1,3},{2,4},{3,5},{4,6},{5,7},{8,10},{9,11},{10,12},{11,13},... | collective-permute-start | bytes 983048 | tf_op jit(solution)/shard_map/ppermute | solution.py:668
  224.3 12.8 %collective-permute-start.14 = (bf16[4,4,3,320,256]{4,3,2,1,0:T(8,128)(2,1)}, bf16[4,4,3,320,256]{4,3,2,1,0:T(8,128)(2,1)}, u32[]{:S(2)}, u32[]{:S(2)}) collective-permute-start(bf16[4,4,3,320,256]{4,3,2,1,0:T(8,128)(2,1)} %get-tuple-element.87), channel_id=1, source_target_pairs={{0,1},{1,0},{2,3},{3,2},{4,5},{5,4},{6,7},{7,6},{8,9},{9,8},{10,11... | collective-permute-start | bytes 23592968 | tf_op jit(solution)/shard_map/ppermute | solution.py:668
  272.5 39.8 %collective-permute-start.16 = (bf16[256,640]{1,0:T(8,128)(2,1)S(1)}, bf16[256,640]{1,0:T(8,128)(2,1)S(1)}, u32[]{:S(2)}, u32[]{:S(2)}) collective-permute-start(bf16[256,640]{1,0:T(8,128)(2,1)S(1)} %get-tuple-element.189), channel_id=1, source_target_pairs={{2,0},{3,1},{4,2},{5,3},{6,4},{7,5},{10,8},{11,9},{12,10},{13,11},... | collective-permute-start | bytes 983048 | tf_op jit(solution)/shard_map/ppermute | solution.py:668
  273.8 61.4 %collective-permute-start.17 = (bf16[256,640]{1,0:T(8,128)(2,1)S(1)}, bf16[256,640]{1,0:T(8,128)(2,1)S(1)}, u32[]{:S(2)}, u32[]{:S(2)}) collective-permute-start(bf16[256,640]{1,0:T(8,128)(2,1)S(1)} %get-tuple-element.188), channel_id=1, source_target_pairs={{4,0},{5,1},{6,2},{7,3},{12,8},{13,9},{14,10},{15,11},{20,16},{21,... | collective-permute-start | bytes 983048 | tf_op jit(solution)/shard_map/ppermute | solution.py:668
  275.1 60.1 %collective-permute-start.18 = (bf16[256,640]{1,0:T(8,128)(2,1)S(1)}, bf16[256,640]{1,0:T(8,128)(2,1)S(1)}, u32[]{:S(2)}, u32[]{:S(2)}) collective-permute-start(bf16[256,640]{1,0:T(8,128)(2,1)S(1)} %get-tuple-element.187), channel_id=1, source_target_pairs={{6,0},{7,1},{14,8},{15,9},{22,16},{23,17},{30,24},{31,25}} | collective-permute-start | bytes 983048 | tf_op jit(solution)/shard_map/ppermute | solution.py:668
  341.4 12.9 %collective-permute-start.20 = (bf16[256,640]{1,0:T(8,128)(2,1)S(1)}, bf16[256,640]{1,0:T(8,128)(2,1)S(1)}, u32[]{:S(2)}, u32[]{:S(2)}) collective-permute-start(bf16[256,640]{1,0:T(8,128)(2,1)S(1)} %get-tuple-element.185), channel_id=1, source_target_pairs={{2,0},{3,1},{4,2},{5,3},{6,4},{7,5},{10,8},{11,9},{12,10},{13,11},... | collective-permute-start | bytes 983048 | tf_op jit(solution)/shard_map/ppermute | solution.py:668
  342.7 29.1 %collective-permute-start.21 = (bf16[256,640]{1,0:T(8,128)(2,1)S(1)}, bf16[256,640]{1,0:T(8,128)(2,1)S(1)}, u32[]{:S(2)}, u32[]{:S(2)}) collective-permute-start(bf16[256,640]{1,0:T(8,128)(2,1)S(1)} %get-tuple-element.184), channel_id=1, source_target_pairs={{4,0},{5,1},{6,2},{7,3},{12,8},{13,9},{14,10},{15,11},{20,16},{21,... | collective-permute-start | bytes 983048 | tf_op jit(solution)/shard_map/ppermute | solution.py:668
  344.0 27.8 %collective-permute-start.22 = (bf16[256,640]{1,0:T(8,128)(2,1)S(1)}, bf16[256,640]{1,0:T(8,128)(2,1)S(1)}, u32[]{:S(2)}, u32[]{:S(2)}) collective-permute-start(bf16[256,640]{1,0:T(8,128)(2,1)S(1)} %get-tuple-element.183), channel_id=1, source_target_pairs={{6,0},{7,1},{14,8},{15,9},{22,16},{23,17},{30,24},{31,25}} | collective-permute-start | bytes 983048 | tf_op jit(solution)/shard_map/ppermute | solution.py:668
  378.9 15.4 %collective-permute-start.35 = (bf16[4,240,240]{2,1,0:T(8,128)(2,1)}, bf16[4,240,240]{2,1,0:T(8,128)(2,1)S(1)}, u32[]{:S(2)}, u32[]{:S(2)}) collective-permute-start(bf16[4,240,240]{2,1,0:T(8,128)(2,1)} %get-tuple-element.163), channel_id=1, source_target_pairs={{0,24},{1,25},{2,26},{3,27},{4,28},{5,29},{6,30},{7,31},{8,16},{9,... | collective-permute-start | bytes 1382408 | tf_op jit(solution)/shard_map/ppermute | solution.py:668
  380.3 27.1 %collective-permute-start.34 = (bf16[4,240,240]{2,1,0:T(8,128)(2,1)}, bf16[4,240,240]{2,1,0:T(8,128)(2,1)}, u32[]{:S(2)}, u32[]{:S(2)}) collective-permute-start(bf16[4,240,240]{2,1,0:T(8,128)(2,1)} %get-tuple-element.164), channel_id=1, source_target_pairs={{0,16},{1,17},{2,18},{3,19},{4,20},{5,21},{6,22},{7,23},{8,24},{9,... | collective-permute-start | bytes 1382408 | tf_op jit(solution)/shard_map/ppermute | solution.py:668
  386.3 22.2 %collective-permute-start.33 = (bf16[4,240,240]{2,1,0:T(8,128)(2,1)}, bf16[4,240,240]{2,1,0:T(8,128)(2,1)}, u32[]{:S(2)}, u32[]{:S(2)}) collective-permute-start(bf16[4,240,240]{2,1,0:T(8,128)(2,1)} %get-tuple-element.162), channel_id=1, source_target_pairs={{0,8},{1,9},{2,10},{3,11},{4,12},{5,13},{6,14},{7,15},{8,0},{9,1},... | collective-permute-start | bytes 1382408 | tf_op jit(solution)/shard_map/ppermute | solution.py:668
  390.2 30.9 %collective-permute-start.23 = (bf16[3,320,256]{2,1,0:T(8,128)(2,1)}, bf16[3,320,256]{2,1,0:T(8,128)(2,1)S(1)}, u32[]{:S(2)}, u32[]{:S(2)}) collective-permute-start(bf16[3,320,256]{2,1,0:T(8,128)(2,1)} %get-tuple-element.161), channel_id=1, source_target_pairs={{0,2},{1,3},{2,4},{3,5},{4,6},{5,7},{6,0},{7,1},{8,10},{9,11},{10,... | collective-permute-start | bytes 1474568 | tf_op jit(solution)/shard_map/ppermute | solution.py:668
  390.2 30.9 %collective-permute-start.24 = (bf16[3,320,256]{2,1,0:T(8,128)(2,1)}, bf16[3,320,256]{2,1,0:T(8,128)(2,1)}, u32[]{:S(2)}, u32[]{:S(2)}) collective-permute-start(bf16[3,320,256]{2,1,0:T(8,128)(2,1)} %get-tuple-element.160), channel_id=1, source_target_pairs={{0,6},{1,7},{2,0},{3,1},{4,2},{5,3},{6,4},{7,5},{8,14},{9,15},{10,... | collective-permute-start | bytes 1474568 | tf_op jit(solution)/shard_map/ppermute | solution.py:668
  420.2 16.5 %collective-permute-start.36 = (bf16[3,320,256]{2,1,0:T(8,128)(2,1)}, bf16[3,320,256]{2,1,0:T(8,128)(2,1)}, u32[]{:S(2)}, u32[]{:S(2)}) collective-permute-start(bf16[3,320,256]{2,1,0:T(8,128)(2,1)} %get-tuple-element.159), channel_id=1, source_target_pairs={{0,4},{1,5},{2,6},{3,7},{4,0},{5,1},{6,2},{7,3},{8,12},{9,13},{10,... | collective-permute-start | bytes 1474568 | tf_op jit(solution)/shard_map/ppermute | solution.py:668
  423.8 27.8 %collective-permute-start.25 = (bf16[4,4,88,240]{3,2,1,0:T(8,128)(2,1)}, bf16[4,4,88,240]{3,2,1,0:T(8,128)(2,1)S(1)}, u32[]{:S(2)}, u32[]{:S(2)}) collective-permute-start(bf16[4,4,88,240]{3,2,1,0:T(8,128)(2,1)} %pad_maximum_fusion.5), channel_id=1, source_target_pairs={{0,1},{1,0},{2,3},{3,2},{4,5},{5,4},{6,7},{7,6},{8,9},{9,8},{10,11... | collective-permute-start | bytes 2027528 | tf_op jit(solution)/shard_map/ppermute | solution.py:668
  439.2 9.9 %collective-permute-start.38 = (bf16[240,240]{1,0:T(8,128)(2,1)}, bf16[240,240]{1,0:T(8,128)(2,1)S(1)}, u32[]{:S(2)}, u32[]{:S(2)}) collective-permute-start(bf16[240,240]{1,0:T(8,128)(2,1)} %get-tuple-element.210), channel_id=1, source_target_pairs={{0,4},{1,5},{2,6},{3,7},{4,0},{5,1},{6,2},{7,3},{8,12},{9,13},{10,... | collective-permute-start | bytes 345608 | tf_op jit(solution)/shard_map/ppermute | solution.py:668
  439.2 9.9 %collective-permute-start.37 = (bf16[240,240]{1,0:T(8,128)(2,1)S(1)}, bf16[240,240]{1,0:T(8,128)(2,1)}, u32[]{:S(2)}, u32[]{:S(2)}) collective-permute-start(bf16[240,240]{1,0:T(8,128)(2,1)S(1)} %get-tuple-element.208), channel_id=1, source_target_pairs={{0,2},{1,3},{2,4},{3,5},{4,6},{5,7},{6,0},{7,1},{8,10},{9,11},{10,... | collective-permute-start | bytes 345608 | tf_op jit(solution)/shard_map/ppermute | solution.py:668
  442.7 14.1 %collective-permute-start.40 = (f32[1,320,120]{2,1,0:T(8,128)S(1)}, f32[1,320,120]{2,1,0:T(8,128)S(1)}, u32[]{:S(2)}, u32[]{:S(2)}) collective-permute-start(f32[1,320,120]{2,1,0:T(8,128)S(1)} %bitcast.306), channel_id=1, source_target_pairs={{0,1},{1,0},{2,3},{3,2},{4,5},{5,4},{6,7},{7,6},{8,9},{9,8},{10,11... | collective-permute-start | bytes 460808 | tf_op jit(solution)/shard_map/ppermute | solution.py:668
  454.1 9.6 %collective-permute-start.27 = (bf16[4,88,240]{2,1,0:T(8,128)(2,1)S(1)}, bf16[4,88,240]{2,1,0:T(8,128)(2,1)S(1)}, u32[]{:S(2)}, u32[]{:S(2)}) collective-permute-start(bf16[4,88,240]{2,1,0:T(8,128)(2,1)S(1)} %get-tuple-element.204), channel_id=1, source_target_pairs={{0,16},{1,17},{2,18},{3,19},{4,20},{5,21},{6,22},{7,23},{8,24},{9,... | collective-permute-start | bytes 506888 | tf_op jit(solution)/shard_map/ppermute | solution.py:668
  456.8 7.9 %collective-permute-start.26 = (bf16[4,88,240]{2,1,0:T(8,128)(2,1)S(1)}, bf16[4,88,240]{2,1,0:T(8,128)(2,1)S(1)}, u32[]{:S(2)}, u32[]{:S(2)}) collective-permute-start(bf16[4,88,240]{2,1,0:T(8,128)(2,1)S(1)} %get-tuple-element.202), channel_id=1, source_target_pairs={{0,8},{1,9},{2,10},{3,11},{4,12},{5,13},{6,14},{7,15},{8,0},{9,1},... | collective-permute-start | bytes 506888 | tf_op jit(solution)/shard_map/ppermute | solution.py:668
  (46 other events, 460.5 us)
Sparse Core Ops, SparseCore 0:
  11.6 162.5 all-gather.4
  249.3 110.8 reduce-scatter.3
